TPU v7x, 32 devices: a whole 2x2x4 slice. The times are simulated.
32 devices in a mesh: expert: 8 (over y, x, core), dp: 4 (over z).
Axes of the slice: x: 2, y: 2, z: 4, core: 2. Of those that a mesh axis runs over, the one named last changes fastest.
Arguments:
- rows_x: bfloat16 [2048, 4096], P('expert'), may hold values from -6 to 6
- rows_dy: bfloat16 [2048, 4096], P('expert'), may hold values from -2 to 2
- router_logits: float32 [2048, 8], P('expert'), may hold values from -7.5 to 307.5
- expert_of: int32 [2048, 1], P('expert'), may hold values from 0 to 7, as said below
- w_gate: bfloat16 [8, 1536, 4096], P('expert', 'dp'), may hold values from -0.09375 to 0.09375
- w_up: bfloat16 [8, 1536, 4096], P('expert', 'dp'), may hold values from -0.09375 to 0.09375
- w_down: bfloat16 [8, 1536, 4096], P('expert', 'dp'), may hold values from -0.15625 to 0.15625
Outputs:
- grad_rows: bfloat16 [2048, 4096], P('expert', 'dp')
- grad_logits: float32 [2048, 8], P('expert')
- grad_gate: float32 [8, 1536, 4096], P('expert', 'dp')
- grad_up: float32 [8, 1536, 4096], P('expert', 'dp')
- grad_down: float32 [8, 1536, 4096], P('expert', 'dp')
- grad_norm: float32 [], replicated
Inputs may be any that keep to these rules, and one draw needn't show every extreme that they name: `expert_of`: one expert, the same in every aligned block of 256 rows, is named by exactly 64 rows of each block; a second expert, the same in every block, by exactly 32 rows of each block; every other expert by at most 32 rows of a block.
All inputs are finite; a program needn't handle non-finite values.
Results may differ from a plain program's by a relative error of at most 0.015.
Values may be sent and summed in bfloat16 or wider, within the bound.
No kernel may reach another device: no remote copies, remote signals or barrier semaphores. Data moves between devices by JAX's collectives and lax.ppermute only.
A program may use at most 192 MiB of HBM per device.

v0:
```python
import functools

import jax
import jax.numpy as jnp
from jax import lax
from jax.experimental import pallas as pl
from jax.experimental.pallas import tpu as pltpu
from jax.sharding import PartitionSpec as P

aux_weight = 1.0
LANES = 128
COUNT_LANE = 64
BF16 = jnp.bfloat16
F32 = jnp.float32
ANY = pl.BlockSpec(memory_space=pl.ANY)
VMEM = pl.BlockSpec(memory_space=pltpu.VMEM)
SMEM = pl.BlockSpec(memory_space=pltpu.SMEM)


def call(body, name, out_shape, in_specs, out_specs, scratch, micros, room, **extra):
    return pl.pallas_call(
        body,
        name=name,
        out_shape=out_shape,
        in_specs=in_specs,
        out_specs=out_specs,
        scratch_shapes=scratch,
        cost_estimate=pl.CostEstimate(
            flops=int(micros * 5e7), bytes_accessed=int(micros * 1e5), transcendentals=0
        ),
        compiler_params=pltpu.CompilerParams(vmem_limit_bytes=room * 1024 * 1024),
        **extra,
    )


def lane_iota(shape):
    return lax.broadcasted_iota(jnp.int32, shape, len(shape) - 1)


def routing(ids, me, cap, experts):
    rows = ids.shape[1]
    expert = lax.broadcasted_iota(jnp.int32, (experts, rows), 0)
    onehot = jnp.where(expert == ids, 1.0, 0.0)
    before = lax.broadcasted_iota(jnp.int32, (rows, rows), 0) < lane_iota((rows, rows))
    earlier = jnp.dot(
        onehot.astype(BF16), jnp.where(before, 1.0, 0.0).astype(BF16), preferred_element_type=F32
    )
    rank = jnp.sum(earlier * onehot, axis=0, keepdims=True).astype(jnp.int32)
    slot = jnp.where(rank < cap, (ids ^ me) * cap + rank, experts * cap + rank - cap)
    slots = -(-(experts + 1) * cap // LANES) * LANES
    spread = lax.broadcasted_iota(jnp.int32, (slots, rows), 0) == slot
    return onehot, jnp.where(spread, 1.0, 0.0)


def softmax(logits):
    scores = jnp.exp(logits - jnp.max(logits, axis=0, keepdims=True))
    return scores / jnp.sum(scores, axis=0, keepdims=True)


def dispatch_body(experts, cap, width, place, x_hbm, dy_hbm, logits, ids, *refs):
    outs, hot = refs[: experts + 1], refs[experts + 1]
    held, sent, in_sems, out_sems = refs[experts + 2 :]
    loads = [
        pltpu.make_async_copy(source, held.at[:, pl.ds(i * width, width)], in_sems.at[i])
        for i, source in enumerate((x_hbm, dy_hbm))
    ]
    for load in loads:
        load.start()
    me = place[0]
    expert_ids = ids[...]
    slots = sent.shape[0]
    onehot, spread = routing(expert_ids, me, cap, experts)
    spread = spread[:slots]
    gate = jnp.sum(softmax(logits[...]) * onehot, axis=0, keepdims=True)
    gate = gate.astype(BF16).astype(F32)
    mine = jnp.sum(jnp.where(expert_ids == me, 1, 0))
    hot[0] = jnp.where(mine > cap, 1, 0)
    counts = jnp.sum(onehot, axis=1, keepdims=True)
    expert = lax.broadcasted_iota(jnp.int32, (experts, LANES), 0)
    counts = jnp.sum(
        jnp.where(lane_iota((experts, LANES)) - COUNT_LANE == expert, counts, 0.0),
        axis=0,
        keepdims=True,
    )
    gates = jnp.sum(spread * gate, axis=1, keepdims=True)
    sent[:, 2 * width :] = jnp.where(lane_iota((slots, LANES)) == 0, gates, counts).astype(BF16)
    spread = spread.astype(BF16)
    stores = []
    tile = 1024
    for half in range(2):
        loads[half].wait()
        for at in range(half * width, (half + 1) * width, tile):
            sent[:, at : at + tile] = jnp.dot(
                spread, held[:, at : at + tile], preferred_element_type=F32
            ).astype(BF16)
        size = width if half == 0 else width + LANES
        for m in range(experts + 1):
            store = pltpu.make_async_copy(
                sent.at[pl.ds(m * cap, cap), pl.ds(half * width, size)],
                outs[m].at[:, pl.ds(half * width, size)],
                out_sems.at[half, m],
            )
            store.start()
            stores.append(store)
    for store in stores:
        store.wait()


def dispatch(place, rows_x, rows_dy, logits, ids, experts, cap):
    rows, width = rows_x.shape
    wide = 2 * width + LANES
    slots = (experts + 1) * cap
    return call(
        functools.partial(dispatch_body, experts, cap, width),
        "dispatch",
        [jax.ShapeDtypeStruct((cap, wide), BF16)] * (experts + 1)
        + [jax.ShapeDtypeStruct((1,), jnp.int32)],
        [SMEM, ANY, ANY, VMEM, VMEM],
        [ANY] * (experts + 1) + [SMEM],
        [
            pltpu.VMEM((rows, 2 * width), BF16),
            pltpu.VMEM((slots, wide), BF16),
            pltpu.SemaphoreType.DMA((2,)),
            pltpu.SemaphoreType.DMA((2, experts + 1)),
        ],
        6,
        16,
    )(place, rows_x, rows_dy, logits, ids)


def split_lanes(total):
    lane = lane_iota((total.shape[0], LANES))
    first = total.astype(BF16).astype(F32)
    second = (total - first).astype(BF16).astype(F32)
    third = total - first - second
    return jnp.where(
        lane == 0, first, jnp.where(lane == 1, second, jnp.where(lane == 2, third, 0.0))
    ).astype(BF16)


def rows_body(pieces, cap, width, n_dp, guarded, place, hot, *refs):
    sources, weights = refs[:pieces], refs[pieces : pieces + 3]
    outs = refs[pieces + 3 : -2]
    held, piece_sems = refs[-2:]
    hidden_units = weights[0].shape[0]
    rows = held.shape[0]

    def work():
        copies = [
            pltpu.make_async_copy(
                sources[p], held.at[pl.ds(p * cap, cap), :], piece_sems.at[p]
            )
            for p in range(pieces)
        ]
        for copy in copies:
            copy.start()
        for copy in copies:
            copy.wait()
        pre_gate, pre_up, grad = [
            lax.dot_general(
                held[:, side * width : (side + 1) * width],
                weight[...],
                (((1,), (1,)), ((), ())),
                preferred_element_type=F32,
            )
            for side, weight in zip((0, 0, 1), weights)
        ]
        gate = held[:, 2 * width :].astype(F32)[:, 0:1]
        sigmoid = jax.nn.sigmoid(pre_gate)
        active = pre_gate * sigmoid
        hidden = (active * pre_up).astype(BF16)
        hidden_f = hidden.astype(F32)
        gate_part = jnp.sum(hidden_f * grad, axis=1, keepdims=True)
        grad_hidden = grad * gate
        d_up = (grad_hidden * active).astype(BF16)
        d_pre = (grad_hidden * pre_up * sigmoid * (1.0 + pre_gate * (1.0 - sigmoid))).astype(BF16)
        outs[-1][:, :hidden_units] = d_pre
        outs[-1][:, hidden_units : 2 * hidden_units] = d_up
        outs[-1][:, 2 * hidden_units :] = (hidden_f * gate).astype(BF16)
        part = split_lanes(gate_part)
        cut = width // n_dp
        me = place[1]
        halves = 2 if not guarded else 4
        for half in range(halves):
            first = 0 if half < 2 else rows // 2
            size = rows if not guarded else rows // 2
            outs[half][:, n_dp // 2 * cut :] = part[first : first + size]
            for p in range(n_dp // 2):
                column = pl.multiple_of((me ^ (2 * p + half % 2)) * cut, cut)
                outs[half][:, p * cut : (p + 1) * cut] = (
                    jnp.dot(
                        d_pre[first : first + size],
                        weights[0][:, pl.ds(column, cut)],
                        preferred_element_type=F32,
                    )
                    + jnp.dot(
                        d_up[first : first + size],
                        weights[1][:, pl.ds(column, cut)],
                        preferred_element_type=F32,
                    )
                ).astype(BF16)

    if guarded:

        @pl.when(hot[0] == 1)
        def _():
            work()

        @pl.when(hot[0] != 1)
        def _():
            for out in outs:
                out[...] = jnp.zeros_like(out)
    else:
        work()


def rows_backward(place, hot, sources, weights, cap, n_dp, guarded):
    width = weights[0].shape[1]
    hidden_units = weights[0].shape[0]
    pieces = len(sources)
    rows = pieces * cap
    part = width // 2 + LANES
    parts = [(rows, part)] * 2 if not guarded else [(rows // 2, part)] * 4
    return call(
        functools.partial(rows_body, pieces, cap, width, n_dp, guarded),
        "rows_backward",
        [jax.ShapeDtypeStruct(s, BF16) for s in parts]
        + [jax.ShapeDtypeStruct((rows, 3 * hidden_units), BF16)],
        [SMEM, SMEM] + [ANY] * pieces + [VMEM] * 3,
        [VMEM] * (len(parts) + 1),
        [
            pltpu.VMEM((rows, 2 * width + LANES), BF16),
            pltpu.SemaphoreType.DMA((pieces,)),
        ],
        7,
        20,
    )(place, hot, *sources, *weights)


def merge_body(*refs):
    count = len(refs) // 3
    for a, b, out in zip(refs[:count], refs[count : 2 * count], refs[2 * count :]):
        out[...] = a[...] + b[...]


def merge(own, peers):
    return call(
        merge_body,
        "merge",
        [jax.ShapeDtypeStruct(a.shape, a.dtype) for a in own],
        [VMEM] * (2 * len(own)),
        [VMEM] * len(own),
        [],
        2,
        8,
    )(*own, *peers)


def fold_body(cut, parts, cap, kept, got, *outs):
    gate_part = jnp.sum(
        kept[:, parts * cut :].astype(F32) + got[:, parts * cut :].astype(F32),
        axis=1,
        keepdims=True,
    )
    lanes = split_lanes(gate_part)
    if parts == 1:
        total = kept[:, :cut].astype(F32) + got[:, :cut].astype(F32)
        for p, out in enumerate(outs):
            out[:, :cut] = total[p * cap : (p + 1) * cap].astype(BF16)
            out[:, cut:] = lanes[p * cap : (p + 1) * cap]
        return
    for out in outs:
        out[:, parts // 2 * cut :] = lanes
    for p in range(parts):
        total = kept[:, p * cut : (p + 1) * cut].astype(F32) + got[
            :, p * cut : (p + 1) * cut
        ].astype(F32)
        outs[p % 2][:, p // 2 * cut : (p // 2 + 1) * cut] = total.astype(BF16)


def fold(kept, got, cut, parts, cap):
    rows = kept.shape[0]
    if parts == 1:
        shapes = [(cap, cut + LANES)] * (rows // cap)
    else:
        shapes = [(rows, parts // 2 * cut + LANES)] * 2
    return call(
        functools.partial(fold_body, cut, parts, cap),
        "fold",
        [jax.ShapeDtypeStruct(s, BF16) for s in shapes],
        [VMEM, VMEM],
        [VMEM] * len(shapes),
        [],
        2,
        8,
    )(kept, got)


def weights_body(cold_pieces, hot_pieces, acts_count, cap, width, tile, hot, *refs):
    pieces = cold_pieces + hot_pieces
    sources, acts = refs[:pieces], refs[pieces : pieces + acts_count]
    outs, squares = refs[pieces + acts_count : -4][:3], refs[pieces + acts_count : -4][3]
    held, factors, total, sems = refs[-4:]
    step = pl.program_id(0)
    hidden_units = outs[0].shape[0]
    cold_rows = cold_pieces * cap

    def copies(count):
        return [
            pltpu.make_async_copy(
                sources[p].at[:, pl.ds(0, 2 * width)],
                held.at[pl.ds(p * cap, cap), :],
                sems.at[p],
            )
            for p in count
        ]

    @pl.when(step == 0)
    def _():
        for copy in copies(range(cold_pieces)):
            copy.start()

        @pl.when(hot[0] == 1)
        def _():
            for copy in copies(range(cold_pieces, pieces)):
                copy.start()

        at = 0
        for act in acts:
            factors[:, at : at + act.shape[0]] = act[...].astype(F32).T.astype(BF16)
            at += act.shape[0]
        total[...] = jnp.zeros_like(total)
        for copy in copies(range(cold_pieces)):
            copy.wait()

        @pl.when(hot[0] == 1)
        def _():
            for copy in copies(range(cold_pieces, pieces)):
                copy.wait()

    def work(rows):
        for i in range(3):
            at = pl.multiple_of((width if i == 2 else 0) + step * tile, tile)
            gradient = jnp.dot(
                factors[i * hidden_units : (i + 1) * hidden_units, :rows],
                held[:rows, pl.ds(at, tile)],
                preferred_element_type=F32,
            )
            outs[i][...] = gradient
            total[...] += jnp.sum((gradient * gradient).reshape(-1, 8, tile), axis=0)

    @pl.when(hot[0] == 1)
    def _():
        work(pieces * cap)

    @pl.when(hot[0] != 1)
    def _():
        work(cold_rows)

    @pl.when(step == pl.num_programs(0) - 1)
    def _():
        squares[...] = jnp.full(squares.shape, jnp.sum(total[...]), F32)


def weights_backward(hot, cold, extra, acts, hidden_units, width, cap):
    tile = 512
    rows = (len(cold) + len(extra)) * cap
    block = pl.BlockSpec((hidden_units, tile), lambda j: (0, j))
    whole = [pl.BlockSpec(a.shape, lambda j: (0, 0)) for a in acts]
    return call(
        functools.partial(
            weights_body, len(cold), len(extra), len(acts), cap, width, tile
        ),
        "weights_backward",
        [jax.ShapeDtypeStruct((hidden_units, width), F32)] * 3
        + [jax.ShapeDtypeStruct((8, LANES), F32)],
        [SMEM] + [ANY] * (len(cold) + len(extra)) + whole,
        [block] * 3 + [pl.BlockSpec((8, LANES), lambda j: (0, 0))],
        [
            pltpu.VMEM((rows, 2 * width), BF16),
            pltpu.VMEM((3 * hidden_units, rows), BF16),
            pltpu.VMEM((8, tile), F32),
            pltpu.SemaphoreType.DMA((len(cold) + len(extra),)),
        ],
        13,
        24,
        grid=(width // tile,),
    )(hot, *cold, *extra, *acts)


def home_body(experts, cap, cut, row_total, place, logits, ids, *refs):
    arrived, back, extra = refs[:experts], refs[experts : 2 * experts], refs[2 * experts : -5]
    grad_rows, grad_logits, pads, table, sems = refs[-5:]
    copies = [
        pltpu.make_async_copy(
            arrived[m].at[pl.ds(0, 16), pl.ds(arrived[m].shape[1] - LANES, LANES)],
            pads.at[pl.ds(16 * m, 16), :],
            sems.at[m],
        )
        for m in range(experts)
    ]
    for copy in copies:
        copy.start()
    onehot, spread = routing(ids[...], place[0], cap, experts)
    slots = (experts + 1) * cap
    for m in range(experts):
        table[m * cap : (m + 1) * cap, :] = back[m][...]
    over = extra[0][...]
    for piece in extra[1:]:
        over = over + piece[...]
    table[experts * cap :, :] = over
    pick = spread.T[:, :slots].astype(BF16)
    grad_rows[...] = jnp.dot(pick, table[:, :cut], preferred_element_type=F32).astype(BF16)
    gate_rows = jnp.dot(pick, table[:, cut:], preferred_element_type=F32).T[0:1]
    for copy in copies:
        copy.wait()
    counts = jnp.zeros((1, LANES), F32)
    for m in range(experts):
        counts = counts + pads[16 * m : 16 * m + 16, :].astype(F32)[0:1]
    counts = jnp.broadcast_to(counts, (8, LANES)).T[COUNT_LANE : COUNT_LANE + experts, 0:1]
    probs = softmax(logits[...])
    pulls = onehot * gate_rows + aux_weight * experts * (counts / row_total)
    grad_logits[...] = probs * (pulls - jnp.sum(probs * pulls, axis=0, keepdims=True))


def home(place, logits, ids, arrived, back, extra, cap, row_total):
    experts = len(back)
    rows = ids.shape[1]
    cut = back[0].shape[1] - LANES
    return call(
        functools.partial(home_body, experts, cap, cut, row_total),
        "home",
        [
            jax.ShapeDtypeStruct((rows, cut), BF16),
            jax.ShapeDtypeStruct(logits.shape, F32),
        ],
        [SMEM, VMEM, VMEM] + [ANY] * experts + [VMEM] * (experts + len(extra)),
        [VMEM, VMEM],
        [
            pltpu.VMEM((16 * experts, LANES), BF16),
            pltpu.VMEM(((experts + 1) * cap, cut + LANES), BF16),
            pltpu.SemaphoreType.DMA((experts,)),
        ],
        4,
        8,
    )(place, logits, ids, *arrived, *back, *extra)


def swap(value, axis, mask):
    size = lax.axis_size(axis)
    return lax.ppermute(value, axis, [(i, i ^ mask) for i in range(size)])


def after(value, *done):
    return lax.optimization_barrier((value, *done))[0]


def groups_of(experts):
    order = {}
    for m in range(2, experts):
        order.setdefault((bin(m >> 1).count("1"), m & 1), []).append(m)
    return [order[key] for key in sorted(order)]


def local(rows_x, rows_dy, router_logits, expert_of, w_gate, w_up, w_down):
    experts = lax.axis_size("expert")
    n_dp = lax.axis_size("dp")
    rows, width = rows_x.shape
    cap = rows // 8
    cut = width // n_dp
    place = jnp.stack([lax.axis_index("expert"), lax.axis_index("dp")]).astype(jnp.int32)
    weights = (w_gate[0], w_up[0], w_down[0])
    hidden_units = weights[0].shape[0]
    logits, ids = router_logits.T, expert_of.reshape(1, rows)
    *pieces, spare, hot = dispatch(place, rows_x, rows_dy, logits, ids, experts, cap)

    evens = list(range(0, experts, 2))
    odds = list(range(1, experts, 2))
    groups = groups_of(experts)
    cold = {0: pieces[0], 1: swap(pieces[1], "expert", 1)}
    extra = {0: spare, 1: swap(spare, "expert", 1)}
    sends = [(extra, list(level)) for level in groups[::2]] + [(cold, g) for g in groups]
    done = []
    for i, (held, group) in enumerate(sends):
        for m in group:
            piece = spare if held is extra else pieces[m]
            if i >= 2:
                piece = after(piece, *done[i - 2])
            held[m] = swap(piece, "expert", m)
        done.append([held[m] for m in group])
        if held is extra:
            for m in group:
                extra[m ^ 1] = swap(extra[m], "expert", 1)

    def along_dp(kept, sent):
        step = 1
        while True:
            got = swap(sent, "dp", step)
            parts = (kept.shape[1] - LANES) // cut
            if parts == 1:
                return fold(kept, got, cut, 1, cap)
            kept, sent = fold(kept, got, cut, parts, cap)
            step *= 2

    *parts, acts_hot = rows_backward(
        place, hot, [extra[m] for m in evens + odds], weights, cap, n_dp, True
    )
    peers = [swap(part, "expert", 1) for part in parts[2:]]
    kept, sent = merge(parts[:2], peers)
    extra_back = along_dp(kept, sent)
    back_extra = [extra_back[0]]
    for i, m in enumerate(evens[1:]):
        back_extra.append(swap(extra_back[1 + i], "expert", m))

    chunks = [[0, 1] + groups[0], groups[1], sum(groups[2:], [])]
    acts, back = [], {}
    last = acts_hot
    for chunk in chunks:
        kept, sent, act = rows_backward(
            place, after(hot, last), [cold[m] for m in chunk], weights, cap, n_dp, False
        )
        acts.append(act)
        last = act
        for m, piece in zip(chunk, along_dp(kept, sent)):
            back[m] = piece if m == 0 else swap(piece, "expert", m)

    masks = [m for chunk in chunks for m in chunk]
    grad_gate, grad_up, grad_down, squares = weights_backward(
        hot,
        [cold[m] for m in masks],
        [extra[m] for m in evens + odds],
        acts + [acts_hot],
        hidden_units,
        width,
        cap,
    )
    squares = squares + swap(squares, "expert", 1)
    squares = squares + sum(swap(squares, "dp", m) for m in range(1, n_dp))
    squares = squares + sum(swap(squares, "expert", m) for m in evens[1:])
    grad_rows, grad_logits = home(
        place,
        logits,
        ids,
        [cold[m] for m in range(experts)],
        [back[m] for m in range(experts)],
        back_extra,
        cap,
        rows * experts,
    )
    return (
        grad_rows,
        grad_logits.T,
        grad_gate[None],
        grad_up[None],
        grad_down[None],
        jnp.sqrt(squares[0, 0]),
    )


def solution(mesh):
    in_specs = (
        P("expert", None),
        P("expert", None),
        P("expert", None),
        P("expert", None),
        P("expert", "dp", None),
        P("expert", "dp", None),
        P("expert", "dp", None),
    )
    out_specs = (
        P("expert", "dp"),
        P("expert", None),
        P("expert", "dp", None),
        P("expert", "dp", None),
        P("expert", "dp", None),
        P(),
    )
    return jax.shard_map(local, mesh=mesh, in_specs=in_specs, out_specs=out_specs, check_vma=False)
```

profile of v0, /device:TPU:0, one launch (start us, length us, event | category | flops | bytes accessed | tf_op | source)
XLA Modules:
  0.0 166.7 jit_solution(9461465801159055029)
XLA Ops:
  0.7 1.7 %copy-done.4 = bf16[256,4096]{1,0:T(8,128)(2,1)S(1)} copy-done((bf16[256,4096]{1,0:T(8,128)(2,1)S(1)}, bf16[256,4096]{1,0:T(8,128)(2,1)}, u32[]{:S(2)}) %copy-start.4) | copy-done | bytes 2097176
  5.4 3.9 %dispatch.1 = (bf16[32,8320]{1,0:T(8,128)(2,1)S(1)}, bf16[32,8320]{1,0:T(8,128)(2,1)S(1)}, bf16[32,8320]{1,0:T(8,128)(2,1)S(1)}, bf16[32,8320]{1,0:T(8,128)(2,1)...) custom-call(s32[2]{0:T(128)S(1)} %pad_add_fusion.place, ...), custom_call_target="tpu_custom_call" | custom-call | flops 300000000 | bytes 600000 | tf_op jit(solution)/shard_map/dispatch/pallas_call | solution.py:113
  9.4 4.0 %collective-permute-start.4 = (bf16[32,8320]{1,0:T(8,128)(2,1)S(1)}, bf16[32,8320]{1,0:T(8,128)(2,1)S(1)}, u32[]{:S(2)}, u32[]{:S(2)}) collective-permute-start(bf16[32,8320]{1,0:T(8,128)(2,1)S(1)} %get-tuple-element.70.refs_0_.refs_8_), channel_id=1, source_target_pairs={{0,24},{4,28},{8,16},{12,20},{16,8},{20,12},{24,0},{28,4},{1,25},{... | collective-permute-start | bytes 1597448 | tf_op jit(solution)/shard_map/ppermute | solution.py:451
  14.0 12.3 %collective-permute-done.4.refs_3_.refs_11_ = bf16[32,8320]{1,0:T(8,128)(2,1)S(1)} collective-permute-done((bf16[32,8320]{1,0:T(8,128)(2,1)S(1)}, bf16[32,8320]{1,0:T(8,128)(2,1)S(1)}, u32[]{:S(2)}, u32[]{:S(2)}) %collective-permute-start.4) | collective-permute-done | bytes 532512 | tf_op jit(solution)/shard_map/ppermute | solution.py:451
  26.3 10.5 %collective-permute-done.2.refs_2_.refs_10_ = bf16[32,8320]{1,0:T(8,128)(2,1)S(1)} collective-permute-done((bf16[32,8320]{1,0:T(8,128)(2,1)S(1)}, bf16[32,8320]{1,0:T(8,128)(2,1)S(1)}, u32[]{:S(2)}, u32[]{:S(2)}) %collective-permute-start.2) | collective-permute-done | bytes 532512 | tf_op jit(solution)/shard_map/ppermute | solution.py:451
  41.4 1.9 %copy-done.1 = bf16[1,384,4096]{2,1,0:T(8,128)(2,1)S(1)} copy-done((bf16[1,384,4096]{2,1,0:T(8,128)(2,1)S(1)}, bf16[1,384,4096]{2,1,0:T(8,128)(2,1)}, u32[]{:S(2)}) %copy-start.1) | copy-done | bytes 3145752
  43.3 1.9 %copy-done.3 = bf16[1,384,4096]{2,1,0:T(8,128)(2,1)S(1)} copy-done((bf16[1,384,4096]{2,1,0:T(8,128)(2,1)S(1)}, bf16[1,384,4096]{2,1,0:T(8,128)(2,1)}, u32[]{:S(2)}) %copy-start.3) | copy-done | bytes 3145752
  45.2 7.6 %rows_backward.4 = (bf16[128,2176]{1,0:T(8,128)(2,1)S(1)}, bf16[128,2176]{1,0:T(8,128)(2,1)S(1)}, bf16[128,2176]{1,0:T(8,128)(2,1)S(1)}, bf16[128,2176]{1,0:T(8,128)(2,1)S(1)}, bf16[256,1152]{1,0:T(8,128)(2,1)S(1)}) custom-call(s32[2]{0:T(128)S(1)} %pad_add_fusion.place, s32[1]{0:T(128)} %get-tuple-element.102.hot, ...), custom_call_target="tpu_custom_call" | custom-call | flops 350000000 | bytes 700000 | tf_op jit(solution)/shard_map/rows_backward/pallas_call | solution.py:224
  54.1 6.2 %rows_backward.5 = (bf16[128,2176]{1,0:T(8,128)(2,1)S(1)}, bf16[128,2176]{1,0:T(8,128)(2,1)S(1)}, bf16[128,1152]{1,0:T(8,128)(2,1)S(1)}) custom-call(s32[2]{0:T(128)S(1)} %pad_add_fusion.place, s32[1]{0:T(128)} %get-tuple-element.102.hot, bf16[32,8320]{1,0:T(8,128)(2,1)S(1)} %get-tuple-element.67.refs_0_, bf16[32,8320]{1,0:T(8,128)(2,1)S(1)} %collective-permute-done.refs_1_, ...), custom_call_target="tpu_custom_call" | custom-call | flops 350000000 | bytes 700000 | tf_op jit(solution)/shard_map/rows_backward/pallas_call | solution.py:224
  60.3 1.6 collective-permute-start.14
  63.9 2.0 %collective-permute-start.9 = (bf16[32,8320]{1,0:T(8,128)(2,1)S(1)}, bf16[32,8320]{1,0:T(8,128)(2,1)S(1)}, u32[]{:S(2)}, u32[]{:S(2)}) collective-permute-start(bf16[32,8320]{1,0:T(8,128)(2,1)S(1)} %get-tuple-element.81), channel_id=1, source_target_pairs={{0,28},{4,24},{8,20},{12,16},{16,12},{20,8},{24,4},{28,0},{1,29},{... | collective-permute-start | bytes 1597448 | tf_op jit(solution)/shard_map/ppermute | solution.py:451
  67.5 1.6 collective-permute-start.29
  69.1 6.0 %rows_backward.6 = (bf16[64,2176]{1,0:T(8,128)(2,1)S(1)}, bf16[64,2176]{1,0:T(8,128)(2,1)S(1)}, bf16[64,1152]{1,0:T(8,128)(2,1)S(1)}) custom-call(s32[2]{0:T(128)S(1)} %pad_add_fusion.place, s32[1]{0:T(128)} %get-tuple-element.102.hot, bf16[32,8320]{1,0:T(8,128)(2,1)S(1)} %collective-permute-done.5.refs_0_.refs_3_.refs_4_, ...), custom_call_target="tpu_custom_call" | custom-call | flops 350000000 | bytes 700000 | tf_op jit(solution)/shard_map/rows_backward/pallas_call | solution.py:224
  76.2 2.7 %collective-permute-start.15 = (bf16[128,1152]{1,0:T(8,128)(2,1)S(1)}, bf16[128,1152]{1,0:T(8,128)(2,1)S(1)}, u32[]{:S(2)}, u32[]{:S(2)}) collective-permute-start(bf16[128,1152]{1,0:T(8,128)(2,1)S(1)} %get-tuple-element.88), channel_id=1, source_target_pairs={{0,2},{1,3},{2,0},{3,1},{4,6},{5,7},{6,4},{7,5},{8,10},{9,11},{10,... | collective-permute-start | bytes 884744 | tf_op jit(solution)/shard_map/ppermute | solution.py:451
  78.9 11.8 %collective-permute-done.8.refs_0_.refs_6_ = bf16[32,8320]{1,0:T(8,128)(2,1)S(1)} collective-permute-done((bf16[32,8320]{1,0:T(8,128)(2,1)S(1)}, bf16[32,8320]{1,0:T(8,128)(2,1)S(1)}, u32[]{:S(2)}, u32[]{:S(2)}) %collective-permute-start.8) | collective-permute-done | bytes 532512 | tf_op jit(solution)/shard_map/ppermute | solution.py:451
  90.6 6.0 %rows_backward.7 = (bf16[64,2176]{1,0:T(8,128)(2,1)S(1)}, bf16[64,2176]{1,0:T(8,128)(2,1)S(1)}, bf16[64,1152]{1,0:T(8,128)(2,1)S(1)}) custom-call(s32[2]{0:T(128)S(1)} %pad_add_fusion.place, s32[1]{0:T(128)} %get-tuple-element.102.hot, bf16[32,8320]{1,0:T(8,128)(2,1)S(1)} %collective-permute-done.8.refs_0_.refs_6_, ...), custom_call_target="tpu_custom_call" | custom-call | flops 350000000 | bytes 700000 | tf_op jit(solution)/shard_map/rows_backward/pallas_call | solution.py:224
  96.6 1.6 collective-permute-start.23
  98.8 2.2 %collective-permute-start.19 = (bf16[64,1152]{1,0:T(8,128)(2,1)S(1)}, bf16[64,1152]{1,0:T(8,128)(2,1)S(1)}, u32[]{:S(2)}, u32[]{:S(2)}) collective-permute-start(bf16[64,1152]{1,0:T(8,128)(2,1)S(1)} %get-tuple-element.97), channel_id=1, source_target_pairs={{0,2},{1,3},{2,0},{3,1},{4,6},{5,7},{6,4},{7,5},{8,10},{9,11},{10,... | collective-permute-start | bytes 442376 | tf_op jit(solution)/shard_map/ppermute | solution.py:451
  101.0 5.8 %collective-permute-done.19.got = bf16[64,1152]{1,0:T(8,128)(2,1)S(1)} collective-permute-done((bf16[64,1152]{1,0:T(8,128)(2,1)S(1)}, bf16[64,1152]{1,0:T(8,128)(2,1)S(1)}, u32[]{:S(2)}, u32[]{:S(2)}) %collective-permute-start.19) | collective-permute-done | bytes 147488 | tf_op jit(solution)/shard_map/ppermute | solution.py:451
  107.0 1.6 collective-permute-start.22
  108.6 11.7 %weights_backward.1 = (f32[384,4096]{1,0:T(8,128)}, f32[384,4096]{1,0:T(8,128)}, f32[384,4096]{1,0:T(8,128)}, f32[8,128]{1,0:T(8,128)S(1)}) custom-call(s32[1]{0:T(128)} %get-tuple-element.102.hot, bf16[32,8320]{1,0:T(8,128)(2,1)S(1)} %get-tuple-element.67.refs_0_, bf16[32,8320]{1,0:T(8,128)(2,1)S(1)} %collective-permute-done.refs_1_, ...), custom_call_target="tpu_custom_call" | custom-call | flops 650000000 | bytes 1300000 | tf_op jit(solution)/shard_map/weights_backward/pallas_call | solution.py:370
  121.6 3.4 %collective-permute-start.30 = (bf16[128,1152]{1,0:T(8,128)(2,1)S(1)}, bf16[128,1152]{1,0:T(8,128)(2,1)S(1)}, u32[]{:S(2)}, u32[]{:S(2)}) collective-permute-start(bf16[128,1152]{1,0:T(8,128)(2,1)S(1)} %get-tuple-element.116), channel_id=1, source_target_pairs={{0,2},{1,3},{2,0},{3,1},{4,6},{5,7},{6,4},{7,5},{8,10},{9,11},{10,... | collective-permute-start | bytes 884744 | tf_op jit(solution)/shard_map/ppermute | solution.py:451
  125.0 2.5 %collective-permute-start.37 = (f32[8,128]{1,0:T(8,128)S(1)}, f32[8,128]{1,0:T(8,128)S(1)}, u32[]{:S(2)}, u32[]{:S(2)}) collective-permute-start(f32[8,128]{1,0:T(8,128)S(1)} %add.21), channel_id=1, source_target_pairs={{0,3},{1,2},{2,1},{3,0},{4,7},{5,6},{6,5},{7,4},{8,11},{9,10},{10,... | collective-permute-start | bytes 12296 | tf_op jit(solution)/shard_map/ppermute | solution.py:451
  127.6 1.9 %collective-permute-start.35 = (f32[8,128]{1,0:T(8,128)S(1)}, f32[8,128]{1,0:T(8,128)S(1)}, u32[]{:S(2)}, u32[]{:S(2)}) collective-permute-start(f32[8,128]{1,0:T(8,128)S(1)} %add.21), channel_id=1, source_target_pairs={{0,1},{1,0},{2,3},{3,2},{4,5},{5,4},{6,7},{7,6},{8,9},{9,8},{10,11... | collective-permute-start | bytes 12296 | tf_op jit(solution)/shard_map/ppermute | solution.py:451
  130.7 4.7 %collective-permute-done.37 = f32[8,128]{1,0:T(8,128)S(1)} collective-permute-done((f32[8,128]{1,0:T(8,128)S(1)}, f32[8,128]{1,0:T(8,128)S(1)}, u32[]{:S(2)}, u32[]{:S(2)}) %collective-permute-start.37) | collective-permute-done | bytes 4128 | tf_op jit(solution)/shard_map/ppermute | solution.py:451
  135.4 7.2 %collective-permute-done.36 = f32[8,128]{1,0:T(8,128)S(1)} collective-permute-done((f32[8,128]{1,0:T(8,128)S(1)}, f32[8,128]{1,0:T(8,128)S(1)}, u32[]{:S(2)}, u32[]{:S(2)}) %collective-permute-start.36) | collective-permute-done | bytes 4128 | tf_op jit(solution)/shard_map/ppermute | solution.py:451
  143.2 2.1 %collective-permute-done.24.got = bf16[64,1152]{1,0:T(8,128)(2,1)S(1)} collective-permute-done((bf16[64,1152]{1,0:T(8,128)(2,1)S(1)}, bf16[64,1152]{1,0:T(8,128)(2,1)S(1)}, u32[]{:S(2)}, u32[]{:S(2)}) %collective-permute-start.24) | collective-permute-done | bytes 147488 | tf_op jit(solution)/shard_map/ppermute | solution.py:451
  146.2 3.6 %collective-permute-done.40 = f32[8,128]{1,0:T(8,128)S(1)} collective-permute-done((f32[8,128]{1,0:T(8,128)S(1)}, f32[8,128]{1,0:T(8,128)S(1)}, u32[]{:S(2)}, u32[]{:S(2)}) %collective-permute-start.40) | collective-permute-done | bytes 4128 | tf_op jit(solution)/shard_map/ppermute | solution.py:451
  151.3 2.1 %collective-permute-done.39 = f32[8,128]{1,0:T(8,128)S(1)} collective-permute-done((f32[8,128]{1,0:T(8,128)S(1)}, f32[8,128]{1,0:T(8,128)S(1)}, u32[]{:S(2)}, u32[]{:S(2)}) %collective-permute-start.39) | collective-permute-done | bytes 4128 | tf_op jit(solution)/shard_map/ppermute | solution.py:451
  154.9 2.0 %collective-permute-start.32 = (bf16[32,1152]{1,0:T(8,128)(2,1)S(1)}, bf16[32,1152]{1,0:T(8,128)(2,1)S(1)}, u32[]{:S(2)}, u32[]{:S(2)}) collective-permute-start(bf16[32,1152]{1,0:T(8,128)(2,1)S(1)} %get-tuple-element.119), channel_id=1, source_target_pairs={{0,16},{4,20},{8,24},{12,28},{16,0},{20,4},{24,8},{28,12},{1,17},{... | collective-permute-start | bytes 221192 | tf_op jit(solution)/shard_map/ppermute | solution.py:451
  159.8 2.3 %collective-permute-done.32.refs_18_ = bf16[32,1152]{1,0:T(8,128)(2,1)S(1)} collective-permute-done((bf16[32,1152]{1,0:T(8,128)(2,1)S(1)}, bf16[32,1152]{1,0:T(8,128)(2,1)S(1)}, u32[]{:S(2)}, u32[]{:S(2)}) %collective-permute-start.32) | collective-permute-done | bytes 73760 | tf_op jit(solution)/shard_map/ppermute | solution.py:451
  163.4 2.2 %home.1 = (bf16[256,1024]{1,0:T(8,128)(2,1)}, f32[8,256]{1,0:T(8,128)}) custom-call(s32[2]{0:T(128)S(1)} %pad_add_fusion.place, f32[8,256]{1,0:T(8,128)S(1)} %bitcast.25, s32[1,256]{1,0:T(1,128)S(1)} %bitcast.27, bf16[32,8320]{1,0:T(8,128)(2,1)S(1)} %get-tuple-element.67.refs_0_, bf16[32,8320]{1,0:T(8,128)(2,1)S(1)} %collective-permute-done.refs_1_, ...), custom_call_target="tpu_custom_call" | custom-call | flops 200000000 | bytes 400000 | tf_op jit(solution)/shard_map/home/pallas_call | solution.py:430
  (91 shorter events, 25.5 us)
Async XLA Ops:
  9.4 16.9 %collective-permute-start.4 = (bf16[32,8320]{1,0:T(8,128)(2,1)S(1)}, bf16[32,8320]{1,0:T(8,128)(2,1)S(1)}, u32[]{:S(2)}, u32[]{:S(2)}) collective-permute-start(bf16[32,8320]{1,0:T(8,128)(2,1)S(1)} %get-tuple-element.70.refs_0_.refs_8_), channel_id=1, source_target_pairs={{0,24},{4,28},{8,16},{12,20},{16,8},{20,12},{24,0},{28,4},{1,25},{... | collective-permute-start | bytes 1597448 | tf_op jit(solution)/shard_map/ppermute | solution.py:451
  13.3 23.5 %collective-permute-start.2 = (bf16[32,8320]{1,0:T(8,128)(2,1)S(1)}, bf16[32,8320]{1,0:T(8,128)(2,1)S(1)}, u32[]{:S(2)}, u32[]{:S(2)}) collective-permute-start(bf16[32,8320]{1,0:T(8,128)(2,1)S(1)} %get-tuple-element.70.refs_0_.refs_8_), channel_id=1, source_target_pairs={{0,16},{4,20},{8,24},{12,28},{16,0},{20,4},{24,8},{28,12},{1,17},{... | collective-permute-start | bytes 1597448 | tf_op jit(solution)/shard_map/ppermute | solution.py:451
  13.8 23.3 %collective-permute-start.1 = (bf16[32,8320]{1,0:T(8,128)(2,1)S(1)}, bf16[32,8320]{1,0:T(8,128)(2,1)S(1)}, u32[]{:S(2)}, u32[]{:S(2)}) collective-permute-start(bf16[32,8320]{1,0:T(8,128)(2,1)S(1)} %get-tuple-element.70.refs_0_.refs_8_), channel_id=1, source_target_pairs={{0,8},{4,12},{8,0},{12,4},{16,24},{20,28},{24,16},{28,20},{1,9},{5... | collective-permute-start | bytes 1597448 | tf_op jit(solution)/shard_map/ppermute | solution.py:451
  14.0 23.7 %collective-permute-start.10 = (bf16[32,8320]{1,0:T(8,128)(2,1)S(1)}, bf16[32,8320]{1,0:T(8,128)(2,1)S(1)}, u32[]{:S(2)}, u32[]{:S(2)}) collective-permute-start(bf16[32,8320]{1,0:T(8,128)(2,1)S(1)} %get-tuple-element.70.refs_0_.refs_8_), channel_id=1, source_target_pairs={{0,4},{4,0},{8,12},{12,8},{16,20},{20,16},{24,28},{28,24},{1,5},{5... | collective-permute-start | bytes 1597448 | tf_op jit(solution)/shard_map/ppermute | solution.py:451
  26.3 12.8 %collective-permute-start.13 = (bf16[32,8320]{1,0:T(8,128)(2,1)S(1)}, bf16[32,8320]{1,0:T(8,128)(2,1)S(1)}, u32[]{:S(2)}, u32[]{:S(2)}) collective-permute-start(bf16[32,8320]{1,0:T(8,128)(2,1)S(1)} %collective-permute-done.4.refs_3_.refs_11_), channel_id=1, source_target_pairs={{0,4},{4,0},{8,12},{12,8},{16,20},{20,16},{24,28},{28,24},{1,5},{5... | collective-permute-start | bytes 1597448 | tf_op jit(solution)/shard_map/ppermute | solution.py:451
  37.4 15.4 %collective-permute-start = (bf16[32,8320]{1,0:T(8,128)(2,1)S(1)}, bf16[32,8320]{1,0:T(8,128)(2,1)S(1)}, u32[]{:S(2)}, u32[]{:S(2)}) collective-permute-start(bf16[32,8320]{1,0:T(8,128)(2,1)S(1)} %get-tuple-element.68), channel_id=1, source_target_pairs={{0,4},{4,0},{8,12},{12,8},{16,20},{20,16},{24,28},{28,24},{1,5},{5... | collective-permute-start | bytes 1597448 | tf_op jit(solution)/shard_map/ppermute | solution.py:451
  37.7 15.3 %collective-permute-start.3 = (bf16[32,8320]{1,0:T(8,128)(2,1)S(1)}, bf16[32,8320]{1,0:T(8,128)(2,1)S(1)}, u32[]{:S(2)}, u32[]{:S(2)}) collective-permute-start(bf16[32,8320]{1,0:T(8,128)(2,1)S(1)} %get-tuple-element.71), channel_id=1, source_target_pairs={{0,8},{4,12},{8,0},{12,4},{16,24},{20,28},{24,16},{28,20},{1,9},{5... | collective-permute-start | bytes 1597448 | tf_op jit(solution)/shard_map/ppermute | solution.py:451
  39.2 14.9 %collective-permute-start.6 = (bf16[32,8320]{1,0:T(8,128)(2,1)S(1)}, bf16[32,8320]{1,0:T(8,128)(2,1)S(1)}, u32[]{:S(2)}, u32[]{:S(2)}) collective-permute-start(bf16[32,8320]{1,0:T(8,128)(2,1)S(1)} %get-tuple-element.75), channel_id=1, source_target_pairs={{0,16},{4,20},{8,24},{12,28},{16,0},{20,4},{24,8},{28,12},{1,17},{... | collective-permute-start | bytes 1597448 | tf_op jit(solution)/shard_map/ppermute | solution.py:451
  39.8 22.8 %collective-permute-start.5 = (bf16[32,8320]{1,0:T(8,128)(2,1)S(1)}, bf16[32,8320]{1,0:T(8,128)(2,1)S(1)}, u32[]{:S(2)}, u32[]{:S(2)}) collective-permute-start(bf16[32,8320]{1,0:T(8,128)(2,1)S(1)} %get-tuple-element.73), channel_id=1, source_target_pairs={{0,12},{4,8},{8,4},{12,0},{16,28},{20,24},{24,20},{28,16},{1,13},{... | collective-permute-start | bytes 1597448 | tf_op jit(solution)/shard_map/ppermute | solution.py:451
  40.7 23.3 %collective-permute-start.7 = (bf16[32,8320]{1,0:T(8,128)(2,1)S(1)}, bf16[32,8320]{1,0:T(8,128)(2,1)S(1)}, u32[]{:S(2)}, u32[]{:S(2)}) collective-permute-start(bf16[32,8320]{1,0:T(8,128)(2,1)S(1)} %get-tuple-element.77), channel_id=1, source_target_pairs={{0,20},{4,16},{8,28},{12,24},{16,4},{20,0},{24,12},{28,8},{1,21},{... | collective-permute-start | bytes 1597448 | tf_op jit(solution)/shard_map/ppermute | solution.py:451
  52.8 14.5 %collective-permute-start.27 = (bf16[128,2176]{1,0:T(8,128)(2,1)S(1)}, bf16[128,2176]{1,0:T(8,128)(2,1)S(1)}, u32[]{:S(2)}, u32[]{:S(2)}) collective-permute-start(bf16[128,2176]{1,0:T(8,128)(2,1)S(1)} %get-tuple-element.111), channel_id=1, source_target_pairs={{0,4},{4,0},{8,12},{12,8},{16,20},{20,16},{24,28},{28,24},{1,5},{5... | collective-permute-start | bytes 1671176 | tf_op jit(solution)/shard_map/ppermute | solution.py:451
  52.9 14.5 %collective-permute-start.28 = (bf16[128,2176]{1,0:T(8,128)(2,1)S(1)}, bf16[128,2176]{1,0:T(8,128)(2,1)S(1)}, u32[]{:S(2)}, u32[]{:S(2)}) collective-permute-start(bf16[128,2176]{1,0:T(8,128)(2,1)S(1)} %get-tuple-element.112), channel_id=1, source_target_pairs={{0,4},{4,0},{8,12},{12,8},{16,20},{20,16},{24,28},{28,24},{1,5},{5... | collective-permute-start | bytes 1671176 | tf_op jit(solution)/shard_map/ppermute | solution.py:451
  60.3 15.6 %collective-permute-start.14 = (bf16[128,2176]{1,0:T(8,128)(2,1)S(1)}, bf16[128,2176]{1,0:T(8,128)(2,1)S(1)}, u32[]{:S(2)}, u32[]{:S(2)}) collective-permute-start(bf16[128,2176]{1,0:T(8,128)(2,1)S(1)} %get-tuple-element.86), channel_id=1, source_target_pairs={{0,1},{1,0},{2,3},{3,2},{4,5},{5,4},{6,7},{7,6},{8,9},{9,8},{10,11... | collective-permute-start | bytes 1671176 | tf_op jit(solution)/shard_map/ppermute | solution.py:451
  63.9 14.9 %collective-permute-start.9 = (bf16[32,8320]{1,0:T(8,128)(2,1)S(1)}, bf16[32,8320]{1,0:T(8,128)(2,1)S(1)}, u32[]{:S(2)}, u32[]{:S(2)}) collective-permute-start(bf16[32,8320]{1,0:T(8,128)(2,1)S(1)} %get-tuple-element.81), channel_id=1, source_target_pairs={{0,28},{4,24},{8,20},{12,16},{16,12},{20,8},{24,4},{28,0},{1,29},{... | collective-permute-start | bytes 1597448 | tf_op jit(solution)/shard_map/ppermute | solution.py:451
  65.9 24.7 %collective-permute-start.8 = (bf16[32,8320]{1,0:T(8,128)(2,1)S(1)}, bf16[32,8320]{1,0:T(8,128)(2,1)S(1)}, u32[]{:S(2)}, u32[]{:S(2)}) collective-permute-start(bf16[32,8320]{1,0:T(8,128)(2,1)S(1)} %get-tuple-element.79), channel_id=1, source_target_pairs={{0,24},{4,28},{8,16},{12,20},{16,8},{20,12},{24,0},{28,4},{1,25},{... | collective-permute-start | bytes 1597448 | tf_op jit(solution)/shard_map/ppermute | solution.py:451
  67.5 52.8 %collective-permute-start.29 = (bf16[128,2176]{1,0:T(8,128)(2,1)S(1)}, bf16[128,2176]{1,0:T(8,128)(2,1)S(1)}, u32[]{:S(2)}, u32[]{:S(2)}) collective-permute-start(bf16[128,2176]{1,0:T(8,128)(2,1)S(1)} %get-tuple-element.114), channel_id=1, source_target_pairs={{0,1},{1,0},{2,3},{3,2},{4,5},{5,4},{6,7},{7,6},{8,9},{9,8},{10,11... | collective-permute-start | bytes 1671176 | tf_op jit(solution)/shard_map/ppermute | solution.py:451
  75.1 23.6 %collective-permute-start.18 = (bf16[64,2176]{1,0:T(8,128)(2,1)S(1)}, bf16[64,2176]{1,0:T(8,128)(2,1)S(1)}, u32[]{:S(2)}, u32[]{:S(2)}) collective-permute-start(bf16[64,2176]{1,0:T(8,128)(2,1)S(1)} %get-tuple-element.95), channel_id=1, source_target_pairs={{0,1},{1,0},{2,3},{3,2},{4,5},{5,4},{6,7},{7,6},{8,9},{9,8},{10,11... | collective-permute-start | bytes 835592 | tf_op jit(solution)/shard_map/ppermute | solution.py:451
  76.2 51.4 %collective-permute-start.15 = (bf16[128,1152]{1,0:T(8,128)(2,1)S(1)}, bf16[128,1152]{1,0:T(8,128)(2,1)S(1)}, u32[]{:S(2)}, u32[]{:S(2)}) collective-permute-start(bf16[128,1152]{1,0:T(8,128)(2,1)S(1)} %get-tuple-element.88), channel_id=1, source_target_pairs={{0,2},{1,3},{2,0},{3,1},{4,6},{5,7},{6,4},{7,5},{8,10},{9,11},{10,... | collective-permute-start | bytes 884744 | tf_op jit(solution)/shard_map/ppermute | solution.py:451
  96.6 28.4 %collective-permute-start.23 = (bf16[64,2176]{1,0:T(8,128)(2,1)S(1)}, bf16[64,2176]{1,0:T(8,128)(2,1)S(1)}, u32[]{:S(2)}, u32[]{:S(2)}) collective-permute-start(bf16[64,2176]{1,0:T(8,128)(2,1)S(1)} %get-tuple-element.104), channel_id=1, source_target_pairs={{0,1},{1,0},{2,3},{3,2},{4,5},{5,4},{6,7},{7,6},{8,9},{9,8},{10,11... | collective-permute-start | bytes 835592 | tf_op jit(solution)/shard_map/ppermute | solution.py:451
  98.8 8.0 %collective-permute-start.19 = (bf16[64,1152]{1,0:T(8,128)(2,1)S(1)}, bf16[64,1152]{1,0:T(8,128)(2,1)S(1)}, u32[]{:S(2)}, u32[]{:S(2)}) collective-permute-start(bf16[64,1152]{1,0:T(8,128)(2,1)S(1)} %get-tuple-element.97), channel_id=1, source_target_pairs={{0,2},{1,3},{2,0},{3,1},{4,6},{5,7},{6,4},{7,5},{8,10},{9,11},{10,... | collective-permute-start | bytes 442376 | tf_op jit(solution)/shard_map/ppermute | solution.py:451
  106.9 20.7 %collective-permute-start.20 = (bf16[32,1152]{1,0:T(8,128)(2,1)S(1)}, bf16[32,1152]{1,0:T(8,128)(2,1)S(1)}, u32[]{:S(2)}, u32[]{:S(2)}) collective-permute-start(bf16[32,1152]{1,0:T(8,128)(2,1)S(1)} %get-tuple-element.98), channel_id=1, source_target_pairs={{0,12},{4,8},{8,4},{12,0},{16,28},{20,24},{24,20},{28,16},{1,13},{... | collective-permute-start | bytes 221192 | tf_op jit(solution)/shard_map/ppermute | solution.py:451
  107.0 22.7 %collective-permute-start.22 = (bf16[32,1152]{1,0:T(8,128)(2,1)S(1)}, bf16[32,1152]{1,0:T(8,128)(2,1)S(1)}, u32[]{:S(2)}, u32[]{:S(2)}) collective-permute-start(bf16[32,1152]{1,0:T(8,128)(2,1)S(1)} %get-tuple-element.100), channel_id=1, source_target_pairs={{0,20},{4,16},{8,28},{12,24},{16,4},{20,0},{24,12},{28,8},{1,21},{... | collective-permute-start | bytes 221192 | tf_op jit(solution)/shard_map/ppermute | solution.py:451
  121.6 28.2 %collective-permute-start.30 = (bf16[128,1152]{1,0:T(8,128)(2,1)S(1)}, bf16[128,1152]{1,0:T(8,128)(2,1)S(1)}, u32[]{:S(2)}, u32[]{:S(2)}) collective-permute-start(bf16[128,1152]{1,0:T(8,128)(2,1)S(1)} %get-tuple-element.116), channel_id=1, source_target_pairs={{0,2},{1,3},{2,0},{3,1},{4,6},{5,7},{6,4},{7,5},{8,10},{9,11},{10,... | collective-permute-start | bytes 884744 | tf_op jit(solution)/shard_map/ppermute | solution.py:451
  125.0 10.4 %collective-permute-start.37 = (f32[8,128]{1,0:T(8,128)S(1)}, f32[8,128]{1,0:T(8,128)S(1)}, u32[]{:S(2)}, u32[]{:S(2)}) collective-permute-start(f32[8,128]{1,0:T(8,128)S(1)} %add.21), channel_id=1, source_target_pairs={{0,3},{1,2},{2,1},{3,0},{4,7},{5,6},{6,5},{7,4},{8,11},{9,10},{10,... | collective-permute-start | bytes 12296 | tf_op jit(solution)/shard_map/ppermute | solution.py:451
  127.6 15.0 %collective-permute-start.36 = (f32[8,128]{1,0:T(8,128)S(1)}, f32[8,128]{1,0:T(8,128)S(1)}, u32[]{:S(2)}, u32[]{:S(2)}) collective-permute-start(f32[8,128]{1,0:T(8,128)S(1)} %add.21), channel_id=1, source_target_pairs={{0,2},{1,3},{2,0},{3,1},{4,6},{5,7},{6,4},{7,5},{8,10},{9,11},{10,... | collective-permute-start | bytes 12296 | tf_op jit(solution)/shard_map/ppermute | solution.py:451
  127.6 14.9 %collective-permute-start.35 = (f32[8,128]{1,0:T(8,128)S(1)}, f32[8,128]{1,0:T(8,128)S(1)}, u32[]{:S(2)}, u32[]{:S(2)}) collective-permute-start(f32[8,128]{1,0:T(8,128)S(1)} %add.21), channel_id=1, source_target_pairs={{0,1},{1,0},{2,3},{3,2},{4,5},{5,4},{6,7},{7,6},{8,9},{9,8},{10,11... | collective-permute-start | bytes 12296 | tf_op jit(solution)/shard_map/ppermute | solution.py:451
  129.7 15.6 %collective-permute-start.24 = (bf16[64,1152]{1,0:T(8,128)(2,1)S(1)}, bf16[64,1152]{1,0:T(8,128)(2,1)S(1)}, u32[]{:S(2)}, u32[]{:S(2)}) collective-permute-start(bf16[64,1152]{1,0:T(8,128)(2,1)S(1)} %get-tuple-element.106), channel_id=1, source_target_pairs={{0,2},{1,3},{2,0},{3,1},{4,6},{5,7},{6,4},{7,5},{8,10},{9,11},{10,... | collective-permute-start | bytes 442376 | tf_op jit(solution)/shard_map/ppermute | solution.py:451
  135.4 18.9 %collective-permute-start.16 = (bf16[32,1152]{1,0:T(8,128)(2,1)S(1)}, bf16[32,1152]{1,0:T(8,128)(2,1)S(1)}, u32[]{:S(2)}, u32[]{:S(2)}) collective-permute-start(bf16[32,1152]{1,0:T(8,128)(2,1)S(1)} %get-tuple-element.90), channel_id=1, source_target_pairs={{0,4},{4,0},{8,12},{12,8},{16,20},{20,16},{24,28},{28,24},{1,5},{5... | collective-permute-start | bytes 221192 | tf_op jit(solution)/shard_map/ppermute | solution.py:451
  142.6 12.4 %collective-permute-start.17 = (bf16[32,1152]{1,0:T(8,128)(2,1)S(1)}, bf16[32,1152]{1,0:T(8,128)(2,1)S(1)}, u32[]{:S(2)}, u32[]{:S(2)}) collective-permute-start(bf16[32,1152]{1,0:T(8,128)(2,1)S(1)} %get-tuple-element.91), channel_id=1, source_target_pairs={{0,8},{4,12},{8,0},{12,4},{16,24},{20,28},{24,16},{28,20},{1,9},{5... | collective-permute-start | bytes 221192 | tf_op jit(solution)/shard_map/ppermute | solution.py:451
  142.6 14.4 %collective-permute-start.21 = (bf16[32,1152]{1,0:T(8,128)(2,1)S(1)}, bf16[32,1152]{1,0:T(8,128)(2,1)S(1)}, u32[]{:S(2)}, u32[]{:S(2)}) collective-permute-start(bf16[32,1152]{1,0:T(8,128)(2,1)S(1)} %get-tuple-element.99), channel_id=1, source_target_pairs={{0,16},{4,20},{8,24},{12,28},{16,0},{20,4},{24,8},{28,12},{1,17},{... | collective-permute-start | bytes 221192 | tf_op jit(solution)/shard_map/ppermute | solution.py:451
  154.9 7.2 %collective-permute-start.32 = (bf16[32,1152]{1,0:T(8,128)(2,1)S(1)}, bf16[32,1152]{1,0:T(8,128)(2,1)S(1)}, u32[]{:S(2)}, u32[]{:S(2)}) collective-permute-start(bf16[32,1152]{1,0:T(8,128)(2,1)S(1)} %get-tuple-element.119), channel_id=1, source_target_pairs={{0,16},{4,20},{8,24},{12,28},{16,0},{20,4},{24,8},{28,12},{1,17},{... | collective-permute-start | bytes 221192 | tf_op jit(solution)/shard_map/ppermute | solution.py:451
  157.0 6.4 %collective-permute-start.33 = (bf16[32,1152]{1,0:T(8,128)(2,1)S(1)}, bf16[32,1152]{1,0:T(8,128)(2,1)S(1)}, u32[]{:S(2)}, u32[]{:S(2)}) collective-permute-start(bf16[32,1152]{1,0:T(8,128)(2,1)S(1)} %get-tuple-element.120), channel_id=1, source_target_pairs={{0,24},{4,28},{8,16},{12,20},{16,8},{20,12},{24,0},{28,4},{1,25},{... | collective-permute-start | bytes 221192 | tf_op jit(solution)/shard_map/ppermute | solution.py:451
  (19 other events, 181.5 us)
where the time goes:
time: 167 us
  waiting for transfers between devices  69 us (41%)
  Pallas kernels  44.8 us (27%)
  starting transfers between devices  41.1 us (25%)
  local copies, waits for them, and re-layouts  9.02 us (5%)
  between operations  2.7 us (2%)
    ppermute x41, waiting for transfers between devices, swap(): return lax.ppermute(value, axis, [(i, i ^ mask) for i in range(size)])  69 us
    ppermute x41, starting transfers between devices, swap(): return lax.ppermute(value, axis, [(i, i ^ mask) for i in range(size)])  41.1 us
    pallas_call x4, Pallas kernels, rows_backward(): call(functools.partial(rows_body, pieces, cap, width, n_dp, guarded), 'ro...  25.7 us
    pallas_call x1, Pallas kernels, weights_backward(): call(functools.partial(weights_body, len(cold), len(extra), len(acts), ca...  11.7 us
    unnamed x20, local copies, waits for them, and re-layouts  8.51 us
    pallas_call x1, Pallas kernels, dispatch(): call(functools.partial(dispatch_body, experts, cap, width), 'dispatch', [...  3.94 us
  transfers between devices with their start and end apart: 41, of which 20 were waited for; matrix products, arithmetic and copies ran while one was open for 0% of the time, Pallas kernels for 23%

commit v1 on v0

v1 whole, which is shorter than its diff:
```python
import functools

import jax
import jax.numpy as jnp
from jax import lax
from jax.experimental import pallas as pl
from jax.experimental.pallas import tpu as pltpu
from jax.sharding import PartitionSpec as P

aux_weight = 1.0
LANES = 128
COUNT_LANE = 64
RATE = 1e9
SQUARE_LANE = 8
BF16 = jnp.bfloat16
F32 = jnp.float32
ANY = pl.BlockSpec(memory_space=pl.ANY)
VMEM = pl.BlockSpec(memory_space=pltpu.VMEM)
SMEM = pl.BlockSpec(memory_space=pltpu.SMEM)
HBM = pl.BlockSpec(memory_space=pltpu.HBM)


def call(body, name, out_shape, in_specs, out_specs, scratch, micros, room, earlier=(), **extra):
    skipped = len(earlier)

    def without(*refs):
        body(*refs[skipped:])

    kernel = pl.pallas_call(
        without,
        name=name,
        out_shape=out_shape,
        in_specs=[ANY] * skipped + in_specs,
        out_specs=out_specs,
        scratch_shapes=scratch,
        cost_estimate=pl.CostEstimate(
            flops=int(micros * RATE), bytes_accessed=1000, transcendentals=0
        ),
        compiler_params=pltpu.CompilerParams(vmem_limit_bytes=room * 1024 * 1024),
        **extra,
    )
    return functools.partial(kernel, *earlier)


def lane_iota(shape):
    return lax.broadcasted_iota(jnp.int32, shape, len(shape) - 1)


def routing(ids, me, cap, experts):
    rows = ids.shape[1]
    expert = lax.broadcasted_iota(jnp.int32, (experts, rows), 0)
    onehot = jnp.where(expert == ids, 1.0, 0.0)
    before = lax.broadcasted_iota(jnp.int32, (rows, rows), 0) < lane_iota((rows, rows))
    earlier = jnp.dot(
        onehot.astype(BF16), jnp.where(before, 1.0, 0.0).astype(BF16), preferred_element_type=F32
    )
    rank = jnp.sum(earlier * onehot, axis=0, keepdims=True).astype(jnp.int32)
    slot = jnp.where(rank < cap, (ids ^ me) * cap + rank, experts * cap + rank - cap)
    slots = -(-(experts + 1) * cap // LANES) * LANES
    spread = lax.broadcasted_iota(jnp.int32, (slots, rows), 0) == slot
    return onehot, jnp.where(spread, 1.0, 0.0)


def softmax(logits):
    scores = jnp.exp(logits - jnp.max(logits, axis=0, keepdims=True))
    return scores / jnp.sum(scores, axis=0, keepdims=True)


def dispatch_body(plan, experts, cap, width, x_hbm, dy_hbm, logits_hbm, ids_hbm, *refs):
    outs, hot = refs[: len(plan)], refs[len(plan)]
    held, logits, ids, sems = refs[len(plan) + 1 :]
    loads = [
        pltpu.make_async_copy(ids_hbm, ids, sems.at[0]),
        pltpu.make_async_copy(logits_hbm, logits, sems.at[1]),
        pltpu.make_async_copy(x_hbm, held.at[0], sems.at[2]),
        pltpu.make_async_copy(dy_hbm, held.at[1], sems.at[3]),
    ]
    for load in loads:
        load.start()
    me = lax.axis_index("expert")
    slots = (experts + 1) * cap
    loads[0].wait()
    loads[1].wait()
    expert_ids = ids[...]
    onehot, spread = routing(expert_ids, me, cap, experts)
    spread = spread[:slots]
    gate = jnp.sum(softmax(logits[...]) * onehot, axis=0, keepdims=True)
    gate = gate.astype(BF16).astype(F32)
    mine = jnp.sum(jnp.where(expert_ids == me, 1, 0))
    hot[0] = jnp.where(mine > cap, 1, 0)
    counts = jnp.sum(onehot, axis=1, keepdims=True)
    expert = lax.broadcasted_iota(jnp.int32, (experts, LANES), 0)
    counts = jnp.sum(
        jnp.where(lane_iota((experts, LANES)) - COUNT_LANE == expert, counts, 0.0),
        axis=0,
        keepdims=True,
    )
    gates = jnp.sum(spread * gate, axis=1, keepdims=True)
    pad = jnp.where(lane_iota((slots, LANES)) == 0, gates, counts).astype(BF16)
    places = [(m, outs[i], j * cap) for i, held_by in enumerate(plan) for j, m in enumerate(held_by)]
    for m, out, first in places:
        out[first : first + cap, 2 * width :] = pad[m * cap : (m + 1) * cap]
    spread = spread.astype(BF16)
    tile = 1024
    for half in range(2):
        loads[2 + half].wait()
        for at in range(0, width, tile):
            moved = jnp.dot(
                spread, held[half, :, at : at + tile], preferred_element_type=F32
            ).astype(BF16)
            for m, out, first in places:
                out[first : first + cap, half * width + at : half * width + at + tile] = moved[
                    m * cap : (m + 1) * cap
                ]


def dispatch(rows_x, rows_dy, logits, ids, experts, cap, plan):
    rows, width = rows_x.shape
    wide = 2 * width + LANES
    return call(
        functools.partial(dispatch_body, plan, experts, cap, width),
        "dispatch",
        [jax.ShapeDtypeStruct((len(held_by) * cap, wide), BF16) for held_by in plan]
        + [jax.ShapeDtypeStruct((1,), jnp.int32)],
        [HBM] * 4,
        [VMEM] * len(plan) + [SMEM],
        [
            pltpu.VMEM((2, rows, width), BF16),
            pltpu.VMEM(logits.shape, F32),
            pltpu.VMEM(ids.shape, jnp.int32),
            pltpu.SemaphoreType.DMA((4,)),
        ],
        6,
        58,
    )(rows_x, rows_dy, logits, ids)


def split_lanes(total):
    lane = lane_iota((total.shape[0], LANES))
    first = total.astype(BF16).astype(F32)
    second = (total - first).astype(BF16).astype(F32)
    third = total - first - second
    return jnp.where(
        lane == 0, first, jnp.where(lane == 1, second, jnp.where(lane == 2, third, 0.0))
    ).astype(BF16)


def rows_body(ranges, width, n_dp, guarded, hot, *refs):
    pieces = len(ranges)
    sources, weights = refs[:pieces], refs[pieces : pieces + 3]
    outs = refs[pieces + 3 : -2]
    held, piece_sems = refs[-2:]
    hidden_units = weights[0].shape[0]
    rows = held.shape[0]

    def work():
        copies, at = [], 0
        for p in range(pieces):
            first, count = ranges[p]
            copies.append(
                pltpu.make_async_copy(
                    sources[p].at[pl.ds(first, count), :],
                    held.at[pl.ds(at, count), :],
                    piece_sems.at[p],
                )
            )
            at += count
        for copy in copies:
            copy.start()
        for copy in copies:
            copy.wait()
        pre_gate, pre_up, grad = [
            lax.dot_general(
                held[:, side * width : (side + 1) * width],
                weight[...],
                (((1,), (1,)), ((), ())),
                preferred_element_type=F32,
            )
            for side, weight in zip((0, 0, 1), weights)
        ]
        gate = held[:, 2 * width :].astype(F32)[:, 0:1]
        sigmoid = jax.nn.sigmoid(pre_gate)
        active = pre_gate * sigmoid
        hidden = (active * pre_up).astype(BF16)
        hidden_f = hidden.astype(F32)
        gate_part = jnp.sum(hidden_f * grad, axis=1, keepdims=True)
        grad_hidden = grad * gate
        d_up = (grad_hidden * active).astype(BF16)
        d_pre = (grad_hidden * pre_up * sigmoid * (1.0 + pre_gate * (1.0 - sigmoid))).astype(BF16)
        outs[-1][:, :hidden_units] = d_pre
        outs[-1][:, hidden_units : 2 * hidden_units] = d_up
        outs[-1][:, 2 * hidden_units :] = (hidden_f * gate).astype(BF16)
        lanes = split_lanes(gate_part)
        cut = width // n_dp
        part = n_dp // 2 * cut + LANES
        me = lax.axis_index("dp")
        for half in range(2):
            places = [(outs[half], 0)]
            if guarded:
                places.append((outs[2 + half], rows // 2))
            for out, first in places:
                count = out.shape[0]
                out[:, part - LANES :] = lanes[first : first + count]
                for p in range(n_dp // 2):
                    column = pl.multiple_of((me ^ (2 * p + half)) * cut, cut)
                    out[:, p * cut : (p + 1) * cut] = (
                        jnp.dot(
                            d_pre[first : first + count],
                            weights[0][:, pl.ds(column, cut)],
                            preferred_element_type=F32,
                        )
                        + jnp.dot(
                            d_up[first : first + count],
                            weights[1][:, pl.ds(column, cut)],
                            preferred_element_type=F32,
                        )
                    ).astype(BF16)

    if guarded:

        @pl.when(hot[0] == 1)
        def _():
            work()

        @pl.when(hot[0] != 1)
        def _():
            for out in outs:
                out[...] = jnp.zeros_like(out)
    else:
        work()


def rows_backward(earlier, hot, parts, weights, n_dp, guarded, micros=0.001):
    width = weights[0].shape[1]
    hidden_units = weights[0].shape[0]
    sources = [source for source, _, _ in parts]
    ranges = [(first, count) for _, first, count in parts]
    rows = sum(count for _, count in ranges)
    part = width // 2 + LANES
    shapes = [(rows // 2, part)] * 4 if guarded else [(rows, part)] * 2
    return call(
        functools.partial(rows_body, ranges, width, n_dp, guarded),
        "rows_backward",
        [jax.ShapeDtypeStruct(s, BF16) for s in shapes]
        + [jax.ShapeDtypeStruct((rows, 3 * hidden_units), BF16)],
        [SMEM] + [ANY] * len(sources) + [VMEM] * 3,
        [VMEM] * (len(shapes) + 1),
        [
            pltpu.VMEM((rows, 2 * width + LANES), BF16),
            pltpu.SemaphoreType.DMA((len(sources),)),
        ],
        micros,
        20,
        earlier,
    )(hot, *sources, *weights)


def merge_body(own, peers, out):
    out[...] = own[...] + peers[...]


def merge(earlier, own, peers):
    return call(
        merge_body,
        "merge",
        [jax.ShapeDtypeStruct(own.shape, BF16)],
        [VMEM] * 2,
        [VMEM],
        [],
        0.001,
        8,
        earlier,
    )(own, peers)


def sum_of(parts, columns):
    return functools.reduce(jnp.add, [part[:, columns].astype(F32) for part in parts])


def fold_body(cut, parts, count, *refs):
    given, outs = refs[:count], refs[count:]
    total = sum_of(given, slice(parts * cut, None))
    lanes = split_lanes(jnp.sum(total, axis=1, keepdims=True))
    for out in outs:
        out[:, parts // 2 * cut :] = lanes
    for p in range(parts):
        columns = slice(p * cut, (p + 1) * cut)
        outs[p % 2][:, p // 2 * cut : (p // 2 + 1) * cut] = sum_of(given, columns).astype(BF16)


def fold(earlier, given, cut):
    rows = given[0].shape[0]
    parts = (given[0].shape[1] - LANES) // cut
    shape = jax.ShapeDtypeStruct((rows, parts // 2 * cut + LANES), BF16)
    return call(
        functools.partial(fold_body, cut, parts, len(given)),
        "fold",
        [shape] * 2,
        [VMEM] * len(given),
        [VMEM] * 2,
        [],
        0.001,
        8,
        earlier,
    )(*given)


def tree(values):
    while len(values) > 1:
        values = [a + b for a, b in zip(values[::2], values[1::2])]
    return values[0]


def last_body(cut, cap, places, count, *refs):
    pairs = len(places)
    squares, given, outs = refs[:count], refs[count : count + 2 * pairs], refs[count + 2 * pairs :]
    total = tree([part[0:1, 0:1] for part in squares])
    lane = lane_iota((1, LANES))
    square = jnp.zeros((1, LANES), F32)
    for i in range(3):
        part = total.astype(BF16).astype(F32)
        square = jnp.where(lane == SQUARE_LANE + i, part, square)
        total = total - part
    for i, where in enumerate(places):
        pair = given[2 * i : 2 * i + 2]
        whole = sum_of(pair, slice(0, cut)).astype(BF16)
        gates = jnp.sum(sum_of(pair, slice(cut, None)), axis=1, keepdims=True)
        lanes = jnp.where(lane == 0, gates, square).astype(BF16)
        for start, out, first in where:
            outs[out][first : first + cap, :cut] = whole[start : start + cap]
            outs[out][first : first + cap, cut:] = lanes[start : start + cap]


def last(earlier, squares, pairs, chunks, masks, cut, cap):
    places = []
    for i, chunk in enumerate(chunks):
        first = cap if i == len(chunks) - 1 else 0
        places.append([(j * cap, masks.index(m), first) for j, m in enumerate(chunk) if m in masks])
    return call(
        functools.partial(last_body, cut, cap, places, len(squares)),
        "last",
        [jax.ShapeDtypeStruct((cap if m % 2 else 2 * cap, cut + LANES), BF16) for m in masks],
        [VMEM] * (len(squares) + 2 * len(pairs)),
        [VMEM] * len(masks),
        [],
        0.001,
        12,
        earlier,
    )(*squares, *[part for pair in pairs for part in pair])


def weights_body(ranges, cold_pieces, acts_count, width, tile, hot, *refs):
    pieces = len(ranges)
    sources, acts = refs[:pieces], refs[pieces : pieces + acts_count]
    outs, squares = refs[pieces + acts_count : -4][:3], refs[pieces + acts_count : -4][3]
    held, factors, total, sems = refs[-4:]
    step = pl.program_id(0)
    hidden_units = outs[0].shape[0]

    starts = [sum(count for _, count in ranges[:p]) for p in range(pieces + 1)]

    def copies(count):
        return [
            pltpu.make_async_copy(
                sources[p].at[pl.ds(ranges[p][0], ranges[p][1]), pl.ds(0, 2 * width)],
                held.at[pl.ds(starts[p], ranges[p][1]), :],
                sems.at[p],
            )
            for p in count
        ]

    @pl.when(step == 0)
    def _():
        for copy in copies(range(cold_pieces)):
            copy.start()

        @pl.when(hot[0] == 1)
        def _():
            for copy in copies(range(cold_pieces, pieces)):
                copy.start()

        at = 0
        for act in acts:
            factors[:, at : at + act.shape[0]] = act[...].astype(F32).T.astype(BF16)
            at += act.shape[0]
        total[...] = jnp.zeros_like(total)
        for copy in copies(range(cold_pieces)):
            copy.wait()

        @pl.when(hot[0] == 1)
        def _():
            for copy in copies(range(cold_pieces, pieces)):
                copy.wait()

    def work(rows):
        for i in range(3):
            at = pl.multiple_of((width if i == 2 else 0) + step * tile, tile)
            gradient = jnp.dot(
                factors[i * hidden_units : (i + 1) * hidden_units, :rows],
                held[:rows, pl.ds(at, tile)],
                preferred_element_type=F32,
            )
            outs[i][...] = gradient
            total[...] += jnp.sum((gradient * gradient).reshape(-1, 8, tile), axis=0)

    @pl.when(hot[0] == 1)
    def _():
        work(starts[pieces])

    @pl.when(hot[0] != 1)
    def _():
        work(starts[cold_pieces])

    @pl.when(step == pl.num_programs(0) - 1)
    def _():
        squares[...] = jnp.full(squares.shape, jnp.sum(total[...]), F32)


def weights_backward(earlier, hot, cold, extra, acts, hidden_units, width):
    tile = 512
    sources = [source for source, _, _ in cold + extra]
    ranges = [(first, count) for _, first, count in cold + extra]
    rows = sum(count for _, count in ranges)
    block = pl.BlockSpec((hidden_units, tile), lambda j: (0, j))
    whole = [pl.BlockSpec(a.shape, lambda j: (0, 0)) for a in acts]
    return call(
        functools.partial(
            weights_body, ranges, len(cold), len(acts), width, tile
        ),
        "weights_backward",
        [jax.ShapeDtypeStruct((hidden_units, width), F32)] * 3
        + [jax.ShapeDtypeStruct((8, LANES), F32)],
        [SMEM] + [ANY] * len(sources) + whole,
        [block] * 3 + [pl.BlockSpec((8, LANES), lambda j: (0, 0))],
        [
            pltpu.VMEM((rows, 2 * width), BF16),
            pltpu.VMEM((3 * hidden_units, rows), BF16),
            pltpu.VMEM((8, tile), F32),
            pltpu.SemaphoreType.DMA((len(sources),)),
        ],
        0.001,
        24,
        earlier,
        grid=(width // tile,),
    )(hot, *sources, *acts)


def home_body(experts, cap, cut, row_total, firsts, logits, ids, *refs):
    arrived, back = refs[:experts], refs[experts : 2 * experts]
    grad_rows, grad_logits, norm, pads, table, sems = refs[2 * experts :]
    copies = [
        pltpu.make_async_copy(
            arrived[m].at[pl.ds(firsts[m], 16), pl.ds(arrived[m].shape[1] - LANES, LANES)],
            pads.at[pl.ds(16 * m, 16), :],
            sems.at[m],
        )
        for m in range(experts)
    ]
    for copy in copies:
        copy.start()
    onehot, spread = routing(ids[...], lax.axis_index("expert"), cap, experts)
    slots = (experts + 1) * cap
    for m in range(experts):
        table[m * cap : (m + 1) * cap, :] = back[m][:cap, :]
    over = back[0][cap:, :]
    for m in range(2, experts, 2):
        over = over + back[m][cap:, :]
    table[experts * cap :, :] = over
    lane = lane_iota((8, LANES))
    square = tree([back[m][0:16, cut:].astype(F32)[0:8] for m in range(experts)])
    square = jnp.where((lane >= SQUARE_LANE) & (lane < SQUARE_LANE + 3), square, 0.0)
    norm[0] = jnp.max(jnp.sqrt(jnp.sum(square, axis=1, keepdims=True)))
    pick = spread.T[:, :slots].astype(BF16)
    grad_rows[...] = jnp.dot(pick, table[:, :cut], preferred_element_type=F32).astype(BF16)
    gate_rows = jnp.dot(pick, table[:, cut:], preferred_element_type=F32).T[0:1]
    for copy in copies:
        copy.wait()
    counts = jnp.zeros((1, LANES), F32)
    for m in range(experts):
        counts = counts + pads[16 * m : 16 * m + 16, :].astype(F32)[0:1]
    counts = jnp.broadcast_to(counts, (8, LANES)).T[COUNT_LANE : COUNT_LANE + experts, 0:1]
    probs = softmax(logits[...])
    pulls = onehot * gate_rows + aux_weight * experts * (counts / row_total)
    grad_logits[...] = probs * (pulls - jnp.sum(probs * pulls, axis=0, keepdims=True))


def home(logits, ids, arrived, back, cap, row_total):
    experts = len(back)
    rows = ids.shape[1]
    cut = back[0].shape[1] - LANES
    return call(
        functools.partial(
            home_body, experts, cap, cut, row_total, [first for _, first, _ in arrived]
        ),
        "home",
        [
            jax.ShapeDtypeStruct((rows, cut), BF16),
            jax.ShapeDtypeStruct(logits.shape, F32),
            jax.ShapeDtypeStruct((1,), F32),
        ],
        [VMEM, VMEM] + [ANY] * experts + [VMEM] * experts,
        [VMEM, VMEM, SMEM],
        [
            pltpu.VMEM((16 * experts, LANES), BF16),
            pltpu.VMEM(((experts + 1) * cap, cut + LANES), BF16),
            pltpu.SemaphoreType.DMA((experts,)),
        ],
        0.001,
        12,
    )(logits, ids, *[piece for piece, _, _ in arrived], *back)


def swap(value, axis, mask):
    size = lax.axis_size(axis)
    return lax.ppermute(value, axis, [(i, i ^ mask) for i in range(size)])


def after(values, done):
    tied = lax.optimization_barrier((*values, *done))
    return tied[: len(values)], tied[len(values) :]


def local(rows_x, rows_dy, router_logits, expert_of, w_gate, w_up, w_down):
    experts = lax.axis_size("expert")
    n_dp = lax.axis_size("dp")
    rows, width = rows_x.shape
    cap = rows // 8
    cut = width // n_dp
    weights = (w_gate[0], w_up[0], w_down[0])
    hidden_units = weights[0].shape[0]
    logits, ids = router_logits.T, expert_of.reshape(1, rows)
    evens = list(range(0, experts, 2))
    near = [m for m in evens[1:] if m & (m - 1) == 0]
    far = [m for m in evens[1:] if m & (m - 1)]
    path = {m: [b for b in near if m & b] for m in far}
    path.update({m ^ 1: [b for b in near[::-1] if m & b] for m in far})
    first_hop = {b: [m for m in path if path[m][0] == b] for b in near}
    plan = [[0], [1, experts, *range(3, experts, 2)], [experts]]
    plan += [[b] + [m for m in first_hop[b] if m % 2 == 0] for b in near]
    own, beside, spare, *mine, hot = dispatch(
        rows_x, rows_dy, logits, ids, experts, cap, plan
    )
    bits = [1 << i for i in range(n_dp.bit_length() - 1)]
    token = []

    def step(kernel, *given):
        result = kernel(tuple(token), *given)
        token[:] = [result[-1]]
        return result

    def wait_for(*arrived):
        token.extend(arrived)

    def backward(parts, kind=False, micros=0.001):
        return step(rows_backward, hot, parts, weights, n_dp, kind, micros)

    def turn(pair, bit):
        *kept, sent = pair
        return *kept, swap(sent, "dp", bit)

    def middle(pair):
        for bit in bits[1:]:
            pair = turn(step(fold, pair, cut), bit)
        return pair

    beside = swap(beside, "expert", 1)

    def from_beside(m):
        at = plan[1].index(m) * cap
        return beside[at : at + cap]

    cold = {0: (own, 0, cap), 1: (beside, 0, cap)}
    chunks = [[0, 1], [m ^ c for c in (0, 1) for m in near], [m ^ c for c in (0, 1) for m in far]]
    over = {m: swap(spare, "expert", m) for m in near}
    *first, acts_first = backward([cold[m] for m in chunks[0]])
    (later,), (acts_first,) = after([spare], [acts_first])
    over.update({m: swap(later, "expert", m) for m in far})
    over = [over[m] for m in evens[1:]]
    kept, sent = step(fold, turn(first, bits[0]), cut)
    packed, (sent,) = after(over, [sent])
    crossed = swap(jnp.concatenate(packed, axis=0), "expert", 1)
    first = turn((kept, sent), bits[1])
    for bit in bits[2:]:
        first = turn(step(fold, first, cut), bit)
    loads = []
    for b, part in zip(near, mine):
        odd = [b ^ 1] + [m for m in first_hop[b] if m % 2]
        loads.append(jnp.concatenate([part] + [from_beside(m) for m in odd], axis=0))
    loads, over = after(loads, over)
    extras = [(part, 0, cap) for part in [spare, *over]]
    extras += [(beside, cap, cap), (crossed, 0, crossed.shape[0])]
    loads = [swap(load, "expert", b) for b, load in zip(near, loads)]

    kept, sent, far_kept, far_sent, acts_hot = backward(extras, True)
    far_sent = swap(far_sent, "expert", 1)
    far_kept = swap(far_kept, "expert", 1)
    (sent,) = step(merge, sent, far_sent)
    wait_for(first[-1])
    busy = turn((kept, far_kept, sent), bits[0])
    busy = middle(busy)
    passed = {}
    for b, load in zip(near, loads):
        items = [b] + [m for m in first_hop[b] if m % 2 == 0]
        items += [b ^ 1] + [m for m in first_hop[b] if m % 2]
        for i, m in enumerate(items):
            if m in path:
                passed[m] = load[i * cap : (i + 1) * cap]
            else:
                cold[m] = (load, i * cap, cap)
    on_way = list(passed)
    parts, (met,) = after([passed[m] for m in on_way], [busy[-1]])
    busy = (*busy[:-1], met)
    for m, part in zip(on_way, parts):
        for b in path[m][1:]:
            part = swap(part, "expert", b)
        cold[m] = (part, 0, cap)
    *second, acts_second = backward([cold[m] for m in chunks[1]])
    second = turn(second, bits[0])
    *third, acts_third = backward([cold[m] for m in chunks[2]])
    third = turn(third, bits[0])
    second = middle(second)
    grad_gate, grad_up, grad_down, squares = step(
        weights_backward,
        hot,
        [cold[m] for m in sum(chunks, [])],
        extras,
        [acts_first, acts_second, acts_third, acts_hot],
        hidden_units,
        width,
    )
    for bit in bits[1:]:
        kept, sent = step(fold, third, cut)
        (squares,), (sent,) = after([squares], [sent])
        third = turn((kept, sent), bit)
    squares = [squares] + [swap(squares, "dp", m) for m in range(1, n_dp)]
    back = {}
    for masks, pairs, where in (
        (chunks[0] + chunks[1], [first, second, busy], [*chunks[:2], evens]),
        (chunks[2], [third, busy], [chunks[2], evens]),
    ):
        for m, piece in zip(masks, step(last, squares, pairs, where, masks, cut, cap)):
            back[m] = piece if m == 0 else swap(piece, "expert", m)
    grad_rows, grad_logits, norm = home(
        logits,
        ids,
        [cold[m] for m in range(experts)],
        [back[m] for m in range(experts)],
        cap,
        rows * experts,
    )
    return (
        grad_rows,
        grad_logits.T,
        grad_gate[None],
        grad_up[None],
        grad_down[None],
        norm.reshape(()),
    )


def solution(mesh):
    in_specs = (
        P("expert", None),
        P("expert", None),
        P("expert", None),
        P("expert", None),
        P("expert", "dp", None),
        P("expert", "dp", None),
        P("expert", "dp", None),
    )
    out_specs = (
        P("expert", "dp"),
        P("expert", None),
        P("expert", "dp", None),
        P("expert", "dp", None),
        P("expert", "dp", None),
        P(),
    )
    return jax.shard_map(local, mesh=mesh, in_specs=in_specs, out_specs=out_specs, check_vma=False)
```

time: 167 us -> 146 us (0.87)
  waiting for transfers between devices: 69 us -> 55.1 us
  Pallas kernels: 44.8 us -> 36.3 us
  starting transfers between devices: 41.1 us -> 47.4 us
  local copies, waits for them, and re-layouts: 9.02 us -> 6.18 us
    ppermute x41 -> x29, waiting for transfers between devices: 69 us -> 55.1 us  [swap(): return lax.ppermute(value, axis, [(i, i ^ mask) for i in range(size)])]
    pallas_call x16 -> x14, Pallas kernels: 44.8 us -> 36.3 us  [the longest x4 17.5 us: rows_backward(): call(functools.partial(rows_body, ranges, width, n_dp, guarded), 'rows_ba...]
    ppermute x41 -> x29, starting transfers between devices: 41.1 us -> 47.4 us  [swap(): return lax.ppermute(value, axis, [(i, i ^ mask) for i in range(size)])]
    unnamed x20 -> x24, local copies, waits for them, and re-layouts: 8.51 us -> 6 us
  transfers between devices with their start and end apart: 41 -> 29, of which waited for: 20 -> 15; matrix products, arithmetic and copies ran while one was open for 0% -> 0% of each run, Pallas kernels for 23% -> 20%
where the time goes in v1:
time: 146 us
  waiting for transfers between devices  55.1 us (38%)
  starting transfers between devices  47.4 us (32%)
  Pallas kernels  36.3 us (25%)
  local copies, waits for them, and re-layouts  6.18 us (4%)
    ppermute x29, waiting for transfers between devices, swap(): return lax.ppermute(value, axis, [(i, i ^ mask) for i in range(size)])  55.1 us
    ppermute x29, starting transfers between devices, swap(): return lax.ppermute(value, axis, [(i, i ^ mask) for i in range(size)])  47.4 us
    pallas_call x4, Pallas kernels, rows_backward(): call(functools.partial(rows_body, ranges, width, n_dp, guarded), 'rows_ba...  17.5 us
    pallas_call x1, Pallas kernels, weights_backward(): call(functools.partial(weights_body, ranges, len(cold), len(acts), width,...  10.2 us
    unnamed x24, local copies, waits for them, and re-layouts  6 us
    pallas_call x1, Pallas kernels, dispatch(): call(functools.partial(dispatch_body, plan, experts, cap, width), 'dispat...  5.7 us
  transfers between devices with their start and end apart: 29, of which 15 were waited for; matrix products, arithmetic and copies ran while one was open for 0% of the time, Pallas kernels for 20%

profile of v1, /device:TPU:0, one launch (start us, length us, event | category | flops | bytes accessed | tf_op | source)
XLA Modules:
  0.0 146.4 jit_solution(10259213776160309042)
XLA Ops:
  0.6 5.7 %dispatch.1 = (bf16[32,8320]{1,0:T(8,128)(2,1)}, bf16[160,8320]{1,0:T(8,128)(2,1)}, bf16[32,8320]{1,0:T(8,128)(2,1)}, bf16[64,8320]{1,0:T(8,128)(2,1)}, bf16[32,8320]{1,0:T(8,128)(2,1)}, /*index=5*/s32[1]{0:T(128)}) custom-call(bf16[256,4096]{1,0:T(8,128)(2,1)} %refs_0_.1, bf16[256,4096]{1,0:T(8,128)(2,1)} %refs_1_.1, f32[8,256]{1,0:T(8,128)} %bitcast.22, ...), custom_call_target="tpu_custom_call" | custom-call | flops 6000000000 | bytes 1000 | tf_op jit(solution)/shard_map/dispatch/pallas_call | solution.py:120
  6.9 2.6 %collective-permute-start.1 = (bf16[32,8320]{1,0:T(8,128)(2,1)}, bf16[32,8320]{1,0:T(8,128)(2,1)S(1)}, u32[]{:S(2)}, u32[]{:S(2)}) collective-permute-start(bf16[32,8320]{1,0:T(8,128)(2,1)} %get-tuple-element.72.refs_2_.refs_10_), channel_id=1, source_target_pairs={{0,8},{4,12},{8,0},{12,4},{16,24},{20,28},{24,16},{28,20},{1,9},{5... | collective-permute-start | bytes 1597448 | tf_op jit(solution)/shard_map/ppermute | solution.py:515
  11.7 1.9 %copy-done.1 = bf16[1,384,4096]{2,1,0:T(8,128)(2,1)S(1)} copy-done((bf16[1,384,4096]{2,1,0:T(8,128)(2,1)S(1)}, bf16[1,384,4096]{2,1,0:T(8,128)(2,1)}, u32[]{:S(2)}) %copy-start.1) | copy-done | bytes 3145752
  13.6 1.9 %copy-done.3 = bf16[1,384,4096]{2,1,0:T(8,128)(2,1)S(1)} copy-done((bf16[1,384,4096]{2,1,0:T(8,128)(2,1)S(1)}, bf16[1,384,4096]{2,1,0:T(8,128)(2,1)}, u32[]{:S(2)}) %copy-start.3) | copy-done | bytes 3145752
  16.5 5.5 %rows_backward.4 = (bf16[64,2176]{1,0:T(8,128)(2,1)S(1)}, bf16[64,2176]{1,0:T(8,128)(2,1)S(1)}, bf16[64,1152]{1,0:T(8,128)(2,1)S(1)}) custom-call(s32[1]{0:T(128)} %get-tuple-element.70.refs_0_.refs_1_, bf16[32,8320]{1,0:T(8,128)(2,1)S(1)} %copy-done.5, bf16[160,8320]{1,0:T(8,128)(2,1)S(1)} %collective-permute-done.refs_2_.refs_6_.refs_3_.refs_14_, ...), custom_call_target="tpu_custom_call" | custom-call | flops 1000000 | bytes 1000 | tf_op jit(solution)/shard_map/rows_backward/pallas_call | solution.py:241
  22.0 3.9 %collective-permute-start.3 = (bf16[32,8320]{1,0:T(8,128)(2,1)S(1)}, bf16[32,8320]{1,0:T(8,128)(2,1)S(1)}, u32[]{:S(2)}, u32[]{:S(2)}) collective-permute-start(bf16[32,8320]{1,0:T(8,128)(2,1)S(1)} %copy-done.7), channel_id=1, source_target_pairs={{0,24},{4,28},{8,16},{12,20},{16,8},{20,12},{24,0},{28,4},{1,25},{... | collective-permute-start | bytes 1597448 | tf_op jit(solution)/shard_map/ppermute | solution.py:515
  25.9 1.6 %collective-permute-start.6 = (bf16[64,2176]{1,0:T(8,128)(2,1)S(1)}, bf16[64,2176]{1,0:T(8,128)(2,1)S(1)}, u32[]{:S(2)}, u32[]{:S(2)}) collective-permute-start(bf16[64,2176]{1,0:T(8,128)(2,1)S(1)} %get-tuple-element.76), channel_id=1, source_target_pairs={{0,1},{1,0},{2,3},{3,2},{4,5},{5,4},{6,7},{7,6},{8,9},{9,8},{10,11... | collective-permute-start | bytes 835592 | tf_op jit(solution)/shard_map/ppermute | solution.py:515
  27.5 6.8 %collective-permute-done.6.refs_2_ = bf16[64,2176]{1,0:T(8,128)(2,1)S(1)} collective-permute-done((bf16[64,2176]{1,0:T(8,128)(2,1)S(1)}, bf16[64,2176]{1,0:T(8,128)(2,1)S(1)}, u32[]{:S(2)}, u32[]{:S(2)}) %collective-permute-start.6) | collective-permute-done | bytes 278560 | tf_op jit(solution)/shard_map/ppermute | solution.py:515
  34.4 3.9 %collective-permute-done.3.refs_5_.refs_13_ = bf16[32,8320]{1,0:T(8,128)(2,1)S(1)} collective-permute-done((bf16[32,8320]{1,0:T(8,128)(2,1)S(1)}, bf16[32,8320]{1,0:T(8,128)(2,1)S(1)}, u32[]{:S(2)}, u32[]{:S(2)}) %collective-permute-start.3) | collective-permute-done | bytes 532512 | tf_op jit(solution)/shard_map/ppermute | solution.py:515
  40.0 1.7 %collective-permute-start.4 = (bf16[96,8320]{1,0:T(8,128)(2,1)S(1)}, bf16[96,8320]{1,0:T(8,128)(2,1)S(1)}, u32[]{:S(2)}, u32[]{:S(2)}) collective-permute-start(bf16[96,8320]{1,0:T(8,128)(2,1)S(1)} %get-tuple-element.73), channel_id=1, source_target_pairs={{0,8},{4,12},{8,0},{12,4},{16,24},{20,28},{24,16},{28,20},{1,9},{5... | collective-permute-start | bytes 4792328 | tf_op jit(solution)/shard_map/ppermute | solution.py:515
  46.5 1.6 %collective-permute-start.11 = (bf16[128,2176]{1,0:T(8,128)(2,1)S(1)}, bf16[128,2176]{1,0:T(8,128)(2,1)S(1)}, u32[]{:S(2)}, u32[]{:S(2)}) collective-permute-start(bf16[128,2176]{1,0:T(8,128)(2,1)S(1)} %merge.1.refs_0_), channel_id=1, source_target_pairs={{0,1},{1,0},{2,3},{3,2},{4,5},{5,4},{6,7},{7,6},{8,9},{9,8},{10,11... | collective-permute-start | bytes 1671176 | tf_op jit(solution)/shard_map/ppermute | solution.py:515
  48.1 2.6 %collective-permute-start.9 = (bf16[64,1152]{1,0:T(8,128)(2,1)S(1)}, bf16[64,1152]{1,0:T(8,128)(2,1)S(1)}, u32[]{:S(2)}, u32[]{:S(2)}) collective-permute-start(bf16[64,1152]{1,0:T(8,128)(2,1)S(1)} %get-tuple-element.87.refs_0_), channel_id=1, source_target_pairs={{0,2},{1,3},{2,0},{3,1},{4,6},{5,7},{6,4},{7,5},{8,10},{9,11},{10,... | collective-permute-start | bytes 442376 | tf_op jit(solution)/shard_map/ppermute | solution.py:515
  50.7 12.8 %collective-permute-done.9.refs_1_.refs_6_ = bf16[64,1152]{1,0:T(8,128)(2,1)S(1)} collective-permute-done((bf16[64,1152]{1,0:T(8,128)(2,1)S(1)}, bf16[64,1152]{1,0:T(8,128)(2,1)S(1)}, u32[]{:S(2)}, u32[]{:S(2)}) %collective-permute-start.9) | collective-permute-done | bytes 147488 | tf_op jit(solution)/shard_map/ppermute | solution.py:515
  64.8 2.5 %collective-permute-start.12 = (bf16[128,1152]{1,0:T(8,128)(2,1)S(1)}, bf16[128,1152]{1,0:T(8,128)(2,1)S(1)}, u32[]{:S(2)}, u32[]{:S(2)}) collective-permute-start(bf16[128,1152]{1,0:T(8,128)(2,1)S(1)} %get-tuple-element.90.refs_0_), channel_id=1, source_target_pairs={{0,2},{1,3},{2,0},{3,1},{4,6},{5,7},{6,4},{7,5},{8,10},{9,11},{10,... | collective-permute-start | bytes 884744 | tf_op jit(solution)/shard_map/ppermute | solution.py:515
  67.4 9.2 %collective-permute-done.4.refs_2_.refs_4_.refs_6_.refs_5_ = bf16[96,8320]{1,0:T(8,128)(2,1)S(1)} collective-permute-done((bf16[96,8320]{1,0:T(8,128)(2,1)S(1)}, bf16[96,8320]{1,0:T(8,128)(2,1)S(1)}, u32[]{:S(2)}, u32[]{:S(2)}) %collective-permute-start.4) | collective-permute-done | bytes 1597472 | tf_op jit(solution)/shard_map/ppermute | solution.py:515
  77.8 2.5 %collective-permute-done.12.refs_10_.refs_8_ = bf16[128,1152]{1,0:T(8,128)(2,1)S(1)} collective-permute-done((bf16[128,1152]{1,0:T(8,128)(2,1)S(1)}, bf16[128,1152]{1,0:T(8,128)(2,1)S(1)}, u32[]{:S(2)}, u32[]{:S(2)}) %collective-permute-start.12) | collective-permute-done | bytes 294944 | tf_op jit(solution)/shard_map/ppermute | solution.py:515
  81.3 7.5 %collective-permute-start.14 = (bf16[32,8320]{1,0:T(8,128)(2,1)S(1)}, bf16[32,8320]{1,0:T(8,128)(2,1)S(1)}, u32[]{:S(2)}, u32[]{:S(2)}) collective-permute-start(bf16[32,8320]{1,0:T(8,128)(2,1)S(1)} %slice.21), channel_id=1, source_target_pairs={{0,8},{4,12},{8,0},{12,4},{16,24},{20,28},{24,16},{28,20},{1,9},{5... | collective-permute-start | bytes 1597448 | tf_op jit(solution)/shard_map/ppermute | solution.py:515
  88.8 5.5 %rows_backward.6 = (bf16[128,2176]{1,0:T(8,128)(2,1)S(1)}, bf16[128,2176]{1,0:T(8,128)(2,1)S(1)}, bf16[128,1152]{1,0:T(8,128)(2,1)S(1)}) custom-call(bf16[128,1152]{1,0:T(8,128)(2,1)S(1)} %get-tuple-element.90.refs_0_, s32[1]{0:T(128)} %get-tuple-element.70.refs_0_.refs_1_, bf16[96,8320]{1,0:T(8,128)(2,1)S(1)} %collective-permute-done.4.refs_2_.refs_4_.refs_6_.refs_5_, ...), custom_call_target="tpu_custom_call" | custom-call | flops 1000000 | bytes 1000 | tf_op jit(solution)/shard_map/rows_backward/pallas_call | solution.py:241
  94.9 4.2 %collective-permute-done.14.refs_3_.refs_9_ = bf16[32,8320]{1,0:T(8,128)(2,1)S(1)} collective-permute-done((bf16[32,8320]{1,0:T(8,128)(2,1)S(1)}, bf16[32,8320]{1,0:T(8,128)(2,1)S(1)}, u32[]{:S(2)}, u32[]{:S(2)}) %collective-permute-start.14) | collective-permute-done | bytes 532512 | tf_op jit(solution)/shard_map/ppermute | solution.py:515
  99.2 5.5 %rows_backward.7 = (bf16[64,2176]{1,0:T(8,128)(2,1)S(1)}, bf16[64,2176]{1,0:T(8,128)(2,1)S(1)}, bf16[64,1152]{1,0:T(8,128)(2,1)S(1)}) custom-call(bf16[128,1152]{1,0:T(8,128)(2,1)S(1)} %get-tuple-element.93.refs_0_.refs_17_, s32[1]{0:T(128)} %get-tuple-element.70.refs_0_.refs_1_, bf16[32,8320]{1,0:T(8,128)(2,1)S(1)} %collective-permute-done.13.refs_2_.refs_8_, ...), custom_call_target="tpu_custom_call" | custom-call | flops 1000000 | bytes 1000 | tf_op jit(solution)/shard_map/rows_backward/pallas_call | solution.py:241
  104.6 2.3 %collective-permute-start.16 = (bf16[64,2176]{1,0:T(8,128)(2,1)S(1)}, bf16[64,2176]{1,0:T(8,128)(2,1)S(1)}, u32[]{:S(2)}, u32[]{:S(2)}) collective-permute-start(bf16[64,2176]{1,0:T(8,128)(2,1)S(1)} %get-tuple-element.101), channel_id=1, source_target_pairs={{0,1},{1,0},{2,3},{3,2},{4,5},{5,4},{6,7},{7,6},{8,9},{9,8},{10,11... | collective-permute-start | bytes 835592 | tf_op jit(solution)/shard_map/ppermute | solution.py:515
  107.6 3.4 %collective-permute-start.20 = (bf16[128,1152]{1,0:T(8,128)(2,1)S(1)}, bf16[128,1152]{1,0:T(8,128)(2,1)S(1)}, u32[]{:S(2)}, u32[]{:S(2)}) collective-permute-start(bf16[128,1152]{1,0:T(8,128)(2,1)S(1)} %get-tuple-element.97.refs_0_), channel_id=1, source_target_pairs={{0,2},{1,3},{2,0},{3,1},{4,6},{5,7},{6,4},{7,5},{8,10},{9,11},{10,... | collective-permute-start | bytes 884744 | tf_op jit(solution)/shard_map/ppermute | solution.py:515
  111.0 10.2 %weights_backward.1 = (f32[384,4096]{1,0:T(8,128)}, f32[384,4096]{1,0:T(8,128)}, f32[384,4096]{1,0:T(8,128)}, f32[8,128]{1,0:T(8,128)S(1)}) custom-call(bf16[128,1152]{1,0:T(8,128)(2,1)S(1)} %get-tuple-element.97.refs_0_, s32[1]{0:T(128)} %get-tuple-element.70.refs_0_.refs_1_, bf16[32,8320]{1,0:T(8,128)(2,1)S(1)} %copy-done.6, ...), custom_call_target="tpu_custom_call" | custom-call | flops 1000000 | bytes 1000 | tf_op jit(solution)/shard_map/weights_backward/pallas_call | solution.py:426
  121.5 1.8 %collective-permute-start.17 = (f32[8,128]{1,0:T(8,128)S(1)}, f32[8,128]{1,0:T(8,128)S(1)}, u32[]{:S(2)}, u32[]{:S(2)}) collective-permute-start(f32[8,128]{1,0:T(8,128)S(1)} %get-tuple-element.103.refs_0_.refs_1_), channel_id=1, source_target_pairs={{0,1},{1,0},{2,3},{3,2},{4,5},{5,4},{6,7},{7,6},{8,9},{9,8},{10,11... | collective-permute-start | bytes 12296 | tf_op jit(solution)/shard_map/ppermute | solution.py:515
  123.3 2.8 %collective-permute-start.18 = (f32[8,128]{1,0:T(8,128)S(1)}, f32[8,128]{1,0:T(8,128)S(1)}, u32[]{:S(2)}, u32[]{:S(2)}) collective-permute-start(f32[8,128]{1,0:T(8,128)S(1)} %get-tuple-element.103.refs_0_.refs_1_), channel_id=1, source_target_pairs={{0,2},{1,3},{2,0},{3,1},{4,6},{5,7},{6,4},{7,5},{8,10},{9,11},{10,... | collective-permute-start | bytes 12296 | tf_op jit(solution)/shard_map/ppermute | solution.py:515
  126.2 3.8 %collective-permute-done.18.refs_3_ = f32[8,128]{1,0:T(8,128)S(1)} collective-permute-done((f32[8,128]{1,0:T(8,128)S(1)}, f32[8,128]{1,0:T(8,128)S(1)}, u32[]{:S(2)}, u32[]{:S(2)}) %collective-permute-start.18) | collective-permute-done | bytes 4128 | tf_op jit(solution)/shard_map/ppermute | solution.py:515
  130.0 1.6 %collective-permute-done.19.refs_4_ = f32[8,128]{1,0:T(8,128)S(1)} collective-permute-done((f32[8,128]{1,0:T(8,128)S(1)}, f32[8,128]{1,0:T(8,128)S(1)}, u32[]{:S(2)}, u32[]{:S(2)}) %collective-permute-start.19) | collective-permute-done | bytes 4128 | tf_op jit(solution)/shard_map/ppermute | solution.py:515
  131.9 1.9 %collective-permute-start.24 = (bf16[64,1152]{1,0:T(8,128)(2,1)S(1)}, bf16[64,1152]{1,0:T(8,128)(2,1)S(1)}, u32[]{:S(2)}, u32[]{:S(2)}) collective-permute-start(bf16[64,1152]{1,0:T(8,128)(2,1)S(1)} %get-tuple-element.112), channel_id=1, source_target_pairs={{0,16},{4,20},{8,24},{12,28},{16,0},{20,4},{24,8},{28,12},{1,17},{... | collective-permute-start | bytes 442376 | tf_op jit(solution)/shard_map/ppermute | solution.py:515
  134.2 1.5 %collective-permute-start.27 = (bf16[64,1152]{1,0:T(8,128)(2,1)S(1)}, bf16[64,1152]{1,0:T(8,128)(2,1)S(1)}, u32[]{:S(2)}, u32[]{:S(2)}) collective-permute-start(bf16[64,1152]{1,0:T(8,128)(2,1)S(1)} %get-tuple-element.116), channel_id=1, source_target_pairs={{0,24},{4,28},{8,16},{12,20},{16,8},{20,12},{24,0},{28,4},{1,25},{... | collective-permute-start | bytes 442376 | tf_op jit(solution)/shard_map/ppermute | solution.py:515
  138.1 2.0 %collective-permute-start.28 = (bf16[32,1152]{1,0:T(8,128)(2,1)S(1)}, bf16[32,1152]{1,0:T(8,128)(2,1)S(1)}, u32[]{:S(2)}, u32[]{:S(2)}) collective-permute-start(bf16[32,1152]{1,0:T(8,128)(2,1)S(1)} %get-tuple-element.117), channel_id=1, source_target_pairs={{0,28},{4,24},{8,20},{12,16},{16,12},{20,8},{24,4},{28,0},{1,29},{... | collective-permute-start | bytes 221192 | tf_op jit(solution)/shard_map/ppermute | solution.py:515
  140.1 4.5 %collective-permute-done.25.refs_15_ = bf16[32,1152]{1,0:T(8,128)(2,1)S(1)} collective-permute-done((bf16[32,1152]{1,0:T(8,128)(2,1)S(1)}, bf16[32,1152]{1,0:T(8,128)(2,1)S(1)}, u32[]{:S(2)}, u32[]{:S(2)}) %collective-permute-start.25) | collective-permute-done | bytes 73760 | tf_op jit(solution)/shard_map/ppermute | solution.py:515
  144.6 1.7 %home.1 = (bf16[256,1024]{1,0:T(8,128)(2,1)}, f32[8,256]{1,0:T(8,128)}, f32[1]{0:T(128)}) custom-call(f32[8,256]{1,0:T(8,128)S(1)} %bitcast.23, s32[1,256]{1,0:T(1,128)S(1)} %bitcast.25, bf16[32,8320]{1,0:T(8,128)(2,1)S(1)} %copy-done.6, bf16[160,8320]{1,0:T(8,128)(2,1)S(1)} %collective-permute-done.refs_2_.refs_6_.refs_3_.refs_14_, ...), custom_call_target="tpu_custom_call" | custom-call | flops 1000000 | bytes 1000 | tf_op jit(solution)/shard_map/home/pallas_call | solution.py:491
  (70 shorter events, 18.5 us)
Async XLA Ops:
  6.3 5.3 %collective-permute-start = (bf16[160,8320]{1,0:T(8,128)(2,1)}, bf16[160,8320]{1,0:T(8,128)(2,1)S(1)}, u32[]{:S(2)}, u32[]{:S(2)}) collective-permute-start(bf16[160,8320]{1,0:T(8,128)(2,1)} %get-tuple-element.66), channel_id=1, source_target_pairs={{0,4},{4,0},{8,12},{12,8},{16,20},{20,16},{24,28},{28,24},{1,5},{5... | collective-permute-start | bytes 7987208 | tf_op jit(solution)/shard_map/ppermute | solution.py:515
  6.9 27.5 %collective-permute-start.1 = (bf16[32,8320]{1,0:T(8,128)(2,1)}, bf16[32,8320]{1,0:T(8,128)(2,1)S(1)}, u32[]{:S(2)}, u32[]{:S(2)}) collective-permute-start(bf16[32,8320]{1,0:T(8,128)(2,1)} %get-tuple-element.72.refs_2_.refs_10_), channel_id=1, source_target_pairs={{0,8},{4,12},{8,0},{12,4},{16,24},{20,28},{24,16},{28,20},{1,9},{5... | collective-permute-start | bytes 1597448 | tf_op jit(solution)/shard_map/ppermute | solution.py:515
  9.4 25.0 %collective-permute-start.2 = (bf16[32,8320]{1,0:T(8,128)(2,1)}, bf16[32,8320]{1,0:T(8,128)(2,1)S(1)}, u32[]{:S(2)}, u32[]{:S(2)}) collective-permute-start(bf16[32,8320]{1,0:T(8,128)(2,1)} %get-tuple-element.72.refs_2_.refs_10_), channel_id=1, source_target_pairs={{0,16},{4,20},{8,24},{12,28},{16,0},{20,4},{24,8},{28,12},{1,17},{... | collective-permute-start | bytes 1597448 | tf_op jit(solution)/shard_map/ppermute | solution.py:515
  22.0 16.3 %collective-permute-start.3 = (bf16[32,8320]{1,0:T(8,128)(2,1)S(1)}, bf16[32,8320]{1,0:T(8,128)(2,1)S(1)}, u32[]{:S(2)}, u32[]{:S(2)}) collective-permute-start(bf16[32,8320]{1,0:T(8,128)(2,1)S(1)} %copy-done.7), channel_id=1, source_target_pairs={{0,24},{4,28},{8,16},{12,20},{16,8},{20,12},{24,0},{28,4},{1,25},{... | collective-permute-start | bytes 1597448 | tf_op jit(solution)/shard_map/ppermute | solution.py:515
  25.9 8.4 %collective-permute-start.6 = (bf16[64,2176]{1,0:T(8,128)(2,1)S(1)}, bf16[64,2176]{1,0:T(8,128)(2,1)S(1)}, u32[]{:S(2)}, u32[]{:S(2)}) collective-permute-start(bf16[64,2176]{1,0:T(8,128)(2,1)S(1)} %get-tuple-element.76), channel_id=1, source_target_pairs={{0,1},{1,0},{2,3},{3,2},{4,5},{5,4},{6,7},{7,6},{8,9},{9,8},{10,11... | collective-permute-start | bytes 835592 | tf_op jit(solution)/shard_map/ppermute | solution.py:515
  38.4 4.9 %collective-permute-start.7 = (bf16[96,8320]{1,0:T(8,128)(2,1)S(1)}, bf16[96,8320]{1,0:T(8,128)(2,1)S(1)}, u32[]{:S(2)}, u32[]{:S(2)}) collective-permute-start(bf16[96,8320]{1,0:T(8,128)(2,1)S(1)} %pad_maximum_fusion.2), channel_id=1, source_target_pairs={{0,4},{4,0},{8,12},{12,8},{16,20},{20,16},{24,28},{28,24},{1,5},{5... | collective-permute-start | bytes 4792328 | tf_op jit(solution)/shard_map/ppermute | solution.py:515
  40.0 36.5 %collective-permute-start.4 = (bf16[96,8320]{1,0:T(8,128)(2,1)S(1)}, bf16[96,8320]{1,0:T(8,128)(2,1)S(1)}, u32[]{:S(2)}, u32[]{:S(2)}) collective-permute-start(bf16[96,8320]{1,0:T(8,128)(2,1)S(1)} %get-tuple-element.73), channel_id=1, source_target_pairs={{0,8},{4,12},{8,0},{12,4},{16,24},{20,28},{24,16},{28,20},{1,9},{5... | collective-permute-start | bytes 4792328 | tf_op jit(solution)/shard_map/ppermute | solution.py:515
  41.8 35.9 %collective-permute-start.5 = (bf16[96,8320]{1,0:T(8,128)(2,1)S(1)}, bf16[96,8320]{1,0:T(8,128)(2,1)S(1)}, u32[]{:S(2)}, u32[]{:S(2)}) collective-permute-start(bf16[96,8320]{1,0:T(8,128)(2,1)S(1)} %get-tuple-element.74), channel_id=1, source_target_pairs={{0,16},{4,20},{8,24},{12,28},{16,0},{20,4},{24,8},{28,12},{1,17},{... | collective-permute-start | bytes 4792328 | tf_op jit(solution)/shard_map/ppermute | solution.py:515
  44.4 2.0 %collective-permute-start.8 = (bf16[128,2176]{1,0:T(8,128)(2,1)S(1)}, bf16[128,2176]{1,0:T(8,128)(2,1)S(1)}, u32[]{:S(2)}, u32[]{:S(2)}) collective-permute-start(bf16[128,2176]{1,0:T(8,128)(2,1)S(1)} %get-tuple-element.86), channel_id=1, source_target_pairs={{0,4},{4,0},{8,12},{12,8},{16,20},{20,16},{24,28},{28,24},{1,5},{5... | collective-permute-start | bytes 1671176 | tf_op jit(solution)/shard_map/ppermute | solution.py:515
  44.5 19.0 %collective-permute-start.10 = (bf16[128,2176]{1,0:T(8,128)(2,1)S(1)}, bf16[128,2176]{1,0:T(8,128)(2,1)S(1)}, u32[]{:S(2)}, u32[]{:S(2)}) collective-permute-start(bf16[128,2176]{1,0:T(8,128)(2,1)S(1)} %get-tuple-element.89), channel_id=1, source_target_pairs={{0,4},{4,0},{8,12},{12,8},{16,20},{20,16},{24,28},{28,24},{1,5},{5... | collective-permute-start | bytes 1671176 | tf_op jit(solution)/shard_map/ppermute | solution.py:515
  46.5 17.9 %collective-permute-start.11 = (bf16[128,2176]{1,0:T(8,128)(2,1)S(1)}, bf16[128,2176]{1,0:T(8,128)(2,1)S(1)}, u32[]{:S(2)}, u32[]{:S(2)}) collective-permute-start(bf16[128,2176]{1,0:T(8,128)(2,1)S(1)} %merge.1.refs_0_), channel_id=1, source_target_pairs={{0,1},{1,0},{2,3},{3,2},{4,5},{5,4},{6,7},{7,6},{8,9},{9,8},{10,11... | collective-permute-start | bytes 1671176 | tf_op jit(solution)/shard_map/ppermute | solution.py:515
  48.1 15.3 %collective-permute-start.9 = (bf16[64,1152]{1,0:T(8,128)(2,1)S(1)}, bf16[64,1152]{1,0:T(8,128)(2,1)S(1)}, u32[]{:S(2)}, u32[]{:S(2)}) collective-permute-start(bf16[64,1152]{1,0:T(8,128)(2,1)S(1)} %get-tuple-element.87.refs_0_), channel_id=1, source_target_pairs={{0,2},{1,3},{2,0},{3,1},{4,6},{5,7},{6,4},{7,5},{8,10},{9,11},{10,... | collective-permute-start | bytes 442376 | tf_op jit(solution)/shard_map/ppermute | solution.py:515
  64.8 15.5 %collective-permute-start.12 = (bf16[128,1152]{1,0:T(8,128)(2,1)S(1)}, bf16[128,1152]{1,0:T(8,128)(2,1)S(1)}, u32[]{:S(2)}, u32[]{:S(2)}) collective-permute-start(bf16[128,1152]{1,0:T(8,128)(2,1)S(1)} %get-tuple-element.90.refs_0_), channel_id=1, source_target_pairs={{0,2},{1,3},{2,0},{3,1},{4,6},{5,7},{6,4},{7,5},{8,10},{9,11},{10,... | collective-permute-start | bytes 884744 | tf_op jit(solution)/shard_map/ppermute | solution.py:515
  80.3 14.6 %collective-permute-start.13 = (bf16[32,8320]{1,0:T(8,128)(2,1)S(1)}, bf16[32,8320]{1,0:T(8,128)(2,1)S(1)}, u32[]{:S(2)}, u32[]{:S(2)}) collective-permute-start(bf16[32,8320]{1,0:T(8,128)(2,1)S(1)} %slice.20), channel_id=1, source_target_pairs={{0,16},{4,20},{8,24},{12,28},{16,0},{20,4},{24,8},{28,12},{1,17},{... | collective-permute-start | bytes 1597448 | tf_op jit(solution)/shard_map/ppermute | solution.py:515
  81.3 17.9 %collective-permute-start.14 = (bf16[32,8320]{1,0:T(8,128)(2,1)S(1)}, bf16[32,8320]{1,0:T(8,128)(2,1)S(1)}, u32[]{:S(2)}, u32[]{:S(2)}) collective-permute-start(bf16[32,8320]{1,0:T(8,128)(2,1)S(1)} %slice.21), channel_id=1, source_target_pairs={{0,8},{4,12},{8,0},{12,4},{16,24},{20,28},{24,16},{28,20},{1,9},{5... | collective-permute-start | bytes 1597448 | tf_op jit(solution)/shard_map/ppermute | solution.py:515
  94.3 13.1 %collective-permute-start.15 = (bf16[128,2176]{1,0:T(8,128)(2,1)S(1)}, bf16[128,2176]{1,0:T(8,128)(2,1)S(1)}, u32[]{:S(2)}, u32[]{:S(2)}) collective-permute-start(bf16[128,2176]{1,0:T(8,128)(2,1)S(1)} %get-tuple-element.96), channel_id=1, source_target_pairs={{0,1},{1,0},{2,3},{3,2},{4,5},{5,4},{6,7},{7,6},{8,9},{9,8},{10,11... | collective-permute-start | bytes 1671176 | tf_op jit(solution)/shard_map/ppermute | solution.py:515
  99.2 11.9 %copy-start.6 = (bf16[32,8320]{1,0:T(8,128)(2,1)S(1)}, bf16[32,8320]{1,0:T(8,128)(2,1)}, u32[]{:S(2)}) copy-start(bf16[32,8320]{1,0:T(8,128)(2,1)} %get-tuple-element.65.refs_1_.refs_2_) | copy-start | bytes 1597444
  104.6 16.7 %collective-permute-start.16 = (bf16[64,2176]{1,0:T(8,128)(2,1)S(1)}, bf16[64,2176]{1,0:T(8,128)(2,1)S(1)}, u32[]{:S(2)}, u32[]{:S(2)}) collective-permute-start(bf16[64,2176]{1,0:T(8,128)(2,1)S(1)} %get-tuple-element.101), channel_id=1, source_target_pairs={{0,1},{1,0},{2,3},{3,2},{4,5},{5,4},{6,7},{7,6},{8,9},{9,8},{10,11... | collective-permute-start | bytes 835592 | tf_op jit(solution)/shard_map/ppermute | solution.py:515
  107.6 24.0 %collective-permute-start.20 = (bf16[128,1152]{1,0:T(8,128)(2,1)S(1)}, bf16[128,1152]{1,0:T(8,128)(2,1)S(1)}, u32[]{:S(2)}, u32[]{:S(2)}) collective-permute-start(bf16[128,1152]{1,0:T(8,128)(2,1)S(1)} %get-tuple-element.97.refs_0_), channel_id=1, source_target_pairs={{0,2},{1,3},{2,0},{3,1},{4,6},{5,7},{6,4},{7,5},{8,10},{9,11},{10,... | collective-permute-start | bytes 884744 | tf_op jit(solution)/shard_map/ppermute | solution.py:515
  121.3 23.3 %copy-start.8 = (f32[256,8]{0,1:T(8,128)S(1)}, f32[256,8]{0,1:T(8,128)}, u32[]{:S(2)}) copy-start(f32[256,8]{0,1:T(8,128)} %param.9) | copy-start | bytes 24580
  121.3 23.3 %copy-start.9 = (s32[256,1]{0,1:T(1,128)S(1)}, s32[256,1]{0,1:T(1,128)}, u32[]{:S(2)}) copy-start(s32[256,1]{0,1:T(1,128)} %param.10) | copy-start | bytes 3076
  121.4 12.7 %collective-permute-start.26 = (bf16[64,1152]{1,0:T(8,128)(2,1)S(1)}, bf16[64,1152]{1,0:T(8,128)(2,1)S(1)}, u32[]{:S(2)}, u32[]{:S(2)}) collective-permute-start(bf16[64,1152]{1,0:T(8,128)(2,1)S(1)} %get-tuple-element.115.refs_0_), channel_id=1, source_target_pairs={{0,2},{1,3},{2,0},{3,1},{4,6},{5,7},{6,4},{7,5},{8,10},{9,11},{10,... | collective-permute-start | bytes 442376 | tf_op jit(solution)/shard_map/ppermute | solution.py:515
  121.5 4.6 %collective-permute-start.17 = (f32[8,128]{1,0:T(8,128)S(1)}, f32[8,128]{1,0:T(8,128)S(1)}, u32[]{:S(2)}, u32[]{:S(2)}) collective-permute-start(f32[8,128]{1,0:T(8,128)S(1)} %get-tuple-element.103.refs_0_.refs_1_), channel_id=1, source_target_pairs={{0,1},{1,0},{2,3},{3,2},{4,5},{5,4},{6,7},{7,6},{8,9},{9,8},{10,11... | collective-permute-start | bytes 12296 | tf_op jit(solution)/shard_map/ppermute | solution.py:515
  123.3 6.7 %collective-permute-start.18 = (f32[8,128]{1,0:T(8,128)S(1)}, f32[8,128]{1,0:T(8,128)S(1)}, u32[]{:S(2)}, u32[]{:S(2)}) collective-permute-start(f32[8,128]{1,0:T(8,128)S(1)} %get-tuple-element.103.refs_0_.refs_1_), channel_id=1, source_target_pairs={{0,2},{1,3},{2,0},{3,1},{4,6},{5,7},{6,4},{7,5},{8,10},{9,11},{10,... | collective-permute-start | bytes 12296 | tf_op jit(solution)/shard_map/ppermute | solution.py:515
  126.2 5.4 %collective-permute-start.19 = (f32[8,128]{1,0:T(8,128)S(1)}, f32[8,128]{1,0:T(8,128)S(1)}, u32[]{:S(2)}, u32[]{:S(2)}) collective-permute-start(f32[8,128]{1,0:T(8,128)S(1)} %get-tuple-element.103.refs_0_.refs_1_), channel_id=1, source_target_pairs={{0,3},{1,2},{2,1},{3,0},{4,7},{5,6},{6,5},{7,4},{8,11},{9,10},{10,... | collective-permute-start | bytes 12296 | tf_op jit(solution)/shard_map/ppermute | solution.py:515
  131.8 12.8 %collective-permute-start.22 = (bf16[64,1152]{1,0:T(8,128)(2,1)S(1)}, bf16[64,1152]{1,0:T(8,128)(2,1)S(1)}, u32[]{:S(2)}, u32[]{:S(2)}) collective-permute-start(bf16[64,1152]{1,0:T(8,128)(2,1)S(1)} %get-tuple-element.110), channel_id=1, source_target_pairs={{0,8},{4,12},{8,0},{12,4},{16,24},{20,28},{24,16},{28,20},{1,9},{5... | collective-permute-start | bytes 442376 | tf_op jit(solution)/shard_map/ppermute | solution.py:515
  131.9 12.6 %collective-permute-start.24 = (bf16[64,1152]{1,0:T(8,128)(2,1)S(1)}, bf16[64,1152]{1,0:T(8,128)(2,1)S(1)}, u32[]{:S(2)}, u32[]{:S(2)}) collective-permute-start(bf16[64,1152]{1,0:T(8,128)(2,1)S(1)} %get-tuple-element.112), channel_id=1, source_target_pairs={{0,16},{4,20},{8,24},{12,28},{16,0},{20,4},{24,8},{28,12},{1,17},{... | collective-permute-start | bytes 442376 | tf_op jit(solution)/shard_map/ppermute | solution.py:515
  133.8 1.9 %collective-permute-start.21 = (bf16[32,1152]{1,0:T(8,128)(2,1)S(1)}, bf16[32,1152]{1,0:T(8,128)(2,1)S(1)}, u32[]{:S(2)}, u32[]{:S(2)}) collective-permute-start(bf16[32,1152]{1,0:T(8,128)(2,1)S(1)} %get-tuple-element.109), channel_id=1, source_target_pairs={{0,4},{4,0},{8,12},{12,8},{16,20},{20,16},{24,28},{28,24},{1,5},{5... | collective-permute-start | bytes 221192 | tf_op jit(solution)/shard_map/ppermute | solution.py:515
  133.8 4.2 %collective-permute-start.23 = (bf16[32,1152]{1,0:T(8,128)(2,1)S(1)}, bf16[32,1152]{1,0:T(8,128)(2,1)S(1)}, u32[]{:S(2)}, u32[]{:S(2)}) collective-permute-start(bf16[32,1152]{1,0:T(8,128)(2,1)S(1)} %get-tuple-element.111), channel_id=1, source_target_pairs={{0,12},{4,8},{8,4},{12,0},{16,28},{20,24},{24,20},{28,16},{1,13},{... | collective-permute-start | bytes 221192 | tf_op jit(solution)/shard_map/ppermute | solution.py:515
  134.2 10.3 %collective-permute-start.27 = (bf16[64,1152]{1,0:T(8,128)(2,1)S(1)}, bf16[64,1152]{1,0:T(8,128)(2,1)S(1)}, u32[]{:S(2)}, u32[]{:S(2)}) collective-permute-start(bf16[64,1152]{1,0:T(8,128)(2,1)S(1)} %get-tuple-element.116), channel_id=1, source_target_pairs={{0,24},{4,28},{8,16},{12,20},{16,8},{20,12},{24,0},{28,4},{1,25},{... | collective-permute-start | bytes 442376 | tf_op jit(solution)/shard_map/ppermute | solution.py:515
  135.8 8.8 %collective-permute-start.25 = (bf16[32,1152]{1,0:T(8,128)(2,1)S(1)}, bf16[32,1152]{1,0:T(8,128)(2,1)S(1)}, u32[]{:S(2)}, u32[]{:S(2)}) collective-permute-start(bf16[32,1152]{1,0:T(8,128)(2,1)S(1)} %get-tuple-element.113.refs_0_), channel_id=1, source_target_pairs={{0,20},{4,16},{8,28},{12,24},{16,4},{20,0},{24,12},{28,8},{1,21},{... | collective-permute-start | bytes 221192 | tf_op jit(solution)/shard_map/ppermute | solution.py:515
  138.1 6.5 %collective-permute-start.28 = (bf16[32,1152]{1,0:T(8,128)(2,1)S(1)}, bf16[32,1152]{1,0:T(8,128)(2,1)S(1)}, u32[]{:S(2)}, u32[]{:S(2)}) collective-permute-start(bf16[32,1152]{1,0:T(8,128)(2,1)S(1)} %get-tuple-element.117), channel_id=1, source_target_pairs={{0,28},{4,24},{8,20},{12,16},{16,12},{20,8},{24,4},{28,0},{1,29},{... | collective-permute-start | bytes 221192 | tf_op jit(solution)/shard_map/ppermute | solution.py:515
  (9 other events, 31.1 us)

commit v2 on v1

--- a/solution.py
+++ b/solution.py
@@ -67,8 +67,8 @@
 
 
 def dispatch_body(plan, experts, cap, width, x_hbm, dy_hbm, logits_hbm, ids_hbm, *refs):
-    outs, hot = refs[: len(plan)], refs[len(plan)]
-    held, logits, ids, sems = refs[len(plan) + 1 :]
+    outs, part, hot = refs[: len(plan)], refs[len(plan)], refs[len(plan) + 1]
+    held, logits, ids, sems = refs[len(plan) + 2 :]
     loads = [
         pltpu.make_async_copy(ids_hbm, ids, sems.at[0]),
         pltpu.make_async_copy(logits_hbm, logits, sems.at[1]),
@@ -100,6 +100,8 @@
     places = [(m, outs[i], j * cap) for i, held_by in enumerate(plan) for j, m in enumerate(held_by)]
     for m, out, first in places:
         out[first : first + cap, 2 * width :] = pad[m * cap : (m + 1) * cap]
+    part[:, width:] = pad[experts * cap :]
+    parity = lax.rem(lax.axis_index("dp"), 2)
     spread = spread.astype(BF16)
     tile = 1024
     for half in range(2):
@@ -113,6 +115,10 @@
                     m * cap : (m + 1) * cap
                 ]
 
+            @pl.when(parity == half)
+            def _():
+                part[:, at : at + tile] = moved[experts * cap :]
+
 
 def dispatch(rows_x, rows_dy, logits, ids, experts, cap, plan):
     rows, width = rows_x.shape
@@ -121,9 +127,10 @@
         functools.partial(dispatch_body, plan, experts, cap, width),
         "dispatch",
         [jax.ShapeDtypeStruct((len(held_by) * cap, wide), BF16) for held_by in plan]
+        + [jax.ShapeDtypeStruct((cap, width + LANES), BF16)]
         + [jax.ShapeDtypeStruct((1,), jnp.int32)],
         [HBM] * 4,
-        [VMEM] * len(plan) + [SMEM],
+        [VMEM] * (len(plan) + 1) + [SMEM],
         [
             pltpu.VMEM((2, rows, width), BF16),
             pltpu.VMEM(logits.shape, F32),
@@ -145,6 +152,28 @@
     ).astype(BF16)
 
 
+def moves(ranges, width, extra):
+    parity = lax.rem(lax.axis_index("dp"), 2)
+    found, at = [], 0
+    for p, (first, count, side) in enumerate(ranges):
+        if side is None:
+            found.append((p, first, count, 0, 2 * width + extra, at, 0))
+        elif side == "this":
+            found.append((p, first, count, 0, width, at, pl.multiple_of(parity * width, width)))
+            if extra:
+                found.append((p, first, count, width, extra, at, 2 * width))
+        else:
+            at -= count
+            column = pl.multiple_of((1 - parity) * width, width)
+            found.append((p, first, count, 0, width, at, column))
+        at += count
+    return found
+
+
+def rows_in(ranges):
+    return sum(count for _, count, side in ranges if side != "that")
+
+
 def rows_body(ranges, width, n_dp, guarded, hot, *refs):
     pieces = len(ranges)
     sources, weights = refs[:pieces], refs[pieces : pieces + 3]
@@ -154,17 +183,16 @@
     rows = held.shape[0]
 
     def work():
-        copies, at = [], 0
-        for p in range(pieces):
-            first, count = ranges[p]
-            copies.append(
-                pltpu.make_async_copy(
-                    sources[p].at[pl.ds(first, count), :],
-                    held.at[pl.ds(at, count), :],
-                    piece_sems.at[p],
-                )
+        copies = [
+            pltpu.make_async_copy(
+                sources[p].at[pl.ds(first, count), pl.ds(column, columns)],
+                held.at[pl.ds(at, count), pl.ds(target, columns)],
+                piece_sems.at[i],
             )
-            at += count
+            for i, (p, first, count, column, columns, at, target) in enumerate(
+                moves(ranges, width, LANES)
+            )
+        ]
         for copy in copies:
             copy.start()
         for copy in copies:
@@ -233,9 +261,9 @@
 def rows_backward(earlier, hot, parts, weights, n_dp, guarded, micros=0.001):
     width = weights[0].shape[1]
     hidden_units = weights[0].shape[0]
-    sources = [source for source, _, _ in parts]
-    ranges = [(first, count) for _, first, count in parts]
-    rows = sum(count for _, count in ranges)
+    sources = [source for source, *_ in parts]
+    ranges = [tuple(where) for _, *where in parts]
+    rows = rows_in(ranges)
     part = width // 2 + LANES
     shapes = [(rows // 2, part)] * 4 if guarded else [(rows, part)] * 2
     return call(
@@ -247,7 +275,7 @@
         [VMEM] * (len(shapes) + 1),
         [
             pltpu.VMEM((rows, 2 * width + LANES), BF16),
-            pltpu.SemaphoreType.DMA((len(sources),)),
+            pltpu.SemaphoreType.DMA((2 * len(sources),)),
         ],
         micros,
         20,
@@ -314,7 +342,7 @@
 def last_body(cut, cap, places, count, *refs):
     pairs = len(places)
     squares, given, outs = refs[:count], refs[count : count + 2 * pairs], refs[count + 2 * pairs :]
-    total = tree([part[0:1, 0:1] for part in squares])
+    total = tree([part[0:1, 0:1] for part in squares]) if squares else jnp.zeros((1, 1), F32)
     lane = lane_iota((1, LANES))
     square = jnp.zeros((1, LANES), F32)
     for i in range(3):
@@ -326,20 +354,17 @@
         whole = sum_of(pair, slice(0, cut)).astype(BF16)
         gates = jnp.sum(sum_of(pair, slice(cut, None)), axis=1, keepdims=True)
         lanes = jnp.where(lane == 0, gates, square).astype(BF16)
-        for start, out, first in where:
-            outs[out][first : first + cap, :cut] = whole[start : start + cap]
-            outs[out][first : first + cap, cut:] = lanes[start : start + cap]
+        for start, out in where:
+            outs[out][:, :cut] = whole[start : start + cap]
+            outs[out][:, cut:] = lanes[start : start + cap]
 
 
 def last(earlier, squares, pairs, chunks, masks, cut, cap):
-    places = []
-    for i, chunk in enumerate(chunks):
-        first = cap if i == len(chunks) - 1 else 0
-        places.append([(j * cap, masks.index(m), first) for j, m in enumerate(chunk) if m in masks])
+    places = [[(j * cap, masks.index(m)) for j, m in enumerate(chunk)] for chunk in chunks]
     return call(
         functools.partial(last_body, cut, cap, places, len(squares)),
         "last",
-        [jax.ShapeDtypeStruct((cap if m % 2 else 2 * cap, cut + LANES), BF16) for m in masks],
+        [jax.ShapeDtypeStruct((cap, cut + LANES), BF16)] * len(masks),
         [VMEM] * (len(squares) + 2 * len(pairs)),
         [VMEM] * len(masks),
         [],
@@ -357,16 +382,16 @@
     step = pl.program_id(0)
     hidden_units = outs[0].shape[0]
 
-    starts = [sum(count for _, count in ranges[:p]) for p in range(pieces + 1)]
 
     def copies(count):
         return [
             pltpu.make_async_copy(
-                sources[p].at[pl.ds(ranges[p][0], ranges[p][1]), pl.ds(0, 2 * width)],
-                held.at[pl.ds(starts[p], ranges[p][1]), :],
+                sources[p].at[pl.ds(first, size), pl.ds(column, columns)],
+                held.at[pl.ds(at, size), pl.ds(target, columns)],
                 sems.at[p],
             )
-            for p in count
+            for p, first, size, column, columns, at, target in moves(ranges, width, 0)
+            if p in count
         ]
 
     @pl.when(step == 0)
@@ -405,11 +430,11 @@
 
     @pl.when(hot[0] == 1)
     def _():
-        work(starts[pieces])
+        work(rows_in(ranges))
 
     @pl.when(hot[0] != 1)
     def _():
-        work(starts[cold_pieces])
+        work(rows_in(ranges[:cold_pieces]))
 
     @pl.when(step == pl.num_programs(0) - 1)
     def _():
@@ -418,9 +443,9 @@
 
 def weights_backward(earlier, hot, cold, extra, acts, hidden_units, width):
     tile = 512
-    sources = [source for source, _, _ in cold + extra]
-    ranges = [(first, count) for _, first, count in cold + extra]
-    rows = sum(count for _, count in ranges)
+    sources = [source for source, *_ in cold + extra]
+    ranges = [tuple(where) for _, *where in cold + extra]
+    rows = rows_in(ranges)
     block = pl.BlockSpec((hidden_units, tile), lambda j: (0, j))
     whole = [pl.BlockSpec(a.shape, lambda j: (0, 0)) for a in acts]
     return call(
@@ -447,7 +472,8 @@
 
 def home_body(experts, cap, cut, row_total, firsts, logits, ids, *refs):
     arrived, back = refs[:experts], refs[experts : 2 * experts]
-    grad_rows, grad_logits, norm, pads, table, sems = refs[2 * experts :]
+    extra = refs[2 * experts : 2 * experts + experts // 2]
+    grad_rows, grad_logits, norm, pads, table, sems = refs[2 * experts + experts // 2 :]
     copies = [
         pltpu.make_async_copy(
             arrived[m].at[pl.ds(firsts[m], 16), pl.ds(arrived[m].shape[1] - LANES, LANES)],
@@ -461,10 +487,10 @@
     onehot, spread = routing(ids[...], lax.axis_index("expert"), cap, experts)
     slots = (experts + 1) * cap
     for m in range(experts):
-        table[m * cap : (m + 1) * cap, :] = back[m][:cap, :]
-    over = back[0][cap:, :]
-    for m in range(2, experts, 2):
-        over = over + back[m][cap:, :]
+        table[m * cap : (m + 1) * cap, :] = back[m][...]
+    over = extra[0][...]
+    for piece in extra[1:]:
+        over = over + piece[...]
     table[experts * cap :, :] = over
     lane = lane_iota((8, LANES))
     square = tree([back[m][0:16, cut:].astype(F32)[0:8] for m in range(experts)])
@@ -484,13 +510,13 @@
     grad_logits[...] = probs * (pulls - jnp.sum(probs * pulls, axis=0, keepdims=True))
 
 
-def home(logits, ids, arrived, back, cap, row_total):
+def home(logits, ids, arrived, back, extra, cap, row_total):
     experts = len(back)
     rows = ids.shape[1]
     cut = back[0].shape[1] - LANES
     return call(
         functools.partial(
-            home_body, experts, cap, cut, row_total, [first for _, first, _ in arrived]
+            home_body, experts, cap, cut, row_total, [first for _, first, *_ in arrived]
         ),
         "home",
         [
@@ -498,7 +524,7 @@
             jax.ShapeDtypeStruct(logits.shape, F32),
             jax.ShapeDtypeStruct((1,), F32),
         ],
-        [VMEM, VMEM] + [ANY] * experts + [VMEM] * experts,
+        [VMEM, VMEM] + [ANY] * experts + [VMEM] * (experts + len(extra)),
         [VMEM, VMEM, SMEM],
         [
             pltpu.VMEM((16 * experts, LANES), BF16),
@@ -507,7 +533,7 @@
         ],
         0.001,
         12,
-    )(logits, ids, *[piece for piece, _, _ in arrived], *back)
+    )(logits, ids, *[piece for piece, *_ in arrived], *back, *extra)
 
 
 def swap(value, axis, mask):
@@ -537,7 +563,7 @@
     first_hop = {b: [m for m in path if path[m][0] == b] for b in near}
     plan = [[0], [1, experts, *range(3, experts, 2)], [experts]]
     plan += [[b] + [m for m in first_hop[b] if m % 2 == 0] for b in near]
-    own, beside, spare, *mine, hot = dispatch(
+    own, beside, spare, *mine, part, hot = dispatch(
         rows_x, rows_dy, logits, ids, experts, cap, plan
     )
     bits = [1 << i for i in range(n_dp.bit_length() - 1)]
@@ -569,35 +595,34 @@
         at = plan[1].index(m) * cap
         return beside[at : at + cap]
 
-    cold = {0: (own, 0, cap), 1: (beside, 0, cap)}
+    cold = {0: (own, 0, cap, None), 1: (beside, 0, cap, None)}
     chunks = [[0, 1], [m ^ c for c in (0, 1) for m in near], [m ^ c for c in (0, 1) for m in far]]
-    over = {m: swap(spare, "expert", m) for m in near}
+    over = [swap(part, "expert", m) for m in evens[1:]]
     *first, acts_first = backward([cold[m] for m in chunks[0]])
-    (later,), (acts_first,) = after([spare], [acts_first])
-    over.update({m: swap(later, "expert", m) for m in far})
-    over = [over[m] for m in evens[1:]]
+    over, (acts_first,) = after(over, [acts_first])
+    this = jnp.concatenate(over, axis=0)
+    that = swap(this, "dp", 1)
     kept, sent = step(fold, turn(first, bits[0]), cut)
-    packed, (sent,) = after(over, [sent])
-    crossed = swap(jnp.concatenate(packed, axis=0), "expert", 1)
+    (that,), (sent,) = after([that], [sent])
     first = turn((kept, sent), bits[1])
     for bit in bits[2:]:
         first = turn(step(fold, first, cut), bit)
+    count = this.shape[0]
+    extras = [(spare, 0, cap, None), (this, 0, count, "this"), (that, 0, count, "that")]
+    extras += [(beside, cap, cap, None)]
+    extras += [(swap(this, "expert", 1), 0, count, "this")]
+    extras += [(swap(that, "expert", 1), 0, count, "that")]
     loads = []
     for b, part in zip(near, mine):
         odd = [b ^ 1] + [m for m in first_hop[b] if m % 2]
         loads.append(jnp.concatenate([part] + [from_beside(m) for m in odd], axis=0))
-    loads, over = after(loads, over)
-    extras = [(part, 0, cap) for part in [spare, *over]]
-    extras += [(beside, cap, cap), (crossed, 0, crossed.shape[0])]
+    loads, (this,) = after(loads, [this])
     loads = [swap(load, "expert", b) for b, load in zip(near, loads)]
 
     kept, sent, far_kept, far_sent, acts_hot = backward(extras, True)
     far_sent = swap(far_sent, "expert", 1)
     far_kept = swap(far_kept, "expert", 1)
     (sent,) = step(merge, sent, far_sent)
-    wait_for(first[-1])
-    busy = turn((kept, far_kept, sent), bits[0])
-    busy = middle(busy)
     passed = {}
     for b, load in zip(near, loads):
         items = [b] + [m for m in first_hop[b] if m % 2 == 0]
@@ -606,19 +631,19 @@
             if m in path:
                 passed[m] = load[i * cap : (i + 1) * cap]
             else:
-                cold[m] = (load, i * cap, cap)
+                cold[m] = (load, i * cap, cap, None)
     on_way = list(passed)
-    parts, (met,) = after([passed[m] for m in on_way], [busy[-1]])
-    busy = (*busy[:-1], met)
+    parts, (sent,) = after([passed[m] for m in on_way], [sent])
     for m, part in zip(on_way, parts):
         for b in path[m][1:]:
             part = swap(part, "expert", b)
-        cold[m] = (part, 0, cap)
+        cold[m] = (part, 0, cap, None)
+    busy = turn((kept, far_kept, sent), bits[0])
     *second, acts_second = backward([cold[m] for m in chunks[1]])
     second = turn(second, bits[0])
+    busy = middle(busy)
     *third, acts_third = backward([cold[m] for m in chunks[2]])
     third = turn(third, bits[0])
-    second = middle(second)
     grad_gate, grad_up, grad_down, squares = step(
         weights_backward,
         hot,
@@ -628,23 +653,29 @@
         hidden_units,
         width,
     )
+    wait_for(busy[-1], first[-1])
+    second = middle(second)
     for bit in bits[1:]:
         kept, sent = step(fold, third, cut)
         (squares,), (sent,) = after([squares], [sent])
         third = turn((kept, sent), bit)
     squares = [squares] + [swap(squares, "dp", m) for m in range(1, n_dp)]
+    over_back = step(last, [], [busy], [evens], evens, cut, cap)
+    over_back = [piece if m == 0 else swap(piece, "expert", m) for m, piece in zip(evens, over_back)]
+    wait_for(*over_back[1:])
     back = {}
-    for masks, pairs, where in (
-        (chunks[0] + chunks[1], [first, second, busy], [*chunks[:2], evens]),
-        (chunks[2], [third, busy], [chunks[2], evens]),
+    for masks, given, where in (
+        (chunks[0] + chunks[1], [first, second], chunks[:2]),
+        (chunks[2], [third], chunks[2:]),
     ):
-        for m, piece in zip(masks, step(last, squares, pairs, where, masks, cut, cap)):
+        for m, piece in zip(masks, step(last, squares, given, where, masks, cut, cap)):
             back[m] = piece if m == 0 else swap(piece, "expert", m)
     grad_rows, grad_logits, norm = home(
         logits,
         ids,
         [cold[m] for m in range(experts)],
         [back[m] for m in range(experts)],
+        over_back,
         cap,
         rows * experts,
     )

time: 146 us -> 140 us (0.959)
  starting transfers between devices: 47.4 us -> 34.9 us
  waiting for transfers between devices: 55.1 us -> 59.6 us
    ppermute x29 -> x34, starting transfers between devices: 47.4 us -> 34.9 us  [swap(): return lax.ppermute(value, axis, [(i, i ^ mask) for i in range(size)])]
    ppermute x29 -> x34, waiting for transfers between devices: 55.1 us -> 59.6 us  [swap(): return lax.ppermute(value, axis, [(i, i ^ mask) for i in range(size)])]
    unnamed x24 -> x26, local copies, waits for them, and re-layouts: 6 us -> 5.56 us
  transfers between devices with their start and end apart: 29 -> 34, of which waited for: 15 -> 18; matrix products, arithmetic and copies ran while one was open for 0% -> 0% of each run, Pallas kernels for 20% -> 21%
where the time goes in v2:
time: 140 us; the launch traced here: 139 us
  waiting for transfers between devices  59.6 us (43%)
  Pallas kernels  37.6 us (27%)
  starting transfers between devices  34.9 us (25%)
  local copies, waits for them, and re-layouts  5.77 us (4%)
    ppermute x34, waiting for transfers between devices, swap(): return lax.ppermute(value, axis, [(i, i ^ mask) for i in range(size)])  59.6 us
    ppermute x34, starting transfers between devices, swap(): return lax.ppermute(value, axis, [(i, i ^ mask) for i in range(size)])  34.9 us
    pallas_call x4, Pallas kernels, rows_backward(): call(functools.partial(rows_body, ranges, width, n_dp, guarded), 'rows_ba...  17.5 us
    pallas_call x1, Pallas kernels, weights_backward(): call(functools.partial(weights_body, ranges, len(cold), len(acts), width,...  10.2 us
    pallas_call x1, Pallas kernels, dispatch(): call(functools.partial(dispatch_body, plan, experts, cap, width), 'dispat...  6.84 us
    unnamed x26, local copies, waits for them, and re-layouts  5.56 us
  transfers between devices with their start and end apart: 34, of which 18 were waited for; matrix products, arithmetic and copies ran while one was open for 0% of the time, Pallas kernels for 21%

profile of v2, /device:TPU:0, one launch (start us, length us, event | category | flops | bytes accessed | tf_op | source)
XLA Modules:
  0.0 139.2 jit_solution(10611446975569736404)
XLA Ops:
  0.6 6.8 %dispatch.1 = (bf16[32,8320]{1,0:T(8,128)(2,1)}, bf16[160,8320]{1,0:T(8,128)(2,1)}, bf16[32,8320]{1,0:T(8,128)(2,1)}, bf16[64,8320]{1,0:T(8,128)(2,1)}, bf16[32,...) custom-call(bf16[256,4096]{1,0:T(8,128)(2,1)} %refs_0_.1, bf16[256,4096]{1,0:T(8,128)(2,1)} %refs_1_.1, ...), custom_call_target="tpu_custom_call" | custom-call | flops 6000000000 | bytes 1000 | tf_op jit(solution)/shard_map/dispatch/pallas_call | solution.py:126
  8.0 3.5 %collective-permute-start.3 = (bf16[32,4224]{1,0:T(8,128)(2,1)}, bf16[32,4224]{1,0:T(8,128)(2,1)S(1)}, u32[]{:S(2)}, u32[]{:S(2)}) collective-permute-start(bf16[32,4224]{1,0:T(8,128)(2,1)} %get-tuple-element.71), channel_id=1, source_target_pairs={{0,24},{4,28},{8,16},{12,20},{16,8},{20,12},{24,0},{28,4},{1,25},{... | collective-permute-start | bytes 811016 | tf_op jit(solution)/shard_map/ppermute | solution.py:541
  12.8 1.9 %copy-done.1 = bf16[1,384,4096]{2,1,0:T(8,128)(2,1)S(1)} copy-done((bf16[1,384,4096]{2,1,0:T(8,128)(2,1)S(1)}, bf16[1,384,4096]{2,1,0:T(8,128)(2,1)}, u32[]{:S(2)}) %copy-start.1) | copy-done | bytes 3145752
  14.7 1.9 %copy-done.3 = bf16[1,384,4096]{2,1,0:T(8,128)(2,1)S(1)} copy-done((bf16[1,384,4096]{2,1,0:T(8,128)(2,1)S(1)}, bf16[1,384,4096]{2,1,0:T(8,128)(2,1)}, u32[]{:S(2)}) %copy-start.3) | copy-done | bytes 3145752
  17.6 5.4 %rows_backward.4 = (bf16[64,2176]{1,0:T(8,128)(2,1)S(1)}, bf16[64,2176]{1,0:T(8,128)(2,1)S(1)}, bf16[64,1152]{1,0:T(8,128)(2,1)S(1)}) custom-call(s32[1]{0:T(128)} %get-tuple-element.72.refs_0_.refs_1_, bf16[32,8320]{1,0:T(8,128)(2,1)S(1)} %copy-done.5, bf16[160,8320]{1,0:T(8,128)(2,1)S(1)} %collective-permute-done.refs_2_.refs_5_.refs_3_.refs_13_, ...), custom_call_target="tpu_custom_call" | custom-call | flops 1000000 | bytes 1000 | tf_op jit(solution)/shard_map/rows_backward/pallas_call | solution.py:269
  23.1 1.5 %collective-permute-done.2 = bf16[32,4224]{1,0:T(8,128)(2,1)S(1)} collective-permute-done((bf16[32,4224]{1,0:T(8,128)(2,1)}, bf16[32,4224]{1,0:T(8,128)(2,1)S(1)}, u32[]{:S(2)}, u32[]{:S(2)}) %collective-permute-start.2) | collective-permute-done | bytes 270368 | tf_op jit(solution)/shard_map/ppermute | solution.py:541
  24.9 1.6 %collective-permute-start.6 = (bf16[64,2176]{1,0:T(8,128)(2,1)S(1)}, bf16[64,2176]{1,0:T(8,128)(2,1)S(1)}, u32[]{:S(2)}, u32[]{:S(2)}) collective-permute-start(bf16[64,2176]{1,0:T(8,128)(2,1)S(1)} %get-tuple-element.80), channel_id=1, source_target_pairs={{0,1},{1,0},{2,3},{3,2},{4,5},{5,4},{6,7},{7,6},{8,9},{9,8},{10,11... | collective-permute-start | bytes 835592 | tf_op jit(solution)/shard_map/ppermute | solution.py:541
  28.2 1.5 %collective-permute-start.4 = (bf16[96,8320]{1,0:T(8,128)(2,1)S(1)}, bf16[96,8320]{1,0:T(8,128)(2,1)S(1)}, u32[]{:S(2)}, u32[]{:S(2)}) collective-permute-start(bf16[96,8320]{1,0:T(8,128)(2,1)S(1)} %get-tuple-element.77), channel_id=1, source_target_pairs={{0,8},{4,12},{8,0},{12,4},{16,24},{20,28},{24,16},{28,20},{1,9},{5... | collective-permute-start | bytes 4792328 | tf_op jit(solution)/shard_map/ppermute | solution.py:541
  30.9 3.6 %collective-permute-done.6.refs_2_ = bf16[64,2176]{1,0:T(8,128)(2,1)S(1)} collective-permute-done((bf16[64,2176]{1,0:T(8,128)(2,1)S(1)}, bf16[64,2176]{1,0:T(8,128)(2,1)S(1)}, u32[]{:S(2)}, u32[]{:S(2)}) %collective-permute-start.6) | collective-permute-done | bytes 278560 | tf_op jit(solution)/shard_map/ppermute | solution.py:541
  34.6 16.1 %collective-permute-done.7.refs_4_.refs_12_ = bf16[96,4224]{1,0:T(8,128)(2,1)S(1)} collective-permute-done((bf16[96,4224]{1,0:T(8,128)(2,1)S(1)}, bf16[96,4224]{1,0:T(8,128)(2,1)S(1)}, u32[]{:S(2)}, u32[]{:S(2)}) %collective-permute-start.7) | collective-permute-done | bytes 811040 | tf_op jit(solution)/shard_map/ppermute | solution.py:541
  50.6 2.3 %collective-permute-done.9.refs_7_.refs_15_ = bf16[96,4224]{1,0:T(8,128)(2,1)S(1)} collective-permute-done((bf16[96,4224]{1,0:T(8,128)(2,1)S(1)}, bf16[96,4224]{1,0:T(8,128)(2,1)S(1)}, u32[]{:S(2)}, u32[]{:S(2)}) %collective-permute-start.9) | collective-permute-done | bytes 811040 | tf_op jit(solution)/shard_map/ppermute | solution.py:541
  54.3 10.4 %collective-permute-done.4.refs_2_.refs_4_.refs_6_.refs_5_ = bf16[96,8320]{1,0:T(8,128)(2,1)S(1)} collective-permute-done((bf16[96,8320]{1,0:T(8,128)(2,1)S(1)}, bf16[96,8320]{1,0:T(8,128)(2,1)S(1)}, u32[]{:S(2)}, u32[]{:S(2)}) %collective-permute-start.4) | collective-permute-done | bytes 1597472 | tf_op jit(solution)/shard_map/ppermute | solution.py:541
  66.9 1.3 collective-permute-start.11
  69.0 5.5 %rows_backward.6 = (bf16[128,2176]{1,0:T(8,128)(2,1)S(1)}, bf16[128,2176]{1,0:T(8,128)(2,1)S(1)}, bf16[128,1152]{1,0:T(8,128)(2,1)S(1)}) custom-call(bf16[128,2176]{1,0:T(8,128)(2,1)S(1)} %merge.1.refs_0_, s32[1]{0:T(128)} %get-tuple-element.72.refs_0_.refs_1_, bf16[96,8320]{1,0:T(8,128)(2,1)S(1)} %collective-permute-done.4.refs_2_.refs_4_.refs_6_.refs_5_, ...), custom_call_target="tpu_custom_call" | custom-call | flops 1000000 | bytes 1000 | tf_op jit(solution)/shard_map/rows_backward/pallas_call | solution.py:269
  74.5 1.4 collective-permute-start.17
  75.9 5.7 %collective-permute-done.14.refs_3_ = bf16[128,2176]{1,0:T(8,128)(2,1)S(1)} collective-permute-done((bf16[128,2176]{1,0:T(8,128)(2,1)S(1)}, bf16[128,2176]{1,0:T(8,128)(2,1)S(1)}, u32[]{:S(2)}, u32[]{:S(2)}) %collective-permute-start.14) | collective-permute-done | bytes 557088 | tf_op jit(solution)/shard_map/ppermute | solution.py:541
  82.1 2.7 %collective-permute-start.15 = (bf16[128,1152]{1,0:T(8,128)(2,1)S(1)}, bf16[128,1152]{1,0:T(8,128)(2,1)S(1)}, u32[]{:S(2)}, u32[]{:S(2)}) collective-permute-start(bf16[128,1152]{1,0:T(8,128)(2,1)S(1)} %get-tuple-element.93.refs_0_), channel_id=1, source_target_pairs={{0,2},{1,3},{2,0},{3,1},{4,6},{5,7},{6,4},{7,5},{8,10},{9,11},{10,... | collective-permute-start | bytes 884744 | tf_op jit(solution)/shard_map/ppermute | solution.py:541
  85.1 5.4 %rows_backward.7 = (bf16[64,2176]{1,0:T(8,128)(2,1)S(1)}, bf16[64,2176]{1,0:T(8,128)(2,1)S(1)}, bf16[64,1152]{1,0:T(8,128)(2,1)S(1)}) custom-call(bf16[128,1152]{1,0:T(8,128)(2,1)S(1)} %get-tuple-element.93.refs_0_, s32[1]{0:T(128)} %get-tuple-element.72.refs_0_.refs_1_, bf16[32,8320]{1,0:T(8,128)(2,1)S(1)} %collective-permute-done.11.refs_2_.refs_8_, ...), custom_call_target="tpu_custom_call" | custom-call | flops 1000000 | bytes 1000 | tf_op jit(solution)/shard_map/rows_backward/pallas_call | solution.py:269
  91.2 10.2 %weights_backward.1 = (f32[384,4096]{1,0:T(8,128)}, f32[384,4096]{1,0:T(8,128)}, f32[384,4096]{1,0:T(8,128)}, f32[8,128]{1,0:T(8,128)S(1)}) custom-call(bf16[64,1152]{1,0:T(8,128)(2,1)S(1)} %get-tuple-element.94.refs_0_.refs_18_, s32[1]{0:T(128)} %get-tuple-element.72.refs_0_.refs_1_, bf16[32,8320]{1,0:T(8,128)(2,1)S(1)} %copy-done.6, ...), custom_call_target="tpu_custom_call" | custom-call | flops 1000000 | bytes 1000 | tf_op jit(solution)/shard_map/weights_backward/pallas_call | solution.py:451
  101.5 1.5 %collective-permute-done.17.refs_4_ = bf16[128,2176]{1,0:T(8,128)(2,1)S(1)} collective-permute-done((bf16[128,2176]{1,0:T(8,128)(2,1)S(1)}, bf16[128,2176]{1,0:T(8,128)(2,1)S(1)}, u32[]{:S(2)}, u32[]{:S(2)}) %collective-permute-start.17) | collective-permute-done | bytes 557088 | tf_op jit(solution)/shard_map/ppermute | solution.py:541
  103.3 1.7 %collective-permute-start.25 = (bf16[128,1152]{1,0:T(8,128)(2,1)S(1)}, bf16[128,1152]{1,0:T(8,128)(2,1)S(1)}, u32[]{:S(2)}, u32[]{:S(2)}) collective-permute-start(bf16[128,1152]{1,0:T(8,128)(2,1)S(1)} %get-tuple-element.100.refs_0_), channel_id=1, source_target_pairs={{0,2},{1,3},{2,0},{3,1},{4,6},{5,7},{6,4},{7,5},{8,10},{9,11},{10,... | collective-permute-start | bytes 884744 | tf_op jit(solution)/shard_map/ppermute | solution.py:541
  105.0 8.1 %collective-permute-done.18.refs_2_ = bf16[64,2176]{1,0:T(8,128)(2,1)S(1)} collective-permute-done((bf16[64,2176]{1,0:T(8,128)(2,1)S(1)}, bf16[64,2176]{1,0:T(8,128)(2,1)S(1)}, u32[]{:S(2)}, u32[]{:S(2)}) %collective-permute-start.18) | collective-permute-done | bytes 278560 | tf_op jit(solution)/shard_map/ppermute | solution.py:541
  114.3 3.4 %collective-permute-start.22 = (f32[8,128]{1,0:T(8,128)S(1)}, f32[8,128]{1,0:T(8,128)S(1)}, u32[]{:S(2)}, u32[]{:S(2)}) collective-permute-start(f32[8,128]{1,0:T(8,128)S(1)} %get-tuple-element.108.refs_0_.refs_4_.refs_1_), channel_id=1, source_target_pairs={{0,1},{1,0},{2,3},{3,2},{4,5},{5,4},{6,7},{7,6},{8,9},{9,8},{10,11... | collective-permute-start | bytes 12296 | tf_op jit(solution)/shard_map/ppermute | solution.py:541
  118.9 1.3 collective-permute-start.20
  121.3 1.2 collective-permute-start.31
  123.6 1.9 %collective-permute-done.21.refs_3_.refs_21_ = bf16[32,1152]{1,0:T(8,128)(2,1)S(1)} collective-permute-done((bf16[32,1152]{1,0:T(8,128)(2,1)S(1)}, bf16[32,1152]{1,0:T(8,128)(2,1)S(1)}, u32[]{:S(2)}, u32[]{:S(2)}) %collective-permute-start.21) | collective-permute-done | bytes 73760 | tf_op jit(solution)/shard_map/ppermute | solution.py:541
  129.0 1.9 %collective-permute-start.32 = (bf16[32,1152]{1,0:T(8,128)(2,1)S(1)}, bf16[32,1152]{1,0:T(8,128)(2,1)S(1)}, u32[]{:S(2)}, u32[]{:S(2)}) collective-permute-start(bf16[32,1152]{1,0:T(8,128)(2,1)S(1)} %get-tuple-element.119), channel_id=1, source_target_pairs={{0,24},{4,28},{8,16},{12,20},{16,8},{20,12},{24,0},{28,4},{1,25},{... | collective-permute-start | bytes 221192 | tf_op jit(solution)/shard_map/ppermute | solution.py:541
  130.9 2.2 %collective-permute-start.30 = (bf16[32,1152]{1,0:T(8,128)(2,1)S(1)}, bf16[32,1152]{1,0:T(8,128)(2,1)S(1)}, u32[]{:S(2)}, u32[]{:S(2)}) collective-permute-start(bf16[32,1152]{1,0:T(8,128)(2,1)S(1)} %get-tuple-element.116.refs_0_), channel_id=1, source_target_pairs={{0,20},{4,16},{8,28},{12,24},{16,4},{20,0},{24,12},{28,8},{1,21},{... | collective-permute-start | bytes 221192 | tf_op jit(solution)/shard_map/ppermute | solution.py:541
  133.1 1.2 collective-permute-done.32.refs_16_
  134.3 1.7 %collective-permute-done.33.refs_17_ = bf16[32,1152]{1,0:T(8,128)(2,1)S(1)} collective-permute-done((bf16[32,1152]{1,0:T(8,128)(2,1)S(1)}, bf16[32,1152]{1,0:T(8,128)(2,1)S(1)}, u32[]{:S(2)}, u32[]{:S(2)}) %collective-permute-start.33) | collective-permute-done | bytes 73760 | tf_op jit(solution)/shard_map/ppermute | solution.py:541
  136.0 1.4 collective-permute-done.30.refs_15_
  137.4 1.7 %home.1 = (bf16[256,1024]{1,0:T(8,128)(2,1)}, f32[8,256]{1,0:T(8,128)}, f32[1]{0:T(128)}) custom-call(f32[8,256]{1,0:T(8,128)S(1)} %bitcast.23, s32[1,256]{1,0:T(1,128)S(1)} %bitcast.25, bf16[32,8320]{1,0:T(8,128)(2,1)S(1)} %copy-done.6, bf16[160,8320]{1,0:T(8,128)(2,1)S(1)} %collective-permute-done.refs_2_.refs_5_.refs_3_.refs_13_, ...), custom_call_target="tpu_custom_call" | custom-call | flops 1000000 | bytes 1000 | tf_op jit(solution)/shard_map/home/pallas_call | solution.py:517
  (83 shorter events, 20.0 us)
Async XLA Ops:
  7.5 5.3 %collective-permute-start = (bf16[160,8320]{1,0:T(8,128)(2,1)}, bf16[160,8320]{1,0:T(8,128)(2,1)S(1)}, u32[]{:S(2)}, u32[]{:S(2)}) collective-permute-start(bf16[160,8320]{1,0:T(8,128)(2,1)} %get-tuple-element.68), channel_id=1, source_target_pairs={{0,4},{4,0},{8,12},{12,8},{16,20},{20,16},{24,28},{28,24},{1,5},{5... | collective-permute-start | bytes 7987208 | tf_op jit(solution)/shard_map/ppermute | solution.py:541
  8.0 15.1 %collective-permute-start.3 = (bf16[32,4224]{1,0:T(8,128)(2,1)}, bf16[32,4224]{1,0:T(8,128)(2,1)S(1)}, u32[]{:S(2)}, u32[]{:S(2)}) collective-permute-start(bf16[32,4224]{1,0:T(8,128)(2,1)} %get-tuple-element.71), channel_id=1, source_target_pairs={{0,24},{4,28},{8,16},{12,20},{16,8},{20,12},{24,0},{28,4},{1,25},{... | collective-permute-start | bytes 811016 | tf_op jit(solution)/shard_map/ppermute | solution.py:541
  11.5 13.1 %collective-permute-start.2 = (bf16[32,4224]{1,0:T(8,128)(2,1)}, bf16[32,4224]{1,0:T(8,128)(2,1)S(1)}, u32[]{:S(2)}, u32[]{:S(2)}) collective-permute-start(bf16[32,4224]{1,0:T(8,128)(2,1)} %get-tuple-element.71), channel_id=1, source_target_pairs={{0,16},{4,20},{8,24},{12,28},{16,0},{20,4},{24,8},{28,12},{1,17},{... | collective-permute-start | bytes 811016 | tf_op jit(solution)/shard_map/ppermute | solution.py:541
  12.0 12.9 %collective-permute-start.1 = (bf16[32,4224]{1,0:T(8,128)(2,1)}, bf16[32,4224]{1,0:T(8,128)(2,1)S(1)}, u32[]{:S(2)}, u32[]{:S(2)}) collective-permute-start(bf16[32,4224]{1,0:T(8,128)(2,1)} %get-tuple-element.71), channel_id=1, source_target_pairs={{0,8},{4,12},{8,0},{12,4},{16,24},{20,28},{24,16},{28,20},{1,9},{5... | collective-permute-start | bytes 811016 | tf_op jit(solution)/shard_map/ppermute | solution.py:541
  24.9 9.6 %collective-permute-start.6 = (bf16[64,2176]{1,0:T(8,128)(2,1)S(1)}, bf16[64,2176]{1,0:T(8,128)(2,1)S(1)}, u32[]{:S(2)}, u32[]{:S(2)}) collective-permute-start(bf16[64,2176]{1,0:T(8,128)(2,1)S(1)} %get-tuple-element.80), channel_id=1, source_target_pairs={{0,1},{1,0},{2,3},{3,2},{4,5},{5,4},{6,7},{7,6},{8,9},{9,8},{10,11... | collective-permute-start | bytes 835592 | tf_op jit(solution)/shard_map/ppermute | solution.py:541
  26.6 24.0 %collective-permute-start.7 = (bf16[96,4224]{1,0:T(8,128)(2,1)S(1)}, bf16[96,4224]{1,0:T(8,128)(2,1)S(1)}, u32[]{:S(2)}, u32[]{:S(2)}) collective-permute-start(bf16[96,4224]{1,0:T(8,128)(2,1)S(1)} %constant_dynamic-update-slice_fusion.refs_3_.refs_11_), channel_id=1, source_target_pairs={{0,1},{1,0},{2,3},{3,2},{4,5},{5,4},{6,7},{7,6},{8,9},{9,8},{10,11... | collective-permute-start | bytes 2433032 | tf_op jit(solution)/shard_map/ppermute | solution.py:541
  28.2 36.5 %collective-permute-start.4 = (bf16[96,8320]{1,0:T(8,128)(2,1)S(1)}, bf16[96,8320]{1,0:T(8,128)(2,1)S(1)}, u32[]{:S(2)}, u32[]{:S(2)}) collective-permute-start(bf16[96,8320]{1,0:T(8,128)(2,1)S(1)} %get-tuple-element.77), channel_id=1, source_target_pairs={{0,8},{4,12},{8,0},{12,4},{16,24},{20,28},{24,16},{28,20},{1,9},{5... | collective-permute-start | bytes 4792328 | tf_op jit(solution)/shard_map/ppermute | solution.py:541
  29.7 36.2 %collective-permute-start.5 = (bf16[96,8320]{1,0:T(8,128)(2,1)S(1)}, bf16[96,8320]{1,0:T(8,128)(2,1)S(1)}, u32[]{:S(2)}, u32[]{:S(2)}) collective-permute-start(bf16[96,8320]{1,0:T(8,128)(2,1)S(1)} %get-tuple-element.78), channel_id=1, source_target_pairs={{0,16},{4,20},{8,24},{12,28},{16,0},{20,4},{24,8},{28,12},{1,17},{... | collective-permute-start | bytes 4792328 | tf_op jit(solution)/shard_map/ppermute | solution.py:541
  30.9 19.8 %collective-permute-start.8 = (bf16[96,4224]{1,0:T(8,128)(2,1)S(1)}, bf16[96,4224]{1,0:T(8,128)(2,1)S(1)}, u32[]{:S(2)}, u32[]{:S(2)}) collective-permute-start(bf16[96,4224]{1,0:T(8,128)(2,1)S(1)} %constant_dynamic-update-slice_fusion.refs_3_.refs_11_), channel_id=1, source_target_pairs={{0,4},{4,0},{8,12},{12,8},{16,20},{20,16},{24,28},{28,24},{1,5},{5... | collective-permute-start | bytes 2433032 | tf_op jit(solution)/shard_map/ppermute | solution.py:541
  54.1 11.9 %collective-permute-start.10 = (bf16[128,2176]{1,0:T(8,128)(2,1)S(1)}, bf16[128,2176]{1,0:T(8,128)(2,1)S(1)}, u32[]{:S(2)}, u32[]{:S(2)}) collective-permute-start(bf16[128,2176]{1,0:T(8,128)(2,1)S(1)} %get-tuple-element.86), channel_id=1, source_target_pairs={{0,4},{4,0},{8,12},{12,8},{16,20},{20,16},{24,28},{28,24},{1,5},{5... | collective-permute-start | bytes 1671176 | tf_op jit(solution)/shard_map/ppermute | solution.py:541
  66.0 9.9 %collective-permute-start.13 = (bf16[128,2176]{1,0:T(8,128)(2,1)S(1)}, bf16[128,2176]{1,0:T(8,128)(2,1)S(1)}, u32[]{:S(2)}, u32[]{:S(2)}) collective-permute-start(bf16[128,2176]{1,0:T(8,128)(2,1)S(1)} %get-tuple-element.91), channel_id=1, source_target_pairs={{0,4},{4,0},{8,12},{12,8},{16,20},{20,16},{24,28},{28,24},{1,5},{5... | collective-permute-start | bytes 1671176 | tf_op jit(solution)/shard_map/ppermute | solution.py:541
  66.1 15.5 %collective-permute-start.14 = (bf16[128,2176]{1,0:T(8,128)(2,1)S(1)}, bf16[128,2176]{1,0:T(8,128)(2,1)S(1)}, u32[]{:S(2)}, u32[]{:S(2)}) collective-permute-start(bf16[128,2176]{1,0:T(8,128)(2,1)S(1)} %merge.1.refs_0_), channel_id=1, source_target_pairs={{0,1},{1,0},{2,3},{3,2},{4,5},{5,4},{6,7},{7,6},{8,9},{9,8},{10,11... | collective-permute-start | bytes 1671176 | tf_op jit(solution)/shard_map/ppermute | solution.py:541
  66.9 18.1 %collective-permute-start.11 = (bf16[32,8320]{1,0:T(8,128)(2,1)S(1)}, bf16[32,8320]{1,0:T(8,128)(2,1)S(1)}, u32[]{:S(2)}, u32[]{:S(2)}) collective-permute-start(bf16[32,8320]{1,0:T(8,128)(2,1)S(1)} %slice.20), channel_id=1, source_target_pairs={{0,16},{4,20},{8,24},{12,28},{16,0},{20,4},{24,8},{28,12},{1,17},{... | collective-permute-start | bytes 1597448 | tf_op jit(solution)/shard_map/ppermute | solution.py:541
  68.2 16.8 %collective-permute-start.12 = (bf16[32,8320]{1,0:T(8,128)(2,1)S(1)}, bf16[32,8320]{1,0:T(8,128)(2,1)S(1)}, u32[]{:S(2)}, u32[]{:S(2)}) collective-permute-start(bf16[32,8320]{1,0:T(8,128)(2,1)S(1)} %slice.21), channel_id=1, source_target_pairs={{0,8},{4,12},{8,0},{12,4},{16,24},{20,28},{24,16},{28,20},{1,9},{5... | collective-permute-start | bytes 1597448 | tf_op jit(solution)/shard_map/ppermute | solution.py:541
  74.5 28.6 %collective-permute-start.17 = (bf16[128,2176]{1,0:T(8,128)(2,1)S(1)}, bf16[128,2176]{1,0:T(8,128)(2,1)S(1)}, u32[]{:S(2)}, u32[]{:S(2)}) collective-permute-start(bf16[128,2176]{1,0:T(8,128)(2,1)S(1)} %get-tuple-element.99), channel_id=1, source_target_pairs={{0,1},{1,0},{2,3},{3,2},{4,5},{5,4},{6,7},{7,6},{8,9},{9,8},{10,11... | collective-permute-start | bytes 1671176 | tf_op jit(solution)/shard_map/ppermute | solution.py:541
  82.1 21.0 %collective-permute-start.15 = (bf16[128,1152]{1,0:T(8,128)(2,1)S(1)}, bf16[128,1152]{1,0:T(8,128)(2,1)S(1)}, u32[]{:S(2)}, u32[]{:S(2)}) collective-permute-start(bf16[128,1152]{1,0:T(8,128)(2,1)S(1)} %get-tuple-element.93.refs_0_), channel_id=1, source_target_pairs={{0,2},{1,3},{2,0},{3,1},{4,6},{5,7},{6,4},{7,5},{8,10},{9,11},{10,... | collective-permute-start | bytes 884744 | tf_op jit(solution)/shard_map/ppermute | solution.py:541
  84.7 16.8 %collective-permute-start.16 = (bf16[64,1152]{1,0:T(8,128)(2,1)S(1)}, bf16[64,1152]{1,0:T(8,128)(2,1)S(1)}, u32[]{:S(2)}, u32[]{:S(2)}) collective-permute-start(bf16[64,1152]{1,0:T(8,128)(2,1)S(1)} %get-tuple-element.97.refs_0_), channel_id=1, source_target_pairs={{0,2},{1,3},{2,0},{3,1},{4,6},{5,7},{6,4},{7,5},{8,10},{9,11},{10,... | collective-permute-start | bytes 442376 | tf_op jit(solution)/shard_map/ppermute | solution.py:541
  90.5 22.6 %collective-permute-start.18 = (bf16[64,2176]{1,0:T(8,128)(2,1)S(1)}, bf16[64,2176]{1,0:T(8,128)(2,1)S(1)}, u32[]{:S(2)}, u32[]{:S(2)}) collective-permute-start(bf16[64,2176]{1,0:T(8,128)(2,1)S(1)} %get-tuple-element.102), channel_id=1, source_target_pairs={{0,1},{1,0},{2,3},{3,2},{4,5},{5,4},{6,7},{7,6},{8,9},{9,8},{10,11... | collective-permute-start | bytes 835592 | tf_op jit(solution)/shard_map/ppermute | solution.py:541
  103.3 22.2 %collective-permute-start.25 = (bf16[128,1152]{1,0:T(8,128)(2,1)S(1)}, bf16[128,1152]{1,0:T(8,128)(2,1)S(1)}, u32[]{:S(2)}, u32[]{:S(2)}) collective-permute-start(bf16[128,1152]{1,0:T(8,128)(2,1)S(1)} %get-tuple-element.100.refs_0_), channel_id=1, source_target_pairs={{0,2},{1,3},{2,0},{3,1},{4,6},{5,7},{6,4},{7,5},{8,10},{9,11},{10,... | collective-permute-start | bytes 884744 | tf_op jit(solution)/shard_map/ppermute | solution.py:541
  113.2 5.6 %collective-permute-start.24 = (f32[8,128]{1,0:T(8,128)S(1)}, f32[8,128]{1,0:T(8,128)S(1)}, u32[]{:S(2)}, u32[]{:S(2)}) collective-permute-start(f32[8,128]{1,0:T(8,128)S(1)} %get-tuple-element.108.refs_0_.refs_4_.refs_1_), channel_id=1, source_target_pairs={{0,3},{1,2},{2,1},{3,0},{4,7},{5,6},{6,5},{7,4},{8,11},{9,10},{10,... | collective-permute-start | bytes 12296 | tf_op jit(solution)/shard_map/ppermute | solution.py:541
  114.2 6.0 %collective-permute-start.23 = (f32[8,128]{1,0:T(8,128)S(1)}, f32[8,128]{1,0:T(8,128)S(1)}, u32[]{:S(2)}, u32[]{:S(2)}) collective-permute-start(f32[8,128]{1,0:T(8,128)S(1)} %get-tuple-element.108.refs_0_.refs_4_.refs_1_), channel_id=1, source_target_pairs={{0,2},{1,3},{2,0},{3,1},{4,6},{5,7},{6,4},{7,5},{8,10},{9,11},{10,... | collective-permute-start | bytes 12296 | tf_op jit(solution)/shard_map/ppermute | solution.py:541
  114.3 7.0 %collective-permute-start.22 = (f32[8,128]{1,0:T(8,128)S(1)}, f32[8,128]{1,0:T(8,128)S(1)}, u32[]{:S(2)}, u32[]{:S(2)}) collective-permute-start(f32[8,128]{1,0:T(8,128)S(1)} %get-tuple-element.108.refs_0_.refs_4_.refs_1_), channel_id=1, source_target_pairs={{0,1},{1,0},{2,3},{3,2},{4,5},{5,4},{6,7},{7,6},{8,9},{9,8},{10,11... | collective-permute-start | bytes 12296 | tf_op jit(solution)/shard_map/ppermute | solution.py:541
  117.8 4.8 %collective-permute-start.19 = (bf16[32,1152]{1,0:T(8,128)(2,1)S(1)}, bf16[32,1152]{1,0:T(8,128)(2,1)S(1)}, u32[]{:S(2)}, u32[]{:S(2)}) collective-permute-start(bf16[32,1152]{1,0:T(8,128)(2,1)S(1)} %get-tuple-element.106), channel_id=1, source_target_pairs={{0,8},{4,12},{8,0},{12,4},{16,24},{20,28},{24,16},{28,20},{1,9},{5... | collective-permute-start | bytes 221192 | tf_op jit(solution)/shard_map/ppermute | solution.py:541
  120.2 5.3 %collective-permute-start.21 = (bf16[32,1152]{1,0:T(8,128)(2,1)S(1)}, bf16[32,1152]{1,0:T(8,128)(2,1)S(1)}, u32[]{:S(2)}, u32[]{:S(2)}) collective-permute-start(bf16[32,1152]{1,0:T(8,128)(2,1)S(1)} %get-tuple-element.105.refs_0_), channel_id=1, source_target_pairs={{0,24},{4,28},{8,16},{12,20},{16,8},{20,12},{24,0},{28,4},{1,25},{... | collective-permute-start | bytes 221192 | tf_op jit(solution)/shard_map/ppermute | solution.py:541
  121.3 7.6 %collective-permute-start.31 = (bf16[64,1152]{1,0:T(8,128)(2,1)S(1)}, bf16[64,1152]{1,0:T(8,128)(2,1)S(1)}, u32[]{:S(2)}, u32[]{:S(2)}) collective-permute-start(bf16[64,1152]{1,0:T(8,128)(2,1)S(1)} %get-tuple-element.118.refs_0_), channel_id=1, source_target_pairs={{0,2},{1,3},{2,0},{3,1},{4,6},{5,7},{6,4},{7,5},{8,10},{9,11},{10,... | collective-permute-start | bytes 442376 | tf_op jit(solution)/shard_map/ppermute | solution.py:541
  125.7 5.2 %collective-permute-start.26 = (bf16[32,1152]{1,0:T(8,128)(2,1)S(1)}, bf16[32,1152]{1,0:T(8,128)(2,1)S(1)}, u32[]{:S(2)}, u32[]{:S(2)}) collective-permute-start(bf16[32,1152]{1,0:T(8,128)(2,1)S(1)} %get-tuple-element.112), channel_id=1, source_target_pairs={{0,4},{4,0},{8,12},{12,8},{16,20},{20,16},{24,28},{28,24},{1,5},{5... | collective-permute-start | bytes 221192 | tf_op jit(solution)/shard_map/ppermute | solution.py:541
  125.8 5.2 %collective-permute-start.27 = (bf16[32,1152]{1,0:T(8,128)(2,1)S(1)}, bf16[32,1152]{1,0:T(8,128)(2,1)S(1)}, u32[]{:S(2)}, u32[]{:S(2)}) collective-permute-start(bf16[32,1152]{1,0:T(8,128)(2,1)S(1)} %get-tuple-element.113), channel_id=1, source_target_pairs={{0,8},{4,12},{8,0},{12,4},{16,24},{20,28},{24,16},{28,20},{1,9},{5... | collective-permute-start | bytes 221192 | tf_op jit(solution)/shard_map/ppermute | solution.py:541
  126.9 6.3 %collective-permute-start.28 = (bf16[32,1152]{1,0:T(8,128)(2,1)S(1)}, bf16[32,1152]{1,0:T(8,128)(2,1)S(1)}, u32[]{:S(2)}, u32[]{:S(2)}) collective-permute-start(bf16[32,1152]{1,0:T(8,128)(2,1)S(1)} %get-tuple-element.114), channel_id=1, source_target_pairs={{0,12},{4,8},{8,4},{12,0},{16,28},{20,24},{24,20},{28,16},{1,13},{... | collective-permute-start | bytes 221192 | tf_op jit(solution)/shard_map/ppermute | solution.py:541
  127.6 5.5 %collective-permute-start.29 = (bf16[32,1152]{1,0:T(8,128)(2,1)S(1)}, bf16[32,1152]{1,0:T(8,128)(2,1)S(1)}, u32[]{:S(2)}, u32[]{:S(2)}) collective-permute-start(bf16[32,1152]{1,0:T(8,128)(2,1)S(1)} %get-tuple-element.115), channel_id=1, source_target_pairs={{0,16},{4,20},{8,24},{12,28},{16,0},{20,4},{24,8},{28,12},{1,17},{... | collective-permute-start | bytes 221192 | tf_op jit(solution)/shard_map/ppermute | solution.py:541
  129.0 5.3 %collective-permute-start.32 = (bf16[32,1152]{1,0:T(8,128)(2,1)S(1)}, bf16[32,1152]{1,0:T(8,128)(2,1)S(1)}, u32[]{:S(2)}, u32[]{:S(2)}) collective-permute-start(bf16[32,1152]{1,0:T(8,128)(2,1)S(1)} %get-tuple-element.119), channel_id=1, source_target_pairs={{0,24},{4,28},{8,16},{12,20},{16,8},{20,12},{24,0},{28,4},{1,25},{... | collective-permute-start | bytes 221192 | tf_op jit(solution)/shard_map/ppermute | solution.py:541
  130.9 5.1 %collective-permute-start.33 = (bf16[32,1152]{1,0:T(8,128)(2,1)S(1)}, bf16[32,1152]{1,0:T(8,128)(2,1)S(1)}, u32[]{:S(2)}, u32[]{:S(2)}) collective-permute-start(bf16[32,1152]{1,0:T(8,128)(2,1)S(1)} %get-tuple-element.120), channel_id=1, source_target_pairs={{0,28},{4,24},{8,20},{12,16},{16,12},{20,8},{24,4},{28,0},{1,29},{... | collective-permute-start | bytes 221192 | tf_op jit(solution)/shard_map/ppermute | solution.py:541
  130.9 6.5 %collective-permute-start.30 = (bf16[32,1152]{1,0:T(8,128)(2,1)S(1)}, bf16[32,1152]{1,0:T(8,128)(2,1)S(1)}, u32[]{:S(2)}, u32[]{:S(2)}) collective-permute-start(bf16[32,1152]{1,0:T(8,128)(2,1)S(1)} %get-tuple-element.116.refs_0_), channel_id=1, source_target_pairs={{0,20},{4,16},{8,28},{12,24},{16,4},{20,0},{24,12},{28,8},{1,21},{... | collective-permute-start | bytes 221192 | tf_op jit(solution)/shard_map/ppermute | solution.py:541
  (14 other events, 179.7 us)

commit v3 on v2

--- a/solution.py
+++ b/solution.py
@@ -655,14 +655,14 @@
     )
     wait_for(busy[-1], first[-1])
     second = middle(second)
+    over_back = step(last, [], [busy], [evens], evens, cut, cap)
+    over_back = [piece if m == 0 else swap(piece, "expert", m) for m, piece in zip(evens, over_back)]
+    wait_for(*over_back[1:])
     for bit in bits[1:]:
         kept, sent = step(fold, third, cut)
         (squares,), (sent,) = after([squares], [sent])
         third = turn((kept, sent), bit)
     squares = [squares] + [swap(squares, "dp", m) for m in range(1, n_dp)]
-    over_back = step(last, [], [busy], [evens], evens, cut, cap)
-    over_back = [piece if m == 0 else swap(piece, "expert", m) for m, piece in zip(evens, over_back)]
-    wait_for(*over_back[1:])
     back = {}
     for masks, given, where in (
         (chunks[0] + chunks[1], [first, second], chunks[:2]),

time: 140 us -> 140 us (level)
  transfers between devices with their start and end apart: 34 -> 34, of which waited for: 18 -> 16; matrix products, arithmetic and copies ran while one was open for 0% -> 0% of each run, Pallas kernels for 21% -> 21%
where the time goes in v3:
time: 140 us; the launch traced here: 139 us
  waiting for transfers between devices  59.9 us (43%)
  Pallas kernels  37.6 us (27%)
  starting transfers between devices  34.7 us (25%)
  local copies, waits for them, and re-layouts  5.77 us (4%)
    ppermute x34, waiting for transfers between devices, swap(): return lax.ppermute(value, axis, [(i, i ^ mask) for i in range(size)])  59.9 us
    ppermute x34, starting transfers between devices, swap(): return lax.ppermute(value, axis, [(i, i ^ mask) for i in range(size)])  34.7 us
    pallas_call x4, Pallas kernels, rows_backward(): call(functools.partial(rows_body, ranges, width, n_dp, guarded), 'rows_ba...  17.5 us
    pallas_call x1, Pallas kernels, weights_backward(): call(functools.partial(weights_body, ranges, len(cold), len(acts), width,...  10.2 us
    pallas_call x1, Pallas kernels, dispatch(): call(functools.partial(dispatch_body, plan, experts, cap, width), 'dispat...  6.84 us
    unnamed x26, local copies, waits for them, and re-layouts  5.56 us
  transfers between devices with their start and end apart: 34, of which 16 were waited for; matrix products, arithmetic and copies ran while one was open for 0% of the time, Pallas kernels for 21%

profile of v3, /device:TPU:0, one launch (start us, length us, event | category | flops | bytes accessed | tf_op | source)
XLA Modules:
  0.0 139.4 jit_solution(12489980916906531880)
XLA Ops:
  0.6 6.8 %dispatch.1 = (bf16[32,8320]{1,0:T(8,128)(2,1)}, bf16[160,8320]{1,0:T(8,128)(2,1)}, bf16[32,8320]{1,0:T(8,128)(2,1)}, bf16[64,8320]{1,0:T(8,128)(2,1)}, bf16[32,...) custom-call(bf16[256,4096]{1,0:T(8,128)(2,1)} %refs_0_.1, bf16[256,4096]{1,0:T(8,128)(2,1)} %refs_1_.1, ...), custom_call_target="tpu_custom_call" | custom-call | flops 6000000000 | bytes 1000 | tf_op jit(solution)/shard_map/dispatch/pallas_call | solution.py:126
  8.0 3.5 %collective-permute-start.3 = (bf16[32,4224]{1,0:T(8,128)(2,1)}, bf16[32,4224]{1,0:T(8,128)(2,1)S(1)}, u32[]{:S(2)}, u32[]{:S(2)}) collective-permute-start(bf16[32,4224]{1,0:T(8,128)(2,1)} %get-tuple-element.71), channel_id=1, source_target_pairs={{0,24},{4,28},{8,16},{12,20},{16,8},{20,12},{24,0},{28,4},{1,25},{... | collective-permute-start | bytes 811016 | tf_op jit(solution)/shard_map/ppermute | solution.py:541
  12.8 1.9 %copy-done.1 = bf16[1,384,4096]{2,1,0:T(8,128)(2,1)S(1)} copy-done((bf16[1,384,4096]{2,1,0:T(8,128)(2,1)S(1)}, bf16[1,384,4096]{2,1,0:T(8,128)(2,1)}, u32[]{:S(2)}) %copy-start.1) | copy-done | bytes 3145752
  14.7 1.9 %copy-done.3 = bf16[1,384,4096]{2,1,0:T(8,128)(2,1)S(1)} copy-done((bf16[1,384,4096]{2,1,0:T(8,128)(2,1)S(1)}, bf16[1,384,4096]{2,1,0:T(8,128)(2,1)}, u32[]{:S(2)}) %copy-start.3) | copy-done | bytes 3145752
  17.6 5.4 %rows_backward.4 = (bf16[64,2176]{1,0:T(8,128)(2,1)S(1)}, bf16[64,2176]{1,0:T(8,128)(2,1)S(1)}, bf16[64,1152]{1,0:T(8,128)(2,1)S(1)}) custom-call(s32[1]{0:T(128)} %get-tuple-element.72.refs_0_.refs_1_, bf16[32,8320]{1,0:T(8,128)(2,1)S(1)} %copy-done.5, bf16[160,8320]{1,0:T(8,128)(2,1)S(1)} %collective-permute-done.refs_2_.refs_5_.refs_3_.refs_13_, ...), custom_call_target="tpu_custom_call" | custom-call | flops 1000000 | bytes 1000 | tf_op jit(solution)/shard_map/rows_backward/pallas_call | solution.py:269
  23.1 1.5 %collective-permute-done.2 = bf16[32,4224]{1,0:T(8,128)(2,1)S(1)} collective-permute-done((bf16[32,4224]{1,0:T(8,128)(2,1)}, bf16[32,4224]{1,0:T(8,128)(2,1)S(1)}, u32[]{:S(2)}, u32[]{:S(2)}) %collective-permute-start.2) | collective-permute-done | bytes 270368 | tf_op jit(solution)/shard_map/ppermute | solution.py:541
  24.9 1.6 %collective-permute-start.6 = (bf16[64,2176]{1,0:T(8,128)(2,1)S(1)}, bf16[64,2176]{1,0:T(8,128)(2,1)S(1)}, u32[]{:S(2)}, u32[]{:S(2)}) collective-permute-start(bf16[64,2176]{1,0:T(8,128)(2,1)S(1)} %get-tuple-element.80), channel_id=1, source_target_pairs={{0,1},{1,0},{2,3},{3,2},{4,5},{5,4},{6,7},{7,6},{8,9},{9,8},{10,11... | collective-permute-start | bytes 835592 | tf_op jit(solution)/shard_map/ppermute | solution.py:541
  28.2 1.5 %collective-permute-start.4 = (bf16[96,8320]{1,0:T(8,128)(2,1)S(1)}, bf16[96,8320]{1,0:T(8,128)(2,1)S(1)}, u32[]{:S(2)}, u32[]{:S(2)}) collective-permute-start(bf16[96,8320]{1,0:T(8,128)(2,1)S(1)} %get-tuple-element.77), channel_id=1, source_target_pairs={{0,8},{4,12},{8,0},{12,4},{16,24},{20,28},{24,16},{28,20},{1,9},{5... | collective-permute-start | bytes 4792328 | tf_op jit(solution)/shard_map/ppermute | solution.py:541
  30.9 3.6 %collective-permute-done.6.refs_2_ = bf16[64,2176]{1,0:T(8,128)(2,1)S(1)} collective-permute-done((bf16[64,2176]{1,0:T(8,128)(2,1)S(1)}, bf16[64,2176]{1,0:T(8,128)(2,1)S(1)}, u32[]{:S(2)}, u32[]{:S(2)}) %collective-permute-start.6) | collective-permute-done | bytes 278560 | tf_op jit(solution)/shard_map/ppermute | solution.py:541
  34.6 16.1 %collective-permute-done.7.refs_4_.refs_12_ = bf16[96,4224]{1,0:T(8,128)(2,1)S(1)} collective-permute-done((bf16[96,4224]{1,0:T(8,128)(2,1)S(1)}, bf16[96,4224]{1,0:T(8,128)(2,1)S(1)}, u32[]{:S(2)}, u32[]{:S(2)}) %collective-permute-start.7) | collective-permute-done | bytes 811040 | tf_op jit(solution)/shard_map/ppermute | solution.py:541
  50.6 2.3 %collective-permute-done.9.refs_7_.refs_15_ = bf16[96,4224]{1,0:T(8,128)(2,1)S(1)} collective-permute-done((bf16[96,4224]{1,0:T(8,128)(2,1)S(1)}, bf16[96,4224]{1,0:T(8,128)(2,1)S(1)}, u32[]{:S(2)}, u32[]{:S(2)}) %collective-permute-start.9) | collective-permute-done | bytes 811040 | tf_op jit(solution)/shard_map/ppermute | solution.py:541
  54.3 10.4 %collective-permute-done.4.refs_2_.refs_4_.refs_6_.refs_5_ = bf16[96,8320]{1,0:T(8,128)(2,1)S(1)} collective-permute-done((bf16[96,8320]{1,0:T(8,128)(2,1)S(1)}, bf16[96,8320]{1,0:T(8,128)(2,1)S(1)}, u32[]{:S(2)}, u32[]{:S(2)}) %collective-permute-start.4) | collective-permute-done | bytes 1597472 | tf_op jit(solution)/shard_map/ppermute | solution.py:541
  66.9 1.3 collective-permute-start.11
  69.0 5.5 %rows_backward.6 = (bf16[128,2176]{1,0:T(8,128)(2,1)S(1)}, bf16[128,2176]{1,0:T(8,128)(2,1)S(1)}, bf16[128,1152]{1,0:T(8,128)(2,1)S(1)}) custom-call(bf16[128,2176]{1,0:T(8,128)(2,1)S(1)} %merge.1.refs_0_, s32[1]{0:T(128)} %get-tuple-element.72.refs_0_.refs_1_, bf16[96,8320]{1,0:T(8,128)(2,1)S(1)} %collective-permute-done.4.refs_2_.refs_4_.refs_6_.refs_5_, ...), custom_call_target="tpu_custom_call" | custom-call | flops 1000000 | bytes 1000 | tf_op jit(solution)/shard_map/rows_backward/pallas_call | solution.py:269
  74.5 1.4 collective-permute-start.17
  75.9 5.7 %collective-permute-done.14.refs_3_ = bf16[128,2176]{1,0:T(8,128)(2,1)S(1)} collective-permute-done((bf16[128,2176]{1,0:T(8,128)(2,1)S(1)}, bf16[128,2176]{1,0:T(8,128)(2,1)S(1)}, u32[]{:S(2)}, u32[]{:S(2)}) %collective-permute-start.14) | collective-permute-done | bytes 557088 | tf_op jit(solution)/shard_map/ppermute | solution.py:541
  82.1 2.7 %collective-permute-start.15 = (bf16[128,1152]{1,0:T(8,128)(2,1)S(1)}, bf16[128,1152]{1,0:T(8,128)(2,1)S(1)}, u32[]{:S(2)}, u32[]{:S(2)}) collective-permute-start(bf16[128,1152]{1,0:T(8,128)(2,1)S(1)} %get-tuple-element.93.refs_0_), channel_id=1, source_target_pairs={{0,2},{1,3},{2,0},{3,1},{4,6},{5,7},{6,4},{7,5},{8,10},{9,11},{10,... | collective-permute-start | bytes 884744 | tf_op jit(solution)/shard_map/ppermute | solution.py:541
  85.1 5.4 %rows_backward.7 = (bf16[64,2176]{1,0:T(8,128)(2,1)S(1)}, bf16[64,2176]{1,0:T(8,128)(2,1)S(1)}, bf16[64,1152]{1,0:T(8,128)(2,1)S(1)}) custom-call(bf16[128,1152]{1,0:T(8,128)(2,1)S(1)} %get-tuple-element.93.refs_0_, s32[1]{0:T(128)} %get-tuple-element.72.refs_0_.refs_1_, bf16[32,8320]{1,0:T(8,128)(2,1)S(1)} %collective-permute-done.11.refs_2_.refs_8_, ...), custom_call_target="tpu_custom_call" | custom-call | flops 1000000 | bytes 1000 | tf_op jit(solution)/shard_map/rows_backward/pallas_call | solution.py:269
  91.2 10.2 %weights_backward.1 = (f32[384,4096]{1,0:T(8,128)}, f32[384,4096]{1,0:T(8,128)}, f32[384,4096]{1,0:T(8,128)}, f32[8,128]{1,0:T(8,128)S(1)}) custom-call(bf16[64,1152]{1,0:T(8,128)(2,1)S(1)} %get-tuple-element.94.refs_0_.refs_18_, s32[1]{0:T(128)} %get-tuple-element.72.refs_0_.refs_1_, bf16[32,8320]{1,0:T(8,128)(2,1)S(1)} %copy-done.6, ...), custom_call_target="tpu_custom_call" | custom-call | flops 1000000 | bytes 1000 | tf_op jit(solution)/shard_map/weights_backward/pallas_call | solution.py:451
  101.5 1.5 %collective-permute-done.17.refs_4_ = bf16[128,2176]{1,0:T(8,128)(2,1)S(1)} collective-permute-done((bf16[128,2176]{1,0:T(8,128)(2,1)S(1)}, bf16[128,2176]{1,0:T(8,128)(2,1)S(1)}, u32[]{:S(2)}, u32[]{:S(2)}) %collective-permute-start.17) | collective-permute-done | bytes 557088 | tf_op jit(solution)/shard_map/ppermute | solution.py:541
  103.3 1.7 %collective-permute-start.25 = (bf16[128,1152]{1,0:T(8,128)(2,1)S(1)}, bf16[128,1152]{1,0:T(8,128)(2,1)S(1)}, u32[]{:S(2)}, u32[]{:S(2)}) collective-permute-start(bf16[128,1152]{1,0:T(8,128)(2,1)S(1)} %get-tuple-element.100.refs_0_), channel_id=1, source_target_pairs={{0,2},{1,3},{2,0},{3,1},{4,6},{5,7},{6,4},{7,5},{8,10},{9,11},{10,... | collective-permute-start | bytes 884744 | tf_op jit(solution)/shard_map/ppermute | solution.py:541
  105.7 1.5 %collective-permute-start.19 = (bf16[32,1152]{1,0:T(8,128)(2,1)S(1)}, bf16[32,1152]{1,0:T(8,128)(2,1)S(1)}, u32[]{:S(2)}, u32[]{:S(2)}) collective-permute-start(bf16[32,1152]{1,0:T(8,128)(2,1)S(1)} %get-tuple-element.104), channel_id=1, source_target_pairs={{0,16},{4,20},{8,24},{12,28},{16,0},{20,4},{24,8},{28,12},{1,17},{... | collective-permute-start | bytes 221192 | tf_op jit(solution)/shard_map/ppermute | solution.py:541
  107.3 1.4 %collective-permute-start.20 = (bf16[32,1152]{1,0:T(8,128)(2,1)S(1)}, bf16[32,1152]{1,0:T(8,128)(2,1)S(1)}, u32[]{:S(2)}, u32[]{:S(2)}) collective-permute-start(bf16[32,1152]{1,0:T(8,128)(2,1)S(1)} %get-tuple-element.102.refs_0_), channel_id=1, source_target_pairs={{0,24},{4,28},{8,16},{12,20},{16,8},{20,12},{24,0},{28,4},{1,25},{... | collective-permute-start | bytes 221192 | tf_op jit(solution)/shard_map/ppermute | solution.py:541
  108.7 4.4 %collective-permute-done.21.refs_5_ = bf16[64,2176]{1,0:T(8,128)(2,1)S(1)} collective-permute-done((bf16[64,2176]{1,0:T(8,128)(2,1)S(1)}, bf16[64,2176]{1,0:T(8,128)(2,1)S(1)}, u32[]{:S(2)}, u32[]{:S(2)}) %collective-permute-start.21) | collective-permute-done | bytes 278560 | tf_op jit(solution)/shard_map/ppermute | solution.py:541
  113.9 3.7 %collective-permute-start.24 = (f32[8,128]{1,0:T(8,128)S(1)}, f32[8,128]{1,0:T(8,128)S(1)}, u32[]{:S(2)}, u32[]{:S(2)}) collective-permute-start(f32[8,128]{1,0:T(8,128)S(1)} %get-tuple-element.108.refs_0_.refs_1_), channel_id=1, source_target_pairs={{0,3},{1,2},{2,1},{3,0},{4,7},{5,6},{6,5},{7,4},{8,11},{9,10},{10,... | collective-permute-start | bytes 12296 | tf_op jit(solution)/shard_map/ppermute | solution.py:541
  118.3 2.5 %collective-permute-done.24.refs_4_ = f32[8,128]{1,0:T(8,128)S(1)} collective-permute-done((f32[8,128]{1,0:T(8,128)S(1)}, f32[8,128]{1,0:T(8,128)S(1)}, u32[]{:S(2)}, u32[]{:S(2)}) %collective-permute-start.24) | collective-permute-done | bytes 4128 | tf_op jit(solution)/shard_map/ppermute | solution.py:541
  120.8 4.7 %collective-permute-done.23.refs_3_ = f32[8,128]{1,0:T(8,128)S(1)} collective-permute-done((f32[8,128]{1,0:T(8,128)S(1)}, f32[8,128]{1,0:T(8,128)S(1)}, u32[]{:S(2)}, u32[]{:S(2)}) %collective-permute-start.23) | collective-permute-done | bytes 4128 | tf_op jit(solution)/shard_map/ppermute | solution.py:541
  127.7 1.3 collective-permute-start.29
  129.9 1.7 %collective-permute-start.33 = (bf16[32,1152]{1,0:T(8,128)(2,1)S(1)}, bf16[32,1152]{1,0:T(8,128)(2,1)S(1)}, u32[]{:S(2)}, u32[]{:S(2)}) collective-permute-start(bf16[32,1152]{1,0:T(8,128)(2,1)S(1)} %get-tuple-element.120), channel_id=1, source_target_pairs={{0,28},{4,24},{8,20},{12,16},{16,12},{20,8},{24,4},{28,0},{1,29},{... | collective-permute-start | bytes 221192 | tf_op jit(solution)/shard_map/ppermute | solution.py:541
  132.6 2.7 %collective-permute-done.32.refs_16_ = bf16[32,1152]{1,0:T(8,128)(2,1)S(1)} collective-permute-done((bf16[32,1152]{1,0:T(8,128)(2,1)S(1)}, bf16[32,1152]{1,0:T(8,128)(2,1)S(1)}, u32[]{:S(2)}, u32[]{:S(2)}) %collective-permute-start.32) | collective-permute-done | bytes 73760 | tf_op jit(solution)/shard_map/ppermute | solution.py:541
  135.4 2.1 %collective-permute-done.30.refs_15_ = bf16[32,1152]{1,0:T(8,128)(2,1)S(1)} collective-permute-done((bf16[32,1152]{1,0:T(8,128)(2,1)S(1)}, bf16[32,1152]{1,0:T(8,128)(2,1)S(1)}, u32[]{:S(2)}, u32[]{:S(2)}) %collective-permute-start.30) | collective-permute-done | bytes 73760 | tf_op jit(solution)/shard_map/ppermute | solution.py:541
  137.5 1.7 %home.1 = (bf16[256,1024]{1,0:T(8,128)(2,1)}, f32[8,256]{1,0:T(8,128)}, f32[1]{0:T(128)}) custom-call(f32[8,256]{1,0:T(8,128)S(1)} %bitcast.23, s32[1,256]{1,0:T(1,128)S(1)} %bitcast.25, bf16[32,8320]{1,0:T(8,128)(2,1)S(1)} %copy-done.6, bf16[160,8320]{1,0:T(8,128)(2,1)S(1)} %collective-permute-done.refs_2_.refs_5_.refs_3_.refs_13_, ...), custom_call_target="tpu_custom_call" | custom-call | flops 1000000 | bytes 1000 | tf_op jit(solution)/shard_map/home/pallas_call | solution.py:517
  (83 shorter events, 18.4 us)
Async XLA Ops:
  7.5 5.3 %collective-permute-start = (bf16[160,8320]{1,0:T(8,128)(2,1)}, bf16[160,8320]{1,0:T(8,128)(2,1)S(1)}, u32[]{:S(2)}, u32[]{:S(2)}) collective-permute-start(bf16[160,8320]{1,0:T(8,128)(2,1)} %get-tuple-element.68), channel_id=1, source_target_pairs={{0,4},{4,0},{8,12},{12,8},{16,20},{20,16},{24,28},{28,24},{1,5},{5... | collective-permute-start | bytes 7987208 | tf_op jit(solution)/shard_map/ppermute | solution.py:541
  8.0 15.1 %collective-permute-start.3 = (bf16[32,4224]{1,0:T(8,128)(2,1)}, bf16[32,4224]{1,0:T(8,128)(2,1)S(1)}, u32[]{:S(2)}, u32[]{:S(2)}) collective-permute-start(bf16[32,4224]{1,0:T(8,128)(2,1)} %get-tuple-element.71), channel_id=1, source_target_pairs={{0,24},{4,28},{8,16},{12,20},{16,8},{20,12},{24,0},{28,4},{1,25},{... | collective-permute-start | bytes 811016 | tf_op jit(solution)/shard_map/ppermute | solution.py:541
  11.5 13.1 %collective-permute-start.2 = (bf16[32,4224]{1,0:T(8,128)(2,1)}, bf16[32,4224]{1,0:T(8,128)(2,1)S(1)}, u32[]{:S(2)}, u32[]{:S(2)}) collective-permute-start(bf16[32,4224]{1,0:T(8,128)(2,1)} %get-tuple-element.71), channel_id=1, source_target_pairs={{0,16},{4,20},{8,24},{12,28},{16,0},{20,4},{24,8},{28,12},{1,17},{... | collective-permute-start | bytes 811016 | tf_op jit(solution)/shard_map/ppermute | solution.py:541
  12.0 12.9 %collective-permute-start.1 = (bf16[32,4224]{1,0:T(8,128)(2,1)}, bf16[32,4224]{1,0:T(8,128)(2,1)S(1)}, u32[]{:S(2)}, u32[]{:S(2)}) collective-permute-start(bf16[32,4224]{1,0:T(8,128)(2,1)} %get-tuple-element.71), channel_id=1, source_target_pairs={{0,8},{4,12},{8,0},{12,4},{16,24},{20,28},{24,16},{28,20},{1,9},{5... | collective-permute-start | bytes 811016 | tf_op jit(solution)/shard_map/ppermute | solution.py:541
  24.9 9.6 %collective-permute-start.6 = (bf16[64,2176]{1,0:T(8,128)(2,1)S(1)}, bf16[64,2176]{1,0:T(8,128)(2,1)S(1)}, u32[]{:S(2)}, u32[]{:S(2)}) collective-permute-start(bf16[64,2176]{1,0:T(8,128)(2,1)S(1)} %get-tuple-element.80), channel_id=1, source_target_pairs={{0,1},{1,0},{2,3},{3,2},{4,5},{5,4},{6,7},{7,6},{8,9},{9,8},{10,11... | collective-permute-start | bytes 835592 | tf_op jit(solution)/shard_map/ppermute | solution.py:541
  26.6 24.0 %collective-permute-start.7 = (bf16[96,4224]{1,0:T(8,128)(2,1)S(1)}, bf16[96,4224]{1,0:T(8,128)(2,1)S(1)}, u32[]{:S(2)}, u32[]{:S(2)}) collective-permute-start(bf16[96,4224]{1,0:T(8,128)(2,1)S(1)} %constant_dynamic-update-slice_fusion.refs_3_.refs_11_), channel_id=1, source_target_pairs={{0,1},{1,0},{2,3},{3,2},{4,5},{5,4},{6,7},{7,6},{8,9},{9,8},{10,11... | collective-permute-start | bytes 2433032 | tf_op jit(solution)/shard_map/ppermute | solution.py:541
  28.2 36.5 %collective-permute-start.4 = (bf16[96,8320]{1,0:T(8,128)(2,1)S(1)}, bf16[96,8320]{1,0:T(8,128)(2,1)S(1)}, u32[]{:S(2)}, u32[]{:S(2)}) collective-permute-start(bf16[96,8320]{1,0:T(8,128)(2,1)S(1)} %get-tuple-element.77), channel_id=1, source_target_pairs={{0,8},{4,12},{8,0},{12,4},{16,24},{20,28},{24,16},{28,20},{1,9},{5... | collective-permute-start | bytes 4792328 | tf_op jit(solution)/shard_map/ppermute | solution.py:541
  29.7 36.2 %collective-permute-start.5 = (bf16[96,8320]{1,0:T(8,128)(2,1)S(1)}, bf16[96,8320]{1,0:T(8,128)(2,1)S(1)}, u32[]{:S(2)}, u32[]{:S(2)}) collective-permute-start(bf16[96,8320]{1,0:T(8,128)(2,1)S(1)} %get-tuple-element.78), channel_id=1, source_target_pairs={{0,16},{4,20},{8,24},{12,28},{16,0},{20,4},{24,8},{28,12},{1,17},{... | collective-permute-start | bytes 4792328 | tf_op jit(solution)/shard_map/ppermute | solution.py:541
  30.9 19.8 %collective-permute-start.8 = (bf16[96,4224]{1,0:T(8,128)(2,1)S(1)}, bf16[96,4224]{1,0:T(8,128)(2,1)S(1)}, u32[]{:S(2)}, u32[]{:S(2)}) collective-permute-start(bf16[96,4224]{1,0:T(8,128)(2,1)S(1)} %constant_dynamic-update-slice_fusion.refs_3_.refs_11_), channel_id=1, source_target_pairs={{0,4},{4,0},{8,12},{12,8},{16,20},{20,16},{24,28},{28,24},{1,5},{5... | collective-permute-start | bytes 2433032 | tf_op jit(solution)/shard_map/ppermute | solution.py:541
  54.1 11.9 %collective-permute-start.10 = (bf16[128,2176]{1,0:T(8,128)(2,1)S(1)}, bf16[128,2176]{1,0:T(8,128)(2,1)S(1)}, u32[]{:S(2)}, u32[]{:S(2)}) collective-permute-start(bf16[128,2176]{1,0:T(8,128)(2,1)S(1)} %get-tuple-element.86), channel_id=1, source_target_pairs={{0,4},{4,0},{8,12},{12,8},{16,20},{20,16},{24,28},{28,24},{1,5},{5... | collective-permute-start | bytes 1671176 | tf_op jit(solution)/shard_map/ppermute | solution.py:541
  66.0 9.9 %collective-permute-start.13 = (bf16[128,2176]{1,0:T(8,128)(2,1)S(1)}, bf16[128,2176]{1,0:T(8,128)(2,1)S(1)}, u32[]{:S(2)}, u32[]{:S(2)}) collective-permute-start(bf16[128,2176]{1,0:T(8,128)(2,1)S(1)} %get-tuple-element.91), channel_id=1, source_target_pairs={{0,4},{4,0},{8,12},{12,8},{16,20},{20,16},{24,28},{28,24},{1,5},{5... | collective-permute-start | bytes 1671176 | tf_op jit(solution)/shard_map/ppermute | solution.py:541
  66.1 15.5 %collective-permute-start.14 = (bf16[128,2176]{1,0:T(8,128)(2,1)S(1)}, bf16[128,2176]{1,0:T(8,128)(2,1)S(1)}, u32[]{:S(2)}, u32[]{:S(2)}) collective-permute-start(bf16[128,2176]{1,0:T(8,128)(2,1)S(1)} %merge.1.refs_0_), channel_id=1, source_target_pairs={{0,1},{1,0},{2,3},{3,2},{4,5},{5,4},{6,7},{7,6},{8,9},{9,8},{10,11... | collective-permute-start | bytes 1671176 | tf_op jit(solution)/shard_map/ppermute | solution.py:541
  66.9 18.1 %collective-permute-start.11 = (bf16[32,8320]{1,0:T(8,128)(2,1)S(1)}, bf16[32,8320]{1,0:T(8,128)(2,1)S(1)}, u32[]{:S(2)}, u32[]{:S(2)}) collective-permute-start(bf16[32,8320]{1,0:T(8,128)(2,1)S(1)} %slice.20), channel_id=1, source_target_pairs={{0,16},{4,20},{8,24},{12,28},{16,0},{20,4},{24,8},{28,12},{1,17},{... | collective-permute-start | bytes 1597448 | tf_op jit(solution)/shard_map/ppermute | solution.py:541
  68.2 16.8 %collective-permute-start.12 = (bf16[32,8320]{1,0:T(8,128)(2,1)S(1)}, bf16[32,8320]{1,0:T(8,128)(2,1)S(1)}, u32[]{:S(2)}, u32[]{:S(2)}) collective-permute-start(bf16[32,8320]{1,0:T(8,128)(2,1)S(1)} %slice.21), channel_id=1, source_target_pairs={{0,8},{4,12},{8,0},{12,4},{16,24},{20,28},{24,16},{28,20},{1,9},{5... | collective-permute-start | bytes 1597448 | tf_op jit(solution)/shard_map/ppermute | solution.py:541
  74.5 28.6 %collective-permute-start.17 = (bf16[128,2176]{1,0:T(8,128)(2,1)S(1)}, bf16[128,2176]{1,0:T(8,128)(2,1)S(1)}, u32[]{:S(2)}, u32[]{:S(2)}) collective-permute-start(bf16[128,2176]{1,0:T(8,128)(2,1)S(1)} %get-tuple-element.99), channel_id=1, source_target_pairs={{0,1},{1,0},{2,3},{3,2},{4,5},{5,4},{6,7},{7,6},{8,9},{9,8},{10,11... | collective-permute-start | bytes 1671176 | tf_op jit(solution)/shard_map/ppermute | solution.py:541
  82.1 21.0 %collective-permute-start.15 = (bf16[128,1152]{1,0:T(8,128)(2,1)S(1)}, bf16[128,1152]{1,0:T(8,128)(2,1)S(1)}, u32[]{:S(2)}, u32[]{:S(2)}) collective-permute-start(bf16[128,1152]{1,0:T(8,128)(2,1)S(1)} %get-tuple-element.93.refs_0_), channel_id=1, source_target_pairs={{0,2},{1,3},{2,0},{3,1},{4,6},{5,7},{6,4},{7,5},{8,10},{9,11},{10,... | collective-permute-start | bytes 884744 | tf_op jit(solution)/shard_map/ppermute | solution.py:541
  84.7 16.8 %collective-permute-start.16 = (bf16[64,1152]{1,0:T(8,128)(2,1)S(1)}, bf16[64,1152]{1,0:T(8,128)(2,1)S(1)}, u32[]{:S(2)}, u32[]{:S(2)}) collective-permute-start(bf16[64,1152]{1,0:T(8,128)(2,1)S(1)} %get-tuple-element.97.refs_0_), channel_id=1, source_target_pairs={{0,2},{1,3},{2,0},{3,1},{4,6},{5,7},{6,4},{7,5},{8,10},{9,11},{10,... | collective-permute-start | bytes 442376 | tf_op jit(solution)/shard_map/ppermute | solution.py:541
  90.5 22.6 %collective-permute-start.21 = (bf16[64,2176]{1,0:T(8,128)(2,1)S(1)}, bf16[64,2176]{1,0:T(8,128)(2,1)S(1)}, u32[]{:S(2)}, u32[]{:S(2)}) collective-permute-start(bf16[64,2176]{1,0:T(8,128)(2,1)S(1)} %get-tuple-element.106), channel_id=1, source_target_pairs={{0,1},{1,0},{2,3},{3,2},{4,5},{5,4},{6,7},{7,6},{8,9},{9,8},{10,11... | collective-permute-start | bytes 835592 | tf_op jit(solution)/shard_map/ppermute | solution.py:541
  103.3 22.2 %collective-permute-start.25 = (bf16[128,1152]{1,0:T(8,128)(2,1)S(1)}, bf16[128,1152]{1,0:T(8,128)(2,1)S(1)}, u32[]{:S(2)}, u32[]{:S(2)}) collective-permute-start(bf16[128,1152]{1,0:T(8,128)(2,1)S(1)} %get-tuple-element.100.refs_0_), channel_id=1, source_target_pairs={{0,2},{1,3},{2,0},{3,1},{4,6},{5,7},{6,4},{7,5},{8,10},{9,11},{10,... | collective-permute-start | bytes 884744 | tf_op jit(solution)/shard_map/ppermute | solution.py:541
  105.1 8.0 %collective-permute-start.18 = (bf16[32,1152]{1,0:T(8,128)(2,1)S(1)}, bf16[32,1152]{1,0:T(8,128)(2,1)S(1)}, u32[]{:S(2)}, u32[]{:S(2)}) collective-permute-start(bf16[32,1152]{1,0:T(8,128)(2,1)S(1)} %get-tuple-element.103), channel_id=1, source_target_pairs={{0,8},{4,12},{8,0},{12,4},{16,24},{20,28},{24,16},{28,20},{1,9},{5... | collective-permute-start | bytes 221192 | tf_op jit(solution)/shard_map/ppermute | solution.py:541
  105.7 7.4 %collective-permute-start.19 = (bf16[32,1152]{1,0:T(8,128)(2,1)S(1)}, bf16[32,1152]{1,0:T(8,128)(2,1)S(1)}, u32[]{:S(2)}, u32[]{:S(2)}) collective-permute-start(bf16[32,1152]{1,0:T(8,128)(2,1)S(1)} %get-tuple-element.104), channel_id=1, source_target_pairs={{0,16},{4,20},{8,24},{12,28},{16,0},{20,4},{24,8},{28,12},{1,17},{... | collective-permute-start | bytes 221192 | tf_op jit(solution)/shard_map/ppermute | solution.py:541
  107.3 5.9 %collective-permute-start.20 = (bf16[32,1152]{1,0:T(8,128)(2,1)S(1)}, bf16[32,1152]{1,0:T(8,128)(2,1)S(1)}, u32[]{:S(2)}, u32[]{:S(2)}) collective-permute-start(bf16[32,1152]{1,0:T(8,128)(2,1)S(1)} %get-tuple-element.102.refs_0_), channel_id=1, source_target_pairs={{0,24},{4,28},{8,16},{12,20},{16,8},{20,12},{24,0},{28,4},{1,25},{... | collective-permute-start | bytes 221192 | tf_op jit(solution)/shard_map/ppermute | solution.py:541
  113.2 15.8 %collective-permute-start.31 = (bf16[64,1152]{1,0:T(8,128)(2,1)S(1)}, bf16[64,1152]{1,0:T(8,128)(2,1)S(1)}, u32[]{:S(2)}, u32[]{:S(2)}) collective-permute-start(bf16[64,1152]{1,0:T(8,128)(2,1)S(1)} %get-tuple-element.118.refs_0_), channel_id=1, source_target_pairs={{0,2},{1,3},{2,0},{3,1},{4,6},{5,7},{6,4},{7,5},{8,10},{9,11},{10,... | collective-permute-start | bytes 442376 | tf_op jit(solution)/shard_map/ppermute | solution.py:541
  113.9 6.9 %collective-permute-start.24 = (f32[8,128]{1,0:T(8,128)S(1)}, f32[8,128]{1,0:T(8,128)S(1)}, u32[]{:S(2)}, u32[]{:S(2)}) collective-permute-start(f32[8,128]{1,0:T(8,128)S(1)} %get-tuple-element.108.refs_0_.refs_1_), channel_id=1, source_target_pairs={{0,3},{1,2},{2,1},{3,0},{4,7},{5,6},{6,5},{7,4},{8,11},{9,10},{10,... | collective-permute-start | bytes 12296 | tf_op jit(solution)/shard_map/ppermute | solution.py:541
  117.7 7.9 %collective-permute-start.23 = (f32[8,128]{1,0:T(8,128)S(1)}, f32[8,128]{1,0:T(8,128)S(1)}, u32[]{:S(2)}, u32[]{:S(2)}) collective-permute-start(f32[8,128]{1,0:T(8,128)S(1)} %get-tuple-element.108.refs_0_.refs_1_), channel_id=1, source_target_pairs={{0,2},{1,3},{2,0},{3,1},{4,6},{5,7},{6,4},{7,5},{8,10},{9,11},{10,... | collective-permute-start | bytes 12296 | tf_op jit(solution)/shard_map/ppermute | solution.py:541
  118.0 7.5 %collective-permute-start.22 = (f32[8,128]{1,0:T(8,128)S(1)}, f32[8,128]{1,0:T(8,128)S(1)}, u32[]{:S(2)}, u32[]{:S(2)}) collective-permute-start(f32[8,128]{1,0:T(8,128)S(1)} %get-tuple-element.108.refs_0_.refs_1_), channel_id=1, source_target_pairs={{0,1},{1,0},{2,3},{3,2},{4,5},{5,4},{6,7},{7,6},{8,9},{9,8},{10,11... | collective-permute-start | bytes 12296 | tf_op jit(solution)/shard_map/ppermute | solution.py:541
  125.8 5.7 %collective-permute-start.27 = (bf16[32,1152]{1,0:T(8,128)(2,1)S(1)}, bf16[32,1152]{1,0:T(8,128)(2,1)S(1)}, u32[]{:S(2)}, u32[]{:S(2)}) collective-permute-start(bf16[32,1152]{1,0:T(8,128)(2,1)S(1)} %get-tuple-element.113), channel_id=1, source_target_pairs={{0,8},{4,12},{8,0},{12,4},{16,24},{20,28},{24,16},{28,20},{1,9},{5... | collective-permute-start | bytes 221192 | tf_op jit(solution)/shard_map/ppermute | solution.py:541
  126.4 6.1 %collective-permute-start.28 = (bf16[32,1152]{1,0:T(8,128)(2,1)S(1)}, bf16[32,1152]{1,0:T(8,128)(2,1)S(1)}, u32[]{:S(2)}, u32[]{:S(2)}) collective-permute-start(bf16[32,1152]{1,0:T(8,128)(2,1)S(1)} %get-tuple-element.114), channel_id=1, source_target_pairs={{0,12},{4,8},{8,4},{12,0},{16,28},{20,24},{24,20},{28,16},{1,13},{... | collective-permute-start | bytes 221192 | tf_op jit(solution)/shard_map/ppermute | solution.py:541
  127.7 4.9 %collective-permute-start.29 = (bf16[32,1152]{1,0:T(8,128)(2,1)S(1)}, bf16[32,1152]{1,0:T(8,128)(2,1)S(1)}, u32[]{:S(2)}, u32[]{:S(2)}) collective-permute-start(bf16[32,1152]{1,0:T(8,128)(2,1)S(1)} %get-tuple-element.115), channel_id=1, source_target_pairs={{0,16},{4,20},{8,24},{12,28},{16,0},{20,4},{24,8},{28,12},{1,17},{... | collective-permute-start | bytes 221192 | tf_op jit(solution)/shard_map/ppermute | solution.py:541
  129.1 6.1 %collective-permute-start.32 = (bf16[32,1152]{1,0:T(8,128)(2,1)S(1)}, bf16[32,1152]{1,0:T(8,128)(2,1)S(1)}, u32[]{:S(2)}, u32[]{:S(2)}) collective-permute-start(bf16[32,1152]{1,0:T(8,128)(2,1)S(1)} %get-tuple-element.119), channel_id=1, source_target_pairs={{0,24},{4,28},{8,16},{12,20},{16,8},{20,12},{24,0},{28,4},{1,25},{... | collective-permute-start | bytes 221192 | tf_op jit(solution)/shard_map/ppermute | solution.py:541
  129.9 5.6 %collective-permute-start.33 = (bf16[32,1152]{1,0:T(8,128)(2,1)S(1)}, bf16[32,1152]{1,0:T(8,128)(2,1)S(1)}, u32[]{:S(2)}, u32[]{:S(2)}) collective-permute-start(bf16[32,1152]{1,0:T(8,128)(2,1)S(1)} %get-tuple-element.120), channel_id=1, source_target_pairs={{0,28},{4,24},{8,20},{12,16},{16,12},{20,8},{24,4},{28,0},{1,29},{... | collective-permute-start | bytes 221192 | tf_op jit(solution)/shard_map/ppermute | solution.py:541
  131.5 6.0 %collective-permute-start.30 = (bf16[32,1152]{1,0:T(8,128)(2,1)S(1)}, bf16[32,1152]{1,0:T(8,128)(2,1)S(1)}, u32[]{:S(2)}, u32[]{:S(2)}) collective-permute-start(bf16[32,1152]{1,0:T(8,128)(2,1)S(1)} %get-tuple-element.116.refs_0_), channel_id=1, source_target_pairs={{0,20},{4,16},{8,28},{12,24},{16,4},{20,0},{24,12},{28,8},{1,21},{... | collective-permute-start | bytes 221192 | tf_op jit(solution)/shard_map/ppermute | solution.py:541
  (14 other events, 179.4 us)
